TPU v7x, 32 devices: a whole 2x2x4 slice. The times are simulated.
32 devices in a mesh: grp: 2 (over y), inp: 8 (over z, x), freq: 2 (over core).
Axes of the slice: x: 2, y: 2, z: 4, core: 2. Of those that a mesh axis runs over, the one named last changes fastest.
Arguments:
- voltages: int32 [2048, 64, 2048], P(('grp', 'inp'), 'freq'), parts along dimension 0, may hold values from -127 to 127, as said below
- coeffs: int32 [8, 2048], replicated, may hold values from -6144 to 6144, as said below
Outputs:
- visibilities: bfloat16 [1024, 2, 36, 128, 128], P(('grp', 'inp', 'freq')), parts along dimension 0
There are 2 independent parts, one for each index of `grp`. A program takes and returns all parts, laid end to end along the dimension named above; an argument that names none is the same for every part. Nothing has to cross between parts.
Inputs may be any that keep to these rules, and one draw needn't show every extreme that they name: `voltages`: signed 8-bit samples. `coeffs`: integer coefficients.
All inputs are finite; a program needn't handle non-finite values.
Results may differ from a plain program's by a relative error of at most 0.0069.
Values may be sent and summed in bfloat16 or wider, within the bound.
No kernel may reach another device: no remote copies, remote signals or barrier semaphores. Data moves between devices by JAX's collectives and lax.ppermute only.
A program may use at most 384 MiB of HBM per device.

v0:
```python
import math

import jax
import jax.numpy as jnp
from jax import lax
from jax.sharding import PartitionSpec as P

SPF = 2048
TAPS = 8
CH = 512
CH0 = 256
INPUTS = 1024
BLK = 128


def passed_along(x, axis, by):
    length = lax.axis_size(axis)
    pairs = [(i, i + by) for i in range(length) if 0 <= i + by < length]
    return lax.ppermute(x, axis, pairs)


def make_table():
    sample = jnp.arange(SPF, dtype=jnp.int32)[:, None]
    channel = jnp.arange(CH, dtype=jnp.int32)[None, :] + CH0
    phase = sample * channel % SPF
    angle = phase.astype(jnp.float32) * (2.0 * math.pi / SPF)
    return jnp.concatenate([jnp.cos(angle), -jnp.sin(angle)], axis=1).astype(jnp.bfloat16)


def per_device(voltages, coeffs):
    inputs_here = voltages.shape[0]
    frames_here = voltages.shape[1]
    inp_count = lax.axis_size("inp")
    freq_count = lax.axis_size("freq")
    frames_all = frames_here * freq_count
    history = voltages[:, frames_here - (TAPS - 1) :, :].astype(jnp.bfloat16)
    earlier = passed_along(history, "freq", 1)
    extended = jnp.concatenate([earlier.astype(jnp.float32), voltages.astype(jnp.float32)], axis=1)
    weights = coeffs.astype(jnp.float32)
    summed = jnp.zeros((inputs_here, frames_here, SPF), jnp.float32)
    for tap_index in range(TAPS):
        begin = TAPS - 1 - tap_index
        summed = summed + weights[tap_index] * extended[:, begin : begin + frames_here, :]
    filtered = summed.astype(jnp.bfloat16).reshape(inputs_here * frames_here, SPF)
    spectrum_t = jnp.einsum("nj,rn->jr", make_table(), filtered, preferred_element_type=jnp.float32)
    spectrum_t = spectrum_t.reshape(2 * CH, inputs_here, frames_here)
    squares = jnp.sum(spectrum_t * spectrum_t, axis=(0, 2))
    power = lax.psum(squares, "freq") / (frames_all * CH)
    gains = 1.0 / jnp.sqrt(power + 1e-06)
    scaled = (spectrum_t * gains[None, :, None]).astype(jnp.bfloat16)
    scaled = scaled.reshape(2, CH, inputs_here * frames_here)
    arrived = lax.all_to_all(scaled[None], ("inp", "freq"), split_axis=2, concat_axis=0, tiled=True)
    width_here = arrived.shape[-2]
    arranged = arrived.reshape(inp_count, freq_count, 2, width_here, inputs_here, frames_here)
    arranged = jnp.transpose(arranged, (3, 0, 4, 2, 1, 5))
    stacked = arranged.reshape(width_here, INPUTS, 2 * frames_all)
    other = jnp.concatenate([-stacked[:, :, frames_all:], stacked[:, :, :frames_all]], axis=2)
    block_count = INPUTS // BLK
    scale = 1.0 / frames_all
    pieces = []
    for row_index in range(block_count):
        row_panel = stacked[:, row_index * BLK : (row_index + 1) * BLK]
        real_part = jnp.einsum(
            "cut,cmt->cum",
            row_panel,
            stacked[:, row_index * BLK :],
            preferred_element_type=jnp.float32,
        )
        imag_part = jnp.einsum(
            "cut,cmt->cum",
            row_panel,
            other[:, row_index * BLK :],
            preferred_element_type=jnp.float32,
        )
        band = jnp.stack([real_part, imag_part], axis=1) * scale
        for col_index in range(row_index, block_count):
            begin = (col_index - row_index) * BLK
            pieces.append(band[:, :, :, begin : begin + BLK])
    return jnp.stack(pieces, axis=2).astype(jnp.bfloat16)


def solution(mesh):
    in_specs = (P(("grp", "inp"), "freq", None), P())
    out_specs = P(("grp", "inp", "freq"), None, None, None, None)
    return jax.shard_map(
        per_device, mesh=mesh, in_specs=in_specs, out_specs=out_specs, check_vma=False
    )
```

profile of v0, /device:TPU:0, one launch (start us, length us, event | category | flops | bytes accessed | tf_op | source)
XLA Modules:
  0.0 860.5 jit_solution(8330098738441136342)
XLA Ops:
  11.2 23.3 %convert_element_type.25 = f32[128,32,2048]{2,1,0:T(8,128)} convert(s32[128,32,2048]{2,1,0:T(8,128)} %param.2) | non-fusion elementwise | flops 8388608 | bytes 67108864 | tf_op jit(solution)/shard_map/convert_element_type | solution.py:38
  34.6 18.8 %cosine_convert_fusion = (bf16[2048,512]{0,1:T(8,128)(2,1)S(1)}, bf16[2048,512]{0,1:T(8,128)(2,1)}) fusion(s32[512]{0:T(512)S(1)} %iota_add_fusion), kind=kLoop, calls=%fused_computation.94 | loop fusion | flops 17825792 | bytes 4196352 | tf_op jit(solution)/shard_map/convert.107
  58.9 108.5 %fusion.4 = bf16[128,32,2048]{2,1,0:T(8,128)(2,1)} fusion(f32[128,32,2048]{2,1,0:T(8,128)} %convert_element_type.25, f32[128,7,2048]{2,1,0:T(8,128)} %copy.77, f32[2048]{0:T(1024)S(1)} %bitcast.225, f32[2048]{0:T(1024)S(1)} %bitcast.226, f32[2048]{0:T(1024)S(1)} %bitcast.227, f32[2048]{0:T(1024)S(1)} %bitcast.228, f32[2048]{0:T(1024)S(1)} %bitcast.229, ...), kind=kLoop, calls=%fused_computation.16 | loop fusion | flops 192937984 | bytes 57737216 | tf_op jit(solution)/shard_map/convert_element_type | solution.py:44
  167.4 32.8 %multiply_reduce_fusion = (f32[128]{0:T(128)S(1)}, f32[1024,128,32]{1,0,2:T(8,128)}) fusion(bf16[128,32,2048]{2,1,0:T(8,128)(2,1)} %fusion.4, bf16[2048,512]{0,1:T(8,128)(2,1)} %get-tuple-element.16, bf16[2048,512]{0,1:T(8,128)(2,1)S(1)} %get-tuple-element.15), kind=kOutput, calls=%fused_computation.47 | convolution fusion | flops 17196646400 | bytes 37749248 | tf_op jit(solution)/shard_map/nj,rn->jr/dot_general | solution.py:45
  202.6 9.2 %multiply_convert_fusion = bf16[1024,128,32]{1,0,2:T(8,128)(2,1)} fusion(f32[1024,128,32]{1,0,2:T(8,128)} %get-tuple-element.18, f32[128]{0:T(128)S(1)} %add_rsqrt_fusion), kind=kLoop, calls=%fused_computation.46 | loop fusion | flops 8388608 | bytes 25166336 | tf_op jit(solution)/shard_map/convert_element_type | solution.py:50
  211.8 12.2 %copy.79 = bf16[1024,128,32]{0,2,1:T(8,128)(2,1)} copy(bf16[1024,128,32]{1,0,2:T(8,128)(2,1)} %multiply_convert_fusion) | data formatting | bytes 16777216 | tf_op jit(solution)/shard_map/convert_element_type | solution.py:50
  224.1 14.6 %broadcast_in_dim_reshape.3 = bf16[1,2,512,4096]{2,1,3,0:T(2,128)(2,1)} reshape(bf16[1024,128,32]{0,2,1:T(8,128)(2,1)} %copy.79) | data formatting | bytes 16777216 | tf_op jit(solution)/shard_map/broadcast_in_dim;reshape | solution.py:52
  238.6 28.3 %copy.80 = bf16[1,2,512,4096]{3,1,0,2:T(2,128)(2,1)} copy(bf16[1,2,512,4096]{2,1,3,0:T(2,128)(2,1)} %broadcast_in_dim_reshape.3) | data formatting | bytes 16777216 | tf_op jit(solution)/shard_map/broadcast_in_dim;reshape | solution.py:52
  266.9 189.4 %all_to_all.15 = bf16[1,2,512,4096]{3,1,0,2:T(2,128)(2,1)} all-to-all(bf16[1,2,512,4096]{3,1,0,2:T(2,128)(2,1)} %copy.80), channel_id=1, replica_groups=mesh['grp'=2,'inp'=8,'freq'=2] {'inp','freq'}, dimensions={2} | all-to-all | bytes 16777216 | tf_op jit(solution)/shard_map/all_to_all | solution.py:52
  456.3 12.8 %copy.81 = bf16[1,2,512,4096]{3,2,1,0:T(8,128)(2,1)} copy(bf16[1,2,512,4096]{3,1,0,2:T(2,128)(2,1)} %all_to_all.15) | data formatting | bytes 16777216 | tf_op jit(solution)/shard_map/all_to_all | solution.py:52
  476.9 32.6 %reshape.56 = bf16[8,2,2,32,128,32]{5,4,3,2,1,0:T(8,128)(2,1)} reshape(bf16[16,1,2,32,4096]{4,3,2,0,1:T(8,128)(2,1)} %copy.82) | data formatting | bytes 16777216 | tf_op jit(solution)/shard_map/reshape | solution.py:54
  509.5 29.2 %copy.83 = bf16[32,8,128,2,2,32]{2,1,5,4,3,0:T(8,128)(2,1)} copy(bf16[32,8,128,2,2,32]{5,2,0,3,4,1:T(8,128)(2,1)} %bitcast.206) | data formatting | bytes 16777216 | tf_op jit(solution)/shard_map/transpose | solution.py:55
  538.7 13.3 %reshape.57 = bf16[32,1024,128]{1,2,0:T(8,128)(2,1)} reshape(bf16[32,8,128,2,2,32]{2,1,5,4,3,0:T(8,128)(2,1)} %copy.83) | data formatting | bytes 16777216 | tf_op jit(solution)/shard_map/reshape | solution.py:56
  577.2 9.1 %neg.7 = bf16[32,1024,64]{2,1,0:T(8,128)(2,1)} negate(bf16[32,1024,64]{2,1,0:T(8,128)(2,1)} %copy.104) | non-fusion elementwise | flops 2097152 | bytes 8388608 | tf_op jit(solution)/shard_map/neg | solution.py:57
  586.3 8.6 %copy.105 = bf16[32,1024,64]{2,1,0:T(8,128)(2,1)} copy(bf16[32,1024,64]{1,2,0:T(8,128)(2,1)} %get-tuple-element.6) | data formatting | bytes 8388608
  595.0 18.1 %convolution_bitcast_fusion = f32[32,1,128,1024]{3,2,0,1:T(8,128)} fusion(bf16[32,1024,64]{2,1,0:T(8,128)(2,1)} %copy.105, bf16[32,1024,64]{2,1,0:T(8,128)(2,1)} %neg.7, bf16[32,1024,128]{1,2,0:T(8,128)(2,1)} %reshape.57), kind=kOutput, calls=%fused_computation.50 | convolution fusion | flops 1090519040 | bytes 34603008 | tf_op jit(solution)/shard_map/cut,cmt->cum/dot_general | solution.py:69
  613.0 15.4 %convolution_bitcast_fusion.2 = f32[32,1,128,896]{3,2,0,1:T(8,128)} fusion(bf16[32,1024,64]{2,1,0:T(8,128)(2,1)} %copy.105, bf16[32,1024,64]{2,1,0:T(8,128)(2,1)} %neg.7, bf16[32,1024,128]{1,2,0:T(8,128)(2,1)} %reshape.57), kind=kOutput, calls=%fused_computation.52 | convolution fusion | flops 954204160 | bytes 32505856 | tf_op jit(solution)/shard_map/cut,cmt->cum/dot_general | solution.py:69
  628.4 11.2 %convolution_bitcast_fusion.3 = f32[32,1,128,896]{3,2,0,1:T(8,128)} fusion(bf16[32,1024,128]{1,2,0:T(8,128)(2,1)} %reshape.57), kind=kOutput, calls=%fused_computation.53 | convolution fusion | flops 939524096 | bytes 23068672 | tf_op jit(solution)/shard_map/cut,cmt->cum/dot_general | solution.py:63
  639.6 10.6 %fusion.50 = f32[32,1,128,768]{3,2,0,1:T(8,128)} fusion(bf16[32,1024,64]{2,1,0:T(8,128)(2,1)} %copy.105, bf16[32,1024,64]{2,1,0:T(8,128)(2,1)} %neg.7, bf16[32,1024,128]{1,2,0:T(8,128)(2,1)} %reshape.57), kind=kOutput, calls=%fused_computation.78 | convolution fusion | flops 817889280 | bytes 30408704 | tf_op jit(solution)/shard_map/cut,cmt->cum/dot_general | solution.py:69
  656.6 9.9 %fusion.68 = f32[32,1,128,640]{3,2,0,1:T(8,128)} fusion(bf16[32,1024,64]{2,1,0:T(8,128)(2,1)} %copy.105, bf16[32,1024,64]{2,1,0:T(8,128)(2,1)S(1)} %bitcast.203, bf16[32,1024,128]{1,2,0:T(8,128)(2,1)S(1)} %bitcast.201), kind=kOutput, calls=%fused_computation.98 | convolution fusion | flops 681574400 | bytes 24117248 | tf_op jit(solution)/shard_map/cut,cmt->cum/dot_general | solution.py:69
  672.0 8.5 fusion.77
  706.5 13.2 %fusion.21 = bf16[32,2,128,1024]{3,2,0,1:T(8,128)(2,1)S(1)} fusion(f32[32,1,128,1024]{3,2,0,1:T(8,128)} %convolution_bitcast_fusion, f32[32,1,128,1024]{3,2,0,1:T(8,128)} %convolution_bitcast_fusion.1), kind=kLoop, calls=%fused_computation.35 | loop fusion | flops 25165824 | bytes 50331648 | tf_op jit(solution)/shard_map/convert.105
  735.0 10.3 %fusion.22 = bf16[32,2,128,896]{3,2,0,1:T(8,128)(2,1)S(1)} fusion(f32[32,1,128,896]{3,2,0,1:T(8,128)S(1)} %bitcast.208, f32[32,1,128,896]{3,2,0,1:T(8,128)} %convolution_bitcast_fusion.3), kind=kLoop, calls=%fused_computation.37 | loop fusion | flops 22020096 | bytes 44040192 | tf_op jit(solution)/shard_map/convert.89
  810.7 49.6 %copy.101 = bf16[32,2,36,128,128]{4,3,2,1,0:T(8,128)(2,1)} copy(bf16[32,2,36,128,128]{4,3,0,1,2:T(8,128)(2,1)} %fusion.92) | data formatting | bytes 150994944 | tf_op jit(solution)/shard_map/stack | solution.py:79
  (141 shorter events, 170.5 us)
Async XLA Ops:
  8.3 26.3 %copy-start.5 = (s32[8,2048]{1,0:T(8,128)S(1)}, s32[8,2048]{1,0:T(8,128)}, u32[]{:S(2)}) copy-start(s32[8,2048]{1,0:T(8,128)} %param.3) | copy-start | bytes 196612
  8.3 45.1 %collective-permute-start = (bf16[128,7,2048]{2,0,1:T(8,128)(2,1)S(1)}, bf16[128,7,2048]{2,0,1:T(8,128)(2,1)S(1)}, u32[]{:S(2)}, u32[]{:S(2)}) collective-permute-start(bf16[128,7,2048]{2,0,1:T(8,128)(2,1)S(1)} %copy_convert_fusion), channel_id=1, source_target_pairs={{0,1},{2,3},{4,5},{6,7},{8,9},{10,11},{12,13},{14,15},{16,17},{18,... | collective-permute-start | bytes 11010056 | tf_op jit(solution)/shard_map/ppermute | solution.py:19
  552.0 8.8 %copy-start = (bf16[32,1024,128]{1,2,0:T(8,128)(2,1)S(1)}, bf16[32,1024,128]{1,2,0:T(8,128)(2,1)}, u32[]{:S(2)}) copy-start(bf16[32,1024,128]{1,2,0:T(8,128)(2,1)} %reshape.57) | copy-start | bytes 25165828
  628.4 21.8 %slice-start = ((s8[8388608]{0:T(1024)(128)(4,1)}), s8[4194304]{0:T(1024)(128)(4,1)S(1)}, s32[]{:S(2)}) async-start(s8[8388608]{0:T(1024)(128)(4,1)} %bitcast.200), calls=%async_computation.1 | async-start | bytes 8388608
  628.4 28.2 %slice-start.2 = ((s8[8388608]{0:T(1024)(128)(4,1)}), s8[4194304]{0:T(1024)(128)(4,1)S(1)}, s32[]{:S(2)}) async-start(s8[8388608]{0:T(1024)(128)(4,1)} %bitcast.202), calls=%async_computation.3 | async-start | bytes 8388608
  639.6 10.6 %slice-start.1 = ((s8[8388608]{0:T(1024)(128)(4,1)}), s8[4194304]{0:T(1024)(128)(4,1)S(1)}, s32[]{:S(2)}) async-start(s8[8388608]{0:T(1024)(128)(4,1)} %bitcast.200), calls=%async_computation.2 | async-start | bytes 8388608
  639.6 17.0 %slice-start.3 = ((s8[8388608]{0:T(1024)(128)(4,1)}), s8[4194304]{0:T(1024)(128)(4,1)S(1)}, s32[]{:S(2)}) async-start(s8[8388608]{0:T(1024)(128)(4,1)} %bitcast.202), calls=%async_computation.4 | async-start | bytes 8388608
  680.5 15.3 %slice-start.4 = ((s8[8388608]{0:T(1024)(128)(4,1)}), s8[4194304]{0:T(1024)(128)(4,1)S(1)}, s32[]{:S(2)}) async-start(s8[8388608]{0:T(1024)(128)(4,1)} %bitcast.204), calls=%async_computation.5 | async-start | bytes 8388608
  685.1 10.7 %slice-start.5 = ((s8[8388608]{0:T(1024)(128)(4,1)}), s8[4194304]{0:T(1024)(128)(4,1)S(1)}, s32[]{:S(2)}) async-start(s8[8388608]{0:T(1024)(128)(4,1)} %bitcast.204), calls=%async_computation.6 | async-start | bytes 8388608
  721.6 13.4 %slice-start.6 = ((s8[14680064]{0:T(1024)(128)(4,1)}), s8[4194304]{0:T(1024)(128)(4,1)S(1)}, s32[]{:S(2)}) async-start(s8[14680064]{0:T(1024)(128)(4,1)} %bitcast.207), calls=%async_computation.7 | async-start | bytes 8388608
  723.5 11.5 %slice-start.7 = ((s8[14680064]{0:T(1024)(128)(4,1)}), s8[4194304]{0:T(1024)(128)(4,1)S(1)}, s32[]{:S(2)}) async-start(s8[14680064]{0:T(1024)(128)(4,1)} %bitcast.207), calls=%async_computation.8 | async-start | bytes 8388608
  727.4 7.6 slice-start.8
  735.0 22.6 %slice-start.13 = ((s8[12582912]{0:T(1024)(128)(4,1)}), s8[4194304]{0:T(1024)(128)(4,1)S(1)}, s32[]{:S(2)}) async-start(s8[12582912]{0:T(1024)(128)(4,1)} %bitcast.211), calls=%async_computation.14 | async-start | bytes 8388608
  735.0 22.6 %slice-start.14 = ((s8[12582912]{0:T(1024)(128)(4,1)}), s8[4194304]{0:T(1024)(128)(4,1)S(1)}, s32[]{:S(2)}) async-start(s8[12582912]{0:T(1024)(128)(4,1)} %bitcast.211), calls=%async_computation.15 | async-start | bytes 8388608
  747.2 10.5 %slice-start.10 = ((s8[12582912]{0:T(1024)(128)(4,1)}), s8[4194304]{0:T(1024)(128)(4,1)S(1)}, s32[]{:S(2)}) async-start(s8[12582912]{0:T(1024)(128)(4,1)} %bitcast.209), calls=%async_computation.11 | async-start | bytes 8388608
  747.2 10.5 %slice-start.15 = ((s8[12582912]{0:T(1024)(128)(4,1)}), s8[4194304]{0:T(1024)(128)(4,1)S(1)}, s32[]{:S(2)}) async-start(s8[12582912]{0:T(1024)(128)(4,1)} %bitcast.211), calls=%async_computation.16 | async-start | bytes 8388608
  750.7 7.0 slice-start.11
  762.9 8.7 %slice-start.16 = ((s8[10485760]{0:T(1024)(128)(4,1)}), s8[4194304]{0:T(1024)(128)(4,1)S(1)}, s32[]{:S(2)}) async-start(s8[10485760]{0:T(1024)(128)(4,1)} %bitcast.213), calls=%async_computation.17 | async-start | bytes 8388608
  764.6 7.0 slice-start.17
  769.9 17.5 %slice-start.21 = ((s8[8388608]{0:T(1024)(128)(4,1)}), s8[4194304]{0:T(1024)(128)(4,1)S(1)}, s32[]{:S(2)}) async-start(s8[8388608]{0:T(1024)(128)(4,1)} %bitcast.217), calls=%async_computation.22 | async-start | bytes 8388608
  771.6 15.7 %slice-start.22 = ((s8[8388608]{0:T(1024)(128)(4,1)}), s8[4194304]{0:T(1024)(128)(4,1)S(1)}, s32[]{:S(2)}) async-start(s8[8388608]{0:T(1024)(128)(4,1)} %bitcast.217), calls=%async_computation.23 | async-start | bytes 8388608
  785.6 11.4 %slice-start.25 = ((s8[6291456]{0:T(1024)(128)(4,1)}), s8[4194304]{0:T(1024)(128)(4,1)S(1)}, s32[]{:S(2)}) async-start(s8[6291456]{0:T(1024)(128)(4,1)} %bitcast.222), calls=%async_computation.26 | async-start | bytes 8388608
  787.4 9.6 %slice-start.26 = ((s8[6291456]{0:T(1024)(128)(4,1)}), s8[2097152]{0:T(1024)(128)(4,1)S(1)}, s32[]{:S(2)}) async-start(s8[6291456]{0:T(1024)(128)(4,1)} %bitcast.222), calls=%async_computation.27 | async-start | bytes 4194304
  789.9 7.0 slice-start.23
  (10 other events, 44.6 us)
where the time goes:
time: 869 us; the launch traced here: 861 us
  local copies, waits for them, and re-layouts  299 us (34%)
  other arithmetic  214 us (25%)
  blocking collectives  192 us (22%)
  matrix products  152 us (17%)
    all_to_all x1, blocking collectives, per_device(): lax.all_to_all(scaled[None], ('inp', 'freq'), split_axis=2, concat_axis=0...  189 us
    convert_element_type x1, other arithmetic, per_device(): summed.astype(jnp.bfloat16).reshape(inputs_here * frames_here, SPF)  109 us
    unnamed x103, local copies, waits for them, and re-layouts  81.1 us
    dot_general x8, matrix products, per_device(): jnp.einsum('cut,cmt->cum', row_panel, other[:, row_index * BLK:], preferr...  75.3 us
    another operation x9, other arithmetic  62.2 us
    another operation x1, local copies, waits for them, and re-layouts, per_device(): return jnp.stack(pieces, axis=2).astype(jnp.bfloat16)  49.6 us
    dot_general x8, matrix products, per_device(): jnp.einsum('cut,cmt->cum', row_panel, stacked[:, row_index * BLK:], prefe...  44.3 us
    another operation x2, local copies, waits for them, and re-layouts, per_device(): scaled[None]  42.9 us
  transfers between devices with their start and end apart: 1, of which 0 were waited for; matrix products, arithmetic and copies ran while one was open for 5% of the time, Pallas kernels for 0%

commit v1 on v0

--- a/solution.py
+++ b/solution.py
@@ -2,7 +2,11 @@
 
 import jax
 import jax.numpy as jnp
+import ml_dtypes
+import numpy as np
 from jax import lax
+from jax.experimental import pallas as pl
+from jax.experimental.pallas import tpu as pltpu
 from jax.sharding import PartitionSpec as P
 
 SPF = 2048
@@ -11,6 +15,10 @@
 CH0 = 256
 INPUTS = 1024
 BLK = 128
+LANES = 128
+UBLK = 16
+TBLK = 16
+HALVES = 2
 
 
 def passed_along(x, axis, by):
@@ -27,7 +35,7 @@
     return jnp.concatenate([jnp.cos(angle), -jnp.sin(angle)], axis=1).astype(jnp.bfloat16)
 
 
-def per_device(voltages, coeffs):
+def any_sizes(voltages, coeffs):
     inputs_here = voltages.shape[0]
     frames_here = voltages.shape[1]
     inp_count = lax.axis_size("inp")
@@ -79,6 +87,317 @@
     return jnp.stack(pieces, axis=2).astype(jnp.bfloat16)
 
 
+def history_kernel(v_ref, out_ref):
+    inputs, frames, _ = v_ref.shape
+    flat = v_ref.reshape(inputs * frames, LANES)
+    for t in range(frames):
+        out_ref[t] = flat[pl.ds(t, inputs, stride=frames), :].astype(jnp.bfloat16)
+
+
+def last_frames(voltages):
+    inputs, frames, _ = voltages.shape
+    last = frames // TAPS - 1
+    return pl.pallas_call(
+        history_kernel,
+        name="history",
+        grid=(SPF // LANES,),
+        in_specs=[pl.BlockSpec((inputs, TAPS, LANES), lambda i: (0, last, i))],
+        out_specs=pl.BlockSpec((TAPS, inputs, LANES), lambda i: (0, 0, i)),
+        out_shape=jax.ShapeDtypeStruct((TAPS, inputs, SPF), jnp.bfloat16),
+    )(voltages)
+
+
+def filter_kernel(first, near_ref, far_ref, near_c_ref, far_c_ref, *refs):
+    even_ref, odd_ref = refs[-2:]
+    inputs, frames, _ = near_ref.shape
+    sources = []
+    for side, (v_ref, c_ref) in enumerate(((near_ref, near_c_ref), (far_ref, far_c_ref))):
+        weights = c_ref[...].astype(jnp.float32)
+        taps = [jnp.broadcast_to(weights[k : k + 1], (UBLK, LANES)) for k in range(TAPS)]
+        hist_ref = refs[side] if first == 0 else None
+        sources.append((v_ref.reshape(inputs * frames, LANES), taps, hist_ref))
+
+    def some_inputs(step, carry):
+        begin = pl.multiple_of(step * UBLK, UBLK)
+        here = pl.ds(begin, UBLK)
+        sides = []
+        for flat, taps, hist_ref in sources:
+            window = []
+            made = []
+            for t in range(first - TAPS + 1, first + TBLK):
+                if t < 0:
+                    value = hist_ref[TAPS + t, here, :]
+                else:
+                    value = flat[pl.ds(begin * frames + t, UBLK, stride=frames), :]
+                window.append(value.astype(jnp.float32))
+                if t >= first:
+                    total = taps[0] * window[-1]
+                    for k in range(1, TAPS):
+                        total = total + taps[k] * window[-1 - k]
+                    made.append(total)
+            sides.append(made)
+        for t in range(TBLK):
+            even_ref[t, here, :] = (sides[0][t] + sides[1][t]).astype(jnp.bfloat16)
+            odd_ref[t, here, :] = (sides[0][t] - sides[1][t]).astype(jnp.bfloat16)
+        return carry
+
+    lax.fori_loop(0, inputs // UBLK, some_inputs, 0)
+
+
+def filtered_frames(block, voltages, coeffs, history=None, made=()):
+    inputs, frames, _ = voltages.shape
+    half = SPF // 2
+    steps = half // LANES
+    shape = jax.ShapeDtypeStruct((frames, inputs, half), jnp.bfloat16)
+    out_spec = pl.BlockSpec((TBLK, inputs, LANES), lambda i: (block, 0, i))
+    read = TBLK if block == 0 else frames
+    in_specs = [
+        pl.BlockSpec((inputs, read, LANES), lambda i: (0, 0, i)),
+        pl.BlockSpec((inputs, read, LANES), lambda i: (0, 0, i + steps)),
+        pl.BlockSpec((TAPS, LANES), lambda i: (0, i)),
+        pl.BlockSpec((TAPS, LANES), lambda i: (0, i + steps)),
+    ]
+    operands = [voltages, voltages, coeffs, coeffs]
+    if block == 0:
+        in_specs.append(pl.BlockSpec((TAPS, inputs, LANES), lambda i: (0, 0, i)))
+        in_specs.append(pl.BlockSpec((TAPS, inputs, LANES), lambda i: (0, 0, i + steps)))
+        operands += [history, history]
+    aliases = {}
+    for index, array in enumerate(made):
+        aliases[len(operands)] = index
+        in_specs.append(pl.BlockSpec(memory_space=pl.ANY))
+        operands.append(array)
+
+    def kernel(*refs):
+        filter_kernel(block * TBLK, *refs)
+
+    return pl.pallas_call(
+        kernel,
+        name=f"filter_{block}",
+        grid=(steps,),
+        in_specs=in_specs,
+        out_specs=[out_spec, out_spec],
+        out_shape=[shape, shape],
+        input_output_aliases=aliases,
+        compiler_params=pltpu.CompilerParams(vmem_limit_bytes=40 * 2**20),
+    )(*operands)
+
+
+def chunk_tables(parts, width):
+    depth = width // (2 * HALVES)
+    tables = []
+    for parity in range(2):
+        for piece in range(HALVES):
+            within = 2 * (piece * depth + np.arange(depth)) + parity
+            channel = (np.arange(parts)[:, None] * width + within[None, :]).reshape(-1) + CH0
+            phase = channel[:, None].astype(np.int64) * np.arange(SPF // 2)[None, :] % SPF
+            angle = phase.astype(np.float32) * np.float32(2.0 * math.pi / SPF)
+            wide = angle.astype(np.float64)
+            both = np.stack([np.cos(wide), -np.sin(wide)], axis=1)
+            both = both.reshape(-1, SPF // 2).astype(np.float32)
+            tables.append(jnp.asarray(both.astype(ml_dtypes.bfloat16)))
+    return tables
+
+
+def transform_kernel(parts, me_ref, x_ref, table_ref, *refs):
+    outs, power_ref, turned = refs[:parts], refs[parts], refs[parts + 1]
+    rows = table_ref.shape[0]
+    own = rows // parts
+    spectrum = lax.dot_general(
+        table_ref[...],
+        x_ref[...].reshape(TBLK * BLK, SPF // 2),
+        (((1,), (1,)), ((), ())),
+        preferred_element_type=jnp.float32,
+    )
+    square = jnp.zeros((8, BLK), jnp.float32)
+    for t in range(TBLK):
+        frame = spectrum[:, t * BLK : (t + 1) * BLK]
+        turned[pl.ds(t, rows, stride=TBLK), :] = frame
+        square = square + jnp.sum((frame * frame).reshape(rows // 8, 8, BLK), axis=0)
+
+    @pl.when(pl.program_id(0) == 0)
+    def _():
+        power_ref[...] = square
+
+    @pl.when(pl.program_id(0) != 0)
+    def _():
+        power_ref[...] += square
+
+    me = me_ref[0]
+    for s in range(parts):
+        there = jnp.bitwise_xor(me, s)
+        begin = pl.multiple_of(there * (own * TBLK), own * TBLK)
+        mine = turned[pl.ds(begin, own * TBLK), :]
+        outs[s][...] = mine.reshape(outs[s].shape).astype(jnp.bfloat16)
+
+
+def transformed(name, parts, me, x, table):
+    frames, inputs, _ = x.shape
+    rows = table.shape[0]
+    depth = rows // parts // 2
+    steps = frames // TBLK
+    message = jax.ShapeDtypeStruct((steps, depth, 2 * TBLK, BLK), jnp.bfloat16)
+
+    def kernel(me_ref, x_ref, table_ref, *refs):
+        transform_kernel(parts, me_ref, x_ref, table_ref, *refs)
+
+    out = pl.pallas_call(
+        kernel,
+        name=name,
+        grid_spec=pltpu.PrefetchScalarGridSpec(
+            num_scalar_prefetch=1,
+            grid=(steps,),
+            in_specs=[
+                pl.BlockSpec((TBLK, inputs, SPF // 2), lambda i, me: (i, 0, 0)),
+                pl.BlockSpec((rows, SPF // 2), lambda i, me: (0, 0)),
+            ],
+            out_specs=[
+                pl.BlockSpec((1, depth, 2 * TBLK, BLK), lambda i, me: (i, 0, 0, 0))
+                for _ in range(parts)
+            ]
+            + [pl.BlockSpec((8, BLK), lambda i, me: (0, 0))],
+            scratch_shapes=[pltpu.VMEM((rows * TBLK, BLK), jnp.float32)],
+        ),
+        out_shape=[message] * parts + [jax.ShapeDtypeStruct((8, BLK), jnp.float32)],
+        compiler_params=pltpu.CompilerParams(vmem_limit_bytes=40 * 2**20),
+    )(me, x, table)
+    return out[:parts], out[parts]
+
+
+def correlate_kernel(parts, steps, me_ref, *refs):
+    messages = refs[:parts]
+    row_ref = refs[parts]
+    out_ref, plain, other, columns = refs[-4:]
+    blocks = INPUTS // BLK
+    freq = parts // blocks
+    span = steps * 2 * TBLK
+    me = me_ref[0]
+
+    @pl.when(pl.program_id(0) == 0)
+    def _():
+        for r in range(blocks):
+            wide = jnp.broadcast_to(row_ref[r : r + 1, :], (BLK, BLK))
+            columns[r * BLK : (r + 1) * BLK, :] = wide.T
+
+    for s in range(parts):
+        source = jnp.bitwise_xor(me, s)
+        block, place = source // freq, source % freq
+        for step in range(steps):
+            begin = pl.multiple_of(place * span + step * 2 * TBLK, 2 * TBLK)
+            real = messages[s][step, 0, :TBLK, :]
+            imag = messages[s][step, 0, TBLK:, :]
+            plain[block, pl.ds(begin, TBLK), :] = real
+            plain[block, pl.ds(begin + TBLK, TBLK), :] = imag
+            other[block, pl.ds(begin, TBLK), :] = -imag
+            other[block, pl.ds(begin + TBLK, TBLK), :] = real
+
+    sides = [plain[r].T for r in range(blocks)]
+    for c in range(blocks):
+        weights = jnp.concatenate([plain[c], other[c]], axis=1)
+        lhs = sides[0] if c == 0 else jnp.concatenate(sides[: c + 1], axis=0)
+        both = jnp.dot(lhs, weights, preferred_element_type=jnp.float32)
+        row_gain = row_ref[c : c + 1, :]
+        for r in range(c + 1):
+            pair = r * blocks - r * (r - 1) // 2 + (c - r)
+            gain = columns[r * BLK : (r + 1) * BLK, :] * (row_gain * (1.0 / (freq * steps * TBLK)))
+            for part in range(2):
+                piece = both[r * BLK : (r + 1) * BLK, part * BLK : (part + 1) * BLK]
+                out_ref[0, part, pair] = (piece * gain).astype(jnp.bfloat16)
+
+
+def correlated(name, me, messages, gains, chunk, width, before=None):
+    parts = len(messages)
+    steps, depth, _, _ = messages[0].shape
+    blocks = INPUTS // BLK
+    pairs = blocks * (blocks + 1) // 2
+    parity, piece = chunk // HALVES, chunk % HALVES
+    span = parts // blocks * steps * 2 * TBLK
+    in_specs = [
+        pl.BlockSpec((steps, 1, 2 * TBLK, BLK), lambda i, me: (0, i, 0, 0)) for _ in range(parts)
+    ] + [pl.BlockSpec((blocks, BLK), lambda i, me: (0, 0))]
+    operands = [me, *messages, gains]
+    aliases = {}
+    if before is not None:
+        aliases[len(operands)] = 0
+        in_specs.append(pl.BlockSpec(memory_space=pl.ANY))
+        operands.append(before)
+
+    def kernel(me_ref, *refs):
+        correlate_kernel(parts, steps, me_ref, *refs)
+
+    return pl.pallas_call(
+        kernel,
+        name=name,
+        grid_spec=pltpu.PrefetchScalarGridSpec(
+            num_scalar_prefetch=1,
+            grid=(depth,),
+            in_specs=in_specs,
+            out_specs=pl.BlockSpec(
+                (1, 2, pairs, BLK, BLK),
+                lambda i, me: (2 * (piece * depth + i) + parity, 0, 0, 0, 0),
+            ),
+            scratch_shapes=[
+                pltpu.VMEM((blocks, span, BLK), jnp.bfloat16),
+                pltpu.VMEM((blocks, span, BLK), jnp.bfloat16),
+                pltpu.VMEM((INPUTS, BLK), jnp.float32),
+            ],
+        ),
+        out_shape=jax.ShapeDtypeStruct((width, 2, pairs, BLK, BLK), jnp.bfloat16),
+        input_output_aliases=aliases,
+        compiler_params=pltpu.CompilerParams(vmem_limit_bytes=40 * 2**20),
+    )(*operands)
+
+
+def exchanged(messages):
+    axes = ("inp", "freq")
+    parts = len(messages)
+    arrived = [messages[0]]
+    for s in range(1, parts):
+        pairs = [(i, i ^ s) for i in range(parts)]
+        arrived.append(lax.ppermute(messages[s], axes, pairs))
+    return arrived
+
+
+def per_device(voltages, coeffs):
+    freq_count = lax.axis_size("freq")
+    parts = lax.axis_size("inp") * freq_count
+    inputs, frames, _ = voltages.shape
+    width = CH // parts
+    chunks = 2 * HALVES
+    fits = (
+        inputs == BLK
+        and frames == 2 * TBLK
+        and TAPS <= TBLK
+        and parts & (parts - 1) == 0
+        and width % (2 * HALVES) == 0
+        and parts * BLK == INPUTS * freq_count
+        and freq_count * frames * 2 == LANES
+    )
+    if not fits:
+        return any_sizes(voltages, coeffs)
+    me = lax.axis_index("inp") * freq_count + lax.axis_index("freq")
+    me = me.astype(jnp.int32).reshape(1)
+    history = passed_along(last_frames(voltages), "freq", 1)
+    made = filtered_frames(1, voltages, coeffs)
+    made = filtered_frames(0, voltages, coeffs, history, made)
+    tables = chunk_tables(parts, width)
+    arrived = []
+    power = 0.0
+    for chunk in range(chunks):
+        messages, squares = transformed(
+            f"spectra_{chunk}", parts, me, made[chunk // HALVES], tables[chunk]
+        )
+        power = power + jnp.sum(squares, axis=0)
+        arrived.append(exchanged(messages))
+    shared = lax.all_gather(power, ("inp", "freq"))
+    shared = jnp.sum(shared.reshape(parts // freq_count, freq_count, BLK), axis=1)
+    gains = 1.0 / jnp.sqrt(shared / (frames * freq_count * CH) + 1e-06)
+    out = None
+    for chunk in range(chunks):
+        out = correlated(f"correlate_{chunk}", me, arrived[chunk], gains, chunk, width, out)
+    return out
+
+
 def solution(mesh):
     in_specs = (P(("grp", "inp"), "freq", None), P())
     out_specs = P(("grp", "inp", "freq"), None, None, None, None)

time: 869 us -> 332 us (0.38)
  local copies, waits for them, and re-layouts: 299 us -> 26 us
  other arithmetic: 214 us -> 0.09 us
  blocking collectives: 192 us -> 19.4 us
  matrix products: 152 us -> 0 us
  starting transfers between devices: 2.9 us -> 125 us
  Pallas kernels: 0 us -> 115 us
  waiting for transfers between devices: 0.01 us -> 45.2 us
    all_to_all x1 -> x0, blocking collectives: 189 us -> none  [per_device(): lax.all_to_all(scaled[None], ('inp', 'freq'), split_axis=2, concat_axis=0...]
    dot_general x17 -> x0, matrix products: 152 us -> none  [the longest x8 75.3 us: per_device(): jnp.einsum('cut,cmt->cum', row_panel, other[:, row_index * BLK:], preferr...]
    convert_element_type x4 -> x0, other arithmetic: 141 us -> none  [the longest x1 109 us: per_device(): summed.astype(jnp.bfloat16).reshape(inputs_here * frames_here, SPF)]
    ppermute x0 -> x60, starting transfers between devices: none -> 120 us  [exchanged(): arrived.append(lax.ppermute(messages[s], axes, pairs))]
    pallas_call x0 -> x11, Pallas kernels: none -> 115 us  [the longest x4 45.8 us: correlated(): pl.pallas_call(kernel, name=name, grid_spec=pltpu.PrefetchScalarGridSpec(...]
    another operation x3 -> x0, local copies, waits for them, and re-layouts: 92.4 us -> none  [the longest x1 49.6 us: per_device(): return jnp.stack(pieces, axis=2).astype(jnp.bfloat16)]
    another operation x10 -> x0, other arithmetic: 64.1 us -> none
    unnamed x103 -> x166, local copies, waits for them, and re-layouts: 81.1 us -> 26 us
  transfers between devices with their start and end apart: 1 -> 61, of which waited for: 0 -> 12; matrix products, arithmetic and copies ran while one was open for 5% -> 0% of each run, Pallas kernels for 0% -> 21%
where the time goes in v1:
time: 332 us; the launch traced here: 331 us
  starting transfers between devices  125 us (38%)
  Pallas kernels  115 us (35%)
  waiting for transfers between devices  45.2 us (14%)
  local copies, waits for them, and re-layouts  26 us (8%)
  blocking collectives  19.4 us (6%)
    ppermute x60, starting transfers between devices, exchanged(): arrived.append(lax.ppermute(messages[s], axes, pairs))  120 us
    pallas_call x4, Pallas kernels, correlated(): pl.pallas_call(kernel, name=name, grid_spec=pltpu.PrefetchScalarGridSpec(...  45.8 us
    ppermute x60, waiting for transfers between devices, exchanged(): arrived.append(lax.ppermute(messages[s], axes, pairs))  45.2 us
    pallas_call x2, Pallas kernels, filtered_frames(): pl.pallas_call(kernel, name=f'filter_{block}', grid=(steps,), in_specs=in...  42.1 us
    unnamed x166, local copies, waits for them, and re-layouts  26 us
    all_gather x1, blocking collectives, per_device(): shared = lax.all_gather(power, ('inp', 'freq'))  19.4 us
    pallas_call x4, Pallas kernels, transformed(): pl.pallas_call(kernel, name=name, grid_spec=pltpu.PrefetchScalarGridSpec(...  15.7 us
    pallas_call x1, Pallas kernels, last_frames(): pl.pallas_call(history_kernel, name='history', grid=(SPF // LANES,), in_s...  11.6 us
  transfers between devices with their start and end apart: 61, of which 12 were waited for; matrix products, arithmetic and copies ran while one was open for 0% of the time, Pallas kernels for 21%

profile of v1, /device:TPU:0, one launch (start us, length us, event | category | flops | bytes accessed | tf_op | source)
XLA Modules:
  0.0 331.4 jit_solution(8312952375239575290)
XLA Ops:
  0.0 11.6 %history.1 = bf16[8,128,2048]{2,1,0:T(8,128)(2,1)} custom-call(s32[128,32,2048]{2,1,0:T(8,128)} %refs_1_.3), custom_call_target="tpu_custom_call" | custom-call | tf_op jit(solution)/shard_map/history/pallas_call | solution.py:100
  11.6 4.4 %collective-permute-start = (bf16[8,128,2048]{2,1,0:T(8,128)(2,1)}, bf16[8,128,2048]{2,1,0:T(8,128)(2,1)}, u32[]{:S(2)}, u32[]{:S(2)}) collective-permute-start(bf16[8,128,2048]{2,1,0:T(8,128)(2,1)} %history.1), channel_id=1, source_target_pairs={{0,1},{2,3},{4,5},{6,7},{8,9},{10,11},{12,13},{14,15},{16,17},{18,... | collective-permute-start | bytes 12582920 | tf_op jit(solution)/shard_map/ppermute | solution.py:27
  16.0 24.9 %filter_1.1 = (bf16[32,128,1024]{2,1,0:T(8,128)(2,1)S(1)}, bf16[32,128,1024]{2,1,0:T(8,128)(2,1)}) custom-call(s32[128,32,2048]{2,1,0:T(8,128)} %refs_1_.3, s32[128,32,2048]{2,1,0:T(8,128)} %refs_1_.3, s32[8,2048]{1,0:T(8,128)S(1)} %copy-done.4, s32[8,2048]{1,0:T(8,128)S(1)} %copy-done.4), custom_call_target="tpu_custom_call" | custom-call | tf_op jit(solution)/shard_map/filter_1/pallas_call | solution.py:174
  47.6 17.2 %filter_0.1 = (bf16[32,128,1024]{2,1,0:T(8,128)(2,1)S(1)}, bf16[32,128,1024]{2,1,0:T(8,128)(2,1)}) custom-call(s32[128,32,2048]{2,1,0:T(8,128)} %refs_1_.3, s32[128,32,2048]{2,1,0:T(8,128)} %refs_1_.3, s32[8,2048]{1,0:T(8,128)S(1)} %copy-done.4, s32[8,2048]{1,0:T(8,128)S(1)} %copy-done.4, ...), custom_call_target="tpu_custom_call", output_to_operand_aliasing={{0}: (6, {}), {1}: (7, {})} | custom-call | tf_op jit(solution)/shard_map/filter_0/pallas_call | solution.py:174
  71.6 3.7 %spectra_2.1 = (bf16[2,8,32,128]{3,2,1,0:T(8,128)(2,1)S(1)}, bf16[2,8,32,128]{3,2,1,0:T(8,128)(2,1)S(1)}, bf16[2,8,32,128]{3,2,1,0:T(8,128)(2,1)S(1)}, bf16[2,8,...) custom-call(s32[1]{0:T(128)} %bitcast.me_ref, ...), custom_call_target="tpu_custom_call" | custom-call | tf_op jit(solution)/shard_map/spectra_2/pallas_call | solution.py:244
  90.8 5.9 %collective-permute-done.21.refs_6_ = bf16[2,8,32,128]{3,2,1,0:T(8,128)(2,1)S(1)} collective-permute-done((bf16[2,8,32,128]{3,2,1,0:T(8,128)(2,1)S(1)}, bf16[2,8,32,128]{3,2,1,0:T(8,128)(2,1)S(1)}, u32[]{:S(2)}, u32[]{:S(2)}) %collective-permute-start.21) | collective-permute-done | bytes 131104 | tf_op jit(solution)/shard_map/ppermute | solution.py:357
  102.0 13.3 %collective-permute-start.29 = (bf16[2,8,32,128]{3,2,1,0:T(8,128)(2,1)S(1)}, bf16[2,8,32,128]{3,2,1,0:T(8,128)(2,1)S(1)}, u32[]{:S(2)}, u32[]{:S(2)}) collective-permute-start(bf16[2,8,32,128]{3,2,1,0:T(8,128)(2,1)S(1)} %get-tuple-element.115), channel_id=1, source_target_pairs={{0,14},{1,15},{2,12},{3,13},{4,10},{5,11},{6,8},{7,9},{8,6},{9,7},... | collective-permute-start | bytes 393224 | tf_op jit(solution)/shard_map/ppermute | solution.py:357
  117.8 3.7 %spectra_3.1 = (bf16[2,8,32,128]{3,2,1,0:T(8,128)(2,1)S(1)}, bf16[2,8,32,128]{3,2,1,0:T(8,128)(2,1)S(1)}, bf16[2,8,32,128]{3,2,1,0:T(8,128)(2,1)S(1)}, bf16[2,8,...) custom-call(s32[1]{0:T(128)} %bitcast.me_ref, ...), custom_call_target="tpu_custom_call" | custom-call | tf_op jit(solution)/shard_map/spectra_3/pallas_call | solution.py:244
  125.5 7.1 %collective-permute-start.4 = (bf16[2,8,32,128]{3,2,1,0:T(8,128)(2,1)S(1)}, bf16[2,8,32,128]{3,2,1,0:T(8,128)(2,1)S(1)}, u32[]{:S(2)}, u32[]{:S(2)}) collective-permute-start(bf16[2,8,32,128]{3,2,1,0:T(8,128)(2,1)S(1)} %get-tuple-element.84), channel_id=1, source_target_pairs={{0,4},{1,5},{2,6},{3,7},{4,0},{5,1},{6,2},{7,3},{8,12},{9,13},{10,... | collective-permute-start | bytes 393224 | tf_op jit(solution)/shard_map/ppermute | solution.py:357
  141.9 3.5 %collective-permute-start.10 = (bf16[2,8,32,128]{3,2,1,0:T(8,128)(2,1)S(1)}, bf16[2,8,32,128]{3,2,1,0:T(8,128)(2,1)S(1)}, u32[]{:S(2)}, u32[]{:S(2)}) collective-permute-start(bf16[2,8,32,128]{3,2,1,0:T(8,128)(2,1)S(1)} %get-tuple-element.90), channel_id=1, source_target_pairs={{0,10},{1,11},{2,8},{3,9},{4,14},{5,15},{6,12},{7,13},{8,2},{9,3},... | collective-permute-start | bytes 393224 | tf_op jit(solution)/shard_map/ppermute | solution.py:357
  145.4 3.8 %spectra_1.1 = (bf16[2,8,32,128]{3,2,1,0:T(8,128)(2,1)S(1)}, bf16[2,8,32,128]{3,2,1,0:T(8,128)(2,1)S(1)}, bf16[2,8,32,128]{3,2,1,0:T(8,128)(2,1)S(1)}, bf16[2,8,...) custom-call(s32[1]{0:T(128)} %bitcast.me_ref, ...), custom_call_target="tpu_custom_call" | custom-call | tf_op jit(solution)/shard_map/spectra_1/pallas_call | solution.py:244
  152.4 4.7 %collective-permute-start.34 = (bf16[2,8,32,128]{3,2,1,0:T(8,128)(2,1)S(1)}, bf16[2,8,32,128]{3,2,1,0:T(8,128)(2,1)S(1)}, u32[]{:S(2)}, u32[]{:S(2)}) collective-permute-start(bf16[2,8,32,128]{3,2,1,0:T(8,128)(2,1)S(1)} %get-tuple-element.121), channel_id=1, source_target_pairs={{0,4},{1,5},{2,6},{3,7},{4,0},{5,1},{6,2},{7,3},{8,12},{9,13},{10,... | collective-permute-start | bytes 393224 | tf_op jit(solution)/shard_map/ppermute | solution.py:357
  169.2 5.6 %collective-permute-done.36.refs_6_ = bf16[2,8,32,128]{3,2,1,0:T(8,128)(2,1)S(1)} collective-permute-done((bf16[2,8,32,128]{3,2,1,0:T(8,128)(2,1)S(1)}, bf16[2,8,32,128]{3,2,1,0:T(8,128)(2,1)S(1)}, u32[]{:S(2)}, u32[]{:S(2)}) %collective-permute-start.36) | collective-permute-done | bytes 131104 | tf_op jit(solution)/shard_map/ppermute | solution.py:357
  182.0 8.1 %collective-permute-done.39.refs_9_ = bf16[2,8,32,128]{3,2,1,0:T(8,128)(2,1)S(1)} collective-permute-done((bf16[2,8,32,128]{3,2,1,0:T(8,128)(2,1)S(1)}, bf16[2,8,32,128]{3,2,1,0:T(8,128)(2,1)S(1)}, u32[]{:S(2)}, u32[]{:S(2)}) %collective-permute-start.39) | collective-permute-done | bytes 131104 | tf_op jit(solution)/shard_map/ppermute | solution.py:357
  195.6 4.4 %spectra_0.1 = (bf16[2,8,32,128]{3,2,1,0:T(8,128)(2,1)S(1)}, bf16[2,8,32,128]{3,2,1,0:T(8,128)(2,1)S(1)}, bf16[2,8,32,128]{3,2,1,0:T(8,128)(2,1)S(1)}, bf16[2,8,...) custom-call(s32[1]{0:T(128)} %bitcast.me_ref, ...), custom_call_target="tpu_custom_call" | custom-call | tf_op jit(solution)/shard_map/spectra_0/pallas_call | solution.py:244
  207.1 4.2 %collective-permute-start.49 = (bf16[2,8,32,128]{3,2,1,0:T(8,128)(2,1)S(1)}, bf16[2,8,32,128]{3,2,1,0:T(8,128)(2,1)S(1)}, u32[]{:S(2)}, u32[]{:S(2)}) collective-permute-start(bf16[2,8,32,128]{3,2,1,0:T(8,128)(2,1)S(1)} %get-tuple-element.137), channel_id=1, source_target_pairs={{0,4},{1,5},{2,6},{3,7},{4,0},{5,1},{6,2},{7,3},{8,12},{9,13},{10,... | collective-permute-start | bytes 393224 | tf_op jit(solution)/shard_map/ppermute | solution.py:357
  222.4 3.8 %collective-permute-done.51.refs_6_ = bf16[2,8,32,128]{3,2,1,0:T(8,128)(2,1)S(1)} collective-permute-done((bf16[2,8,32,128]{3,2,1,0:T(8,128)(2,1)}, bf16[2,8,32,128]{3,2,1,0:T(8,128)(2,1)S(1)}, u32[]{:S(2)}, u32[]{:S(2)}) %collective-permute-start.51) | collective-permute-done | bytes 131104 | tf_op jit(solution)/shard_map/ppermute | solution.py:357
  231.7 11.4 %collective-permute-done.54.refs_9_ = bf16[2,8,32,128]{3,2,1,0:T(8,128)(2,1)S(1)} collective-permute-done((bf16[2,8,32,128]{3,2,1,0:T(8,128)(2,1)}, bf16[2,8,32,128]{3,2,1,0:T(8,128)(2,1)S(1)}, u32[]{:S(2)}, u32[]{:S(2)}) %collective-permute-start.54) | collective-permute-done | bytes 131104 | tf_op jit(solution)/shard_map/ppermute | solution.py:357
  248.5 19.4 %all-gather.1 = f32[16,1,128]{2,1,0:T(1,128)S(1)} all-gather(f32[1,1,128]{2,1,0:T(1,128)S(1)} %add_bitcast_fusion), channel_id=2, replica_groups=mesh['grp'=2,'inp'=8,'freq'=2] {'inp','freq'}, dimensions={0}, use_global_device_ids=true | all-gather | bytes 8704 | tf_op jit(solution)/shard_map/all_gather | solution.py:392
  267.9 9.0 %collective-permute-start.11 = (bf16[2,8,32,128]{3,2,1,0:T(8,128)(2,1)}, bf16[2,8,32,128]{3,2,1,0:T(8,128)(2,1)S(1)}, u32[]{:S(2)}, u32[]{:S(2)}) collective-permute-start(bf16[2,8,32,128]{3,2,1,0:T(8,128)(2,1)} %copy-done.77), channel_id=1, source_target_pairs={{0,11},{1,10},{2,9},{3,8},{4,15},{5,14},{6,13},{7,12},{8,3},{9,2},... | collective-permute-start | bytes 393224 | tf_op jit(solution)/shard_map/ppermute | solution.py:357
  285.1 11.5 %correlate_0.1.refs_17_ = bf16[32,2,36,128,128]{4,3,2,1,0:T(8,128)(2,1)} custom-call(s32[1]{0:T(128)} %bitcast.me_ref, bf16[2,8,32,128]{3,2,1,0:T(8,128)(2,1)S(1)} %get-tuple-element.133.refs_0_, bf16[2,8,32,128]{3,2,1,0:T(8,128)(2,1)S(1)} %collective-permute-done.46.refs_1_, bf16[2,8,32,128]{3,2,1,0:T(8,128)(2,1)S(1)} %collective-permute-done.47.refs_2_, ...), custom_call_target="tpu_custom_call" | custom-call | tf_op jit(solution)/shard_map/correlate_0/pallas_call | solution.py:328
  296.7 11.5 %correlate_1.1.refs_17_ = bf16[32,2,36,128,128]{4,3,2,1,0:T(8,128)(2,1)} custom-call(s32[1]{0:T(128)} %bitcast.me_ref, bf16[2,8,32,128]{3,2,1,0:T(8,128)(2,1)S(1)} %copy-done.42, bf16[2,8,32,128]{3,2,1,0:T(8,128)(2,1)S(1)} %copy-done.44, bf16[2,8,32,128]{3,2,1,0:T(8,128)(2,1)S(1)} %copy-done.46, ...), custom_call_target="tpu_custom_call", output_to_operand_aliasing={{}: (18, {})} | custom-call | tf_op jit(solution)/shard_map/correlate_1/pallas_call | solution.py:328
  308.3 11.5 %correlate_2.1.refs_17_ = bf16[32,2,36,128,128]{4,3,2,1,0:T(8,128)(2,1)} custom-call(s32[1]{0:T(128)} %bitcast.me_ref, bf16[2,8,32,128]{3,2,1,0:T(8,128)(2,1)S(1)} %get-tuple-element.101.refs_0_, bf16[2,8,32,128]{3,2,1,0:T(8,128)(2,1)S(1)} %collective-permute-done.16.refs_1_, ...), custom_call_target="tpu_custom_call", output_to_operand_aliasing={{}: (18, {})} | custom-call | tf_op jit(solution)/shard_map/correlate_2/pallas_call | solution.py:328
  319.9 11.5 %correlate_3.1 = bf16[32,2,36,128,128]{4,3,2,1,0:T(8,128)(2,1)} custom-call(s32[1]{0:T(128)} %bitcast.me_ref, bf16[2,8,32,128]{3,2,1,0:T(8,128)(2,1)S(1)} %copy-done.18, bf16[2,8,32,128]{3,2,1,0:T(8,128)(2,1)S(1)} %copy-done.22, bf16[2,8,32,128]{3,2,1,0:T(8,128)(2,1)S(1)} %copy-done.24, ...), custom_call_target="tpu_custom_call", output_to_operand_aliasing={{}: (18, {})} | custom-call | tf_op jit(solution)/shard_map/correlate_3/pallas_call | solution.py:328
  (284 shorter events, 114.8 us)
Async XLA Ops:
  11.6 32.7 %collective-permute-start = (bf16[8,128,2048]{2,1,0:T(8,128)(2,1)}, bf16[8,128,2048]{2,1,0:T(8,128)(2,1)}, u32[]{:S(2)}, u32[]{:S(2)}) collective-permute-start(bf16[8,128,2048]{2,1,0:T(8,128)(2,1)} %history.1), channel_id=1, source_target_pairs={{0,1},{2,3},{4,5},{6,7},{8,9},{10,11},{12,13},{14,15},{16,17},{18,... | collective-permute-start | bytes 12582920 | tf_op jit(solution)/shard_map/ppermute | solution.py:27
  87.5 27.8 %collective-permute-start.25 = (bf16[2,8,32,128]{3,2,1,0:T(8,128)(2,1)S(1)}, bf16[2,8,32,128]{3,2,1,0:T(8,128)(2,1)S(1)}, u32[]{:S(2)}, u32[]{:S(2)}) collective-permute-start(bf16[2,8,32,128]{3,2,1,0:T(8,128)(2,1)S(1)} %get-tuple-element.111), channel_id=1, source_target_pairs={{0,10},{1,11},{2,8},{3,9},{4,14},{5,15},{6,12},{7,13},{8,2},{9,3},... | collective-permute-start | bytes 393224 | tf_op jit(solution)/shard_map/ppermute | solution.py:357
  96.7 26.1 %collective-permute-start.26 = (bf16[2,8,32,128]{3,2,1,0:T(8,128)(2,1)S(1)}, bf16[2,8,32,128]{3,2,1,0:T(8,128)(2,1)S(1)}, u32[]{:S(2)}, u32[]{:S(2)}) collective-permute-start(bf16[2,8,32,128]{3,2,1,0:T(8,128)(2,1)S(1)} %get-tuple-element.112), channel_id=1, source_target_pairs={{0,11},{1,10},{2,9},{3,8},{4,15},{5,14},{6,13},{7,12},{8,3},{9,2},... | collective-permute-start | bytes 393224 | tf_op jit(solution)/shard_map/ppermute | solution.py:357
  98.4 25.6 %collective-permute-start.27 = (bf16[2,8,32,128]{3,2,1,0:T(8,128)(2,1)S(1)}, bf16[2,8,32,128]{3,2,1,0:T(8,128)(2,1)S(1)}, u32[]{:S(2)}, u32[]{:S(2)}) collective-permute-start(bf16[2,8,32,128]{3,2,1,0:T(8,128)(2,1)S(1)} %get-tuple-element.113), channel_id=1, source_target_pairs={{0,12},{1,13},{2,14},{3,15},{4,8},{5,9},{6,10},{7,11},{8,4},{9,5},... | collective-permute-start | bytes 393224 | tf_op jit(solution)/shard_map/ppermute | solution.py:357
  99.8 25.7 %collective-permute-start.28 = (bf16[2,8,32,128]{3,2,1,0:T(8,128)(2,1)S(1)}, bf16[2,8,32,128]{3,2,1,0:T(8,128)(2,1)S(1)}, u32[]{:S(2)}, u32[]{:S(2)}) collective-permute-start(bf16[2,8,32,128]{3,2,1,0:T(8,128)(2,1)S(1)} %get-tuple-element.114), channel_id=1, source_target_pairs={{0,13},{1,12},{2,15},{3,14},{4,9},{5,8},{6,11},{7,10},{8,5},{9,4},... | collective-permute-start | bytes 393224 | tf_op jit(solution)/shard_map/ppermute | solution.py:357
  102.0 23.5 %collective-permute-start.29 = (bf16[2,8,32,128]{3,2,1,0:T(8,128)(2,1)S(1)}, bf16[2,8,32,128]{3,2,1,0:T(8,128)(2,1)S(1)}, u32[]{:S(2)}, u32[]{:S(2)}) collective-permute-start(bf16[2,8,32,128]{3,2,1,0:T(8,128)(2,1)S(1)} %get-tuple-element.115), channel_id=1, source_target_pairs={{0,14},{1,15},{2,12},{3,13},{4,10},{5,11},{6,8},{7,9},{8,6},{9,7},... | collective-permute-start | bytes 393224 | tf_op jit(solution)/shard_map/ppermute | solution.py:357
  141.9 18.4 %collective-permute-start.10 = (bf16[2,8,32,128]{3,2,1,0:T(8,128)(2,1)S(1)}, bf16[2,8,32,128]{3,2,1,0:T(8,128)(2,1)S(1)}, u32[]{:S(2)}, u32[]{:S(2)}) collective-permute-start(bf16[2,8,32,128]{3,2,1,0:T(8,128)(2,1)S(1)} %get-tuple-element.90), channel_id=1, source_target_pairs={{0,10},{1,11},{2,8},{3,9},{4,14},{5,15},{6,12},{7,13},{8,2},{9,3},... | collective-permute-start | bytes 393224 | tf_op jit(solution)/shard_map/ppermute | solution.py:357
  165.2 24.9 %collective-permute-start.39 = (bf16[2,8,32,128]{3,2,1,0:T(8,128)(2,1)S(1)}, bf16[2,8,32,128]{3,2,1,0:T(8,128)(2,1)S(1)}, u32[]{:S(2)}, u32[]{:S(2)}) collective-permute-start(bf16[2,8,32,128]{3,2,1,0:T(8,128)(2,1)S(1)} %get-tuple-element.126), channel_id=1, source_target_pairs={{0,9},{1,8},{2,11},{3,10},{4,13},{5,12},{6,15},{7,14},{8,1},{9,0},... | collective-permute-start | bytes 393224 | tf_op jit(solution)/shard_map/ppermute | solution.py:357
  166.8 26.7 %collective-permute-start.40 = (bf16[2,8,32,128]{3,2,1,0:T(8,128)(2,1)S(1)}, bf16[2,8,32,128]{3,2,1,0:T(8,128)(2,1)S(1)}, u32[]{:S(2)}, u32[]{:S(2)}) collective-permute-start(bf16[2,8,32,128]{3,2,1,0:T(8,128)(2,1)S(1)} %get-tuple-element.127), channel_id=1, source_target_pairs={{0,10},{1,11},{2,8},{3,9},{4,14},{5,15},{6,12},{7,13},{8,2},{9,3},... | collective-permute-start | bytes 393224 | tf_op jit(solution)/shard_map/ppermute | solution.py:357
  175.4 26.6 %collective-permute-start.41 = (bf16[2,8,32,128]{3,2,1,0:T(8,128)(2,1)S(1)}, bf16[2,8,32,128]{3,2,1,0:T(8,128)(2,1)S(1)}, u32[]{:S(2)}, u32[]{:S(2)}) collective-permute-start(bf16[2,8,32,128]{3,2,1,0:T(8,128)(2,1)S(1)} %get-tuple-element.128), channel_id=1, source_target_pairs={{0,11},{1,10},{2,9},{3,8},{4,15},{5,14},{6,13},{7,12},{8,3},{9,2},... | collective-permute-start | bytes 393224 | tf_op jit(solution)/shard_map/ppermute | solution.py:357
  178.0 25.7 %collective-permute-start.42 = (bf16[2,8,32,128]{3,2,1,0:T(8,128)(2,1)S(1)}, bf16[2,8,32,128]{3,2,1,0:T(8,128)(2,1)S(1)}, u32[]{:S(2)}, u32[]{:S(2)}) collective-permute-start(bf16[2,8,32,128]{3,2,1,0:T(8,128)(2,1)S(1)} %get-tuple-element.129), channel_id=1, source_target_pairs={{0,12},{1,13},{2,14},{3,15},{4,8},{5,9},{6,10},{7,11},{8,4},{9,5},... | collective-permute-start | bytes 393224 | tf_op jit(solution)/shard_map/ppermute | solution.py:357
  180.3 25.5 %collective-permute-start.43 = (bf16[2,8,32,128]{3,2,1,0:T(8,128)(2,1)S(1)}, bf16[2,8,32,128]{3,2,1,0:T(8,128)(2,1)S(1)}, u32[]{:S(2)}, u32[]{:S(2)}) collective-permute-start(bf16[2,8,32,128]{3,2,1,0:T(8,128)(2,1)S(1)} %get-tuple-element.130), channel_id=1, source_target_pairs={{0,13},{1,12},{2,15},{3,14},{4,9},{5,8},{6,11},{7,10},{8,5},{9,4},... | collective-permute-start | bytes 393224 | tf_op jit(solution)/shard_map/ppermute | solution.py:357
  218.5 24.6 %collective-permute-start.54 = (bf16[2,8,32,128]{3,2,1,0:T(8,128)(2,1)}, bf16[2,8,32,128]{3,2,1,0:T(8,128)(2,1)S(1)}, u32[]{:S(2)}, u32[]{:S(2)}) collective-permute-start(bf16[2,8,32,128]{3,2,1,0:T(8,128)(2,1)} %get-tuple-element.142), channel_id=1, source_target_pairs={{0,9},{1,8},{2,11},{3,10},{4,13},{5,12},{6,15},{7,14},{8,1},{9,0},... | collective-permute-start | bytes 393224 | tf_op jit(solution)/shard_map/ppermute | solution.py:357
  219.4 27.4 %collective-permute-start.55 = (bf16[2,8,32,128]{3,2,1,0:T(8,128)(2,1)}, bf16[2,8,32,128]{3,2,1,0:T(8,128)(2,1)S(1)}, u32[]{:S(2)}, u32[]{:S(2)}) collective-permute-start(bf16[2,8,32,128]{3,2,1,0:T(8,128)(2,1)} %get-tuple-element.143), channel_id=1, source_target_pairs={{0,10},{1,11},{2,8},{3,9},{4,14},{5,15},{6,12},{7,13},{8,2},{9,3},... | collective-permute-start | bytes 393224 | tf_op jit(solution)/shard_map/ppermute | solution.py:357
  226.2 41.7 %collective-permute-start.56 = (bf16[2,8,32,128]{3,2,1,0:T(8,128)(2,1)}, bf16[2,8,32,128]{3,2,1,0:T(8,128)(2,1)S(1)}, u32[]{:S(2)}, u32[]{:S(2)}) collective-permute-start(bf16[2,8,32,128]{3,2,1,0:T(8,128)(2,1)} %copy-done.80), channel_id=1, source_target_pairs={{0,11},{1,10},{2,9},{3,8},{4,15},{5,14},{6,13},{7,12},{8,3},{9,2},... | collective-permute-start | bytes 393224 | tf_op jit(solution)/shard_map/ppermute | solution.py:357
  227.9 49.0 %collective-permute-start.57 = (bf16[2,8,32,128]{3,2,1,0:T(8,128)(2,1)}, bf16[2,8,32,128]{3,2,1,0:T(8,128)(2,1)S(1)}, u32[]{:S(2)}, u32[]{:S(2)}) collective-permute-start(bf16[2,8,32,128]{3,2,1,0:T(8,128)(2,1)} %copy-done.79), channel_id=1, source_target_pairs={{0,12},{1,13},{2,14},{3,15},{4,8},{5,9},{6,10},{7,11},{8,4},{9,5},... | collective-permute-start | bytes 393224 | tf_op jit(solution)/shard_map/ppermute | solution.py:357
  230.5 47.9 %collective-permute-start.58 = (bf16[2,8,32,128]{3,2,1,0:T(8,128)(2,1)}, bf16[2,8,32,128]{3,2,1,0:T(8,128)(2,1)S(1)}, u32[]{:S(2)}, u32[]{:S(2)}) collective-permute-start(bf16[2,8,32,128]{3,2,1,0:T(8,128)(2,1)} %get-tuple-element.146), channel_id=1, source_target_pairs={{0,13},{1,12},{2,15},{3,14},{4,9},{5,8},{6,11},{7,10},{8,5},{9,4},... | collective-permute-start | bytes 393224 | tf_op jit(solution)/shard_map/ppermute | solution.py:357
  243.1 37.2 %collective-permute-start.59 = (bf16[2,8,32,128]{3,2,1,0:T(8,128)(2,1)}, bf16[2,8,32,128]{3,2,1,0:T(8,128)(2,1)S(1)}, u32[]{:S(2)}, u32[]{:S(2)}) collective-permute-start(bf16[2,8,32,128]{3,2,1,0:T(8,128)(2,1)} %get-tuple-element.147), channel_id=1, source_target_pairs={{0,14},{1,15},{2,12},{3,13},{4,10},{5,11},{6,8},{7,9},{8,6},{9,7},... | collective-permute-start | bytes 393224 | tf_op jit(solution)/shard_map/ppermute | solution.py:357
  246.7 36.0 %collective-permute-start.60 = (bf16[2,8,32,128]{3,2,1,0:T(8,128)(2,1)}, bf16[2,8,32,128]{3,2,1,0:T(8,128)(2,1)S(1)}, u32[]{:S(2)}, u32[]{:S(2)}) collective-permute-start(bf16[2,8,32,128]{3,2,1,0:T(8,128)(2,1)} %copy-done.78), channel_id=1, source_target_pairs={{0,15},{1,14},{2,13},{3,12},{4,11},{5,10},{6,9},{7,8},{8,7},{9,6},... | collective-permute-start | bytes 393224 | tf_op jit(solution)/shard_map/ppermute | solution.py:357
  267.9 51.8 %collective-permute-start.11 = (bf16[2,8,32,128]{3,2,1,0:T(8,128)(2,1)}, bf16[2,8,32,128]{3,2,1,0:T(8,128)(2,1)S(1)}, u32[]{:S(2)}, u32[]{:S(2)}) collective-permute-start(bf16[2,8,32,128]{3,2,1,0:T(8,128)(2,1)} %copy-done.77), channel_id=1, source_target_pairs={{0,11},{1,10},{2,9},{3,8},{4,15},{5,14},{6,13},{7,12},{8,3},{9,2},... | collective-permute-start | bytes 393224 | tf_op jit(solution)/shard_map/ppermute | solution.py:357
  276.9 42.9 %collective-permute-start.12 = (bf16[2,8,32,128]{3,2,1,0:T(8,128)(2,1)}, bf16[2,8,32,128]{3,2,1,0:T(8,128)(2,1)S(1)}, u32[]{:S(2)}, u32[]{:S(2)}) collective-permute-start(bf16[2,8,32,128]{3,2,1,0:T(8,128)(2,1)} %copy-done.76), channel_id=1, source_target_pairs={{0,12},{1,13},{2,14},{3,15},{4,8},{5,9},{6,10},{7,11},{8,4},{9,5},... | collective-permute-start | bytes 393224 | tf_op jit(solution)/shard_map/ppermute | solution.py:357
  278.4 41.4 %collective-permute-start.13 = (bf16[2,8,32,128]{3,2,1,0:T(8,128)(2,1)}, bf16[2,8,32,128]{3,2,1,0:T(8,128)(2,1)S(1)}, u32[]{:S(2)}, u32[]{:S(2)}) collective-permute-start(bf16[2,8,32,128]{3,2,1,0:T(8,128)(2,1)} %copy-done.75), channel_id=1, source_target_pairs={{0,13},{1,12},{2,15},{3,14},{4,9},{5,8},{6,11},{7,10},{8,5},{9,4},... | collective-permute-start | bytes 393224 | tf_op jit(solution)/shard_map/ppermute | solution.py:357
  280.3 39.5 %collective-permute-start.14 = (bf16[2,8,32,128]{3,2,1,0:T(8,128)(2,1)}, bf16[2,8,32,128]{3,2,1,0:T(8,128)(2,1)S(1)}, u32[]{:S(2)}, u32[]{:S(2)}) collective-permute-start(bf16[2,8,32,128]{3,2,1,0:T(8,128)(2,1)} %copy-done.74), channel_id=1, source_target_pairs={{0,14},{1,15},{2,12},{3,13},{4,10},{5,11},{6,8},{7,9},{8,6},{9,7},... | collective-permute-start | bytes 393224 | tf_op jit(solution)/shard_map/ppermute | solution.py:357
  282.7 37.1 %collective-permute-start.15 = (bf16[2,8,32,128]{3,2,1,0:T(8,128)(2,1)}, bf16[2,8,32,128]{3,2,1,0:T(8,128)(2,1)S(1)}, u32[]{:S(2)}, u32[]{:S(2)}) collective-permute-start(bf16[2,8,32,128]{3,2,1,0:T(8,128)(2,1)} %copy-done.73), channel_id=1, source_target_pairs={{0,15},{1,14},{2,13},{3,12},{4,11},{5,10},{6,9},{7,8},{8,7},{9,6},... | collective-permute-start | bytes 393224 | tf_op jit(solution)/shard_map/ppermute | solution.py:357
  (120 other events, 2444.0 us)

commit v2 on v0

--- a/solution.py
+++ b/solution.py
@@ -2,7 +2,11 @@
 
 import jax
 import jax.numpy as jnp
+import ml_dtypes
+import numpy as np
 from jax import lax
+from jax.experimental import pallas as pl
+from jax.experimental.pallas import tpu as pltpu
 from jax.sharding import PartitionSpec as P
 
 SPF = 2048
@@ -11,6 +15,10 @@
 CH0 = 256
 INPUTS = 1024
 BLK = 128
+LANES = 128
+UBLK = 16
+TBLK = 16
+PITCH = TBLK + 1
 
 
 def passed_along(x, axis, by):
@@ -27,7 +35,7 @@
     return jnp.concatenate([jnp.cos(angle), -jnp.sin(angle)], axis=1).astype(jnp.bfloat16)
 
 
-def per_device(voltages, coeffs):
+def any_sizes(voltages, coeffs):
     inputs_here = voltages.shape[0]
     frames_here = voltages.shape[1]
     inp_count = lax.axis_size("inp")
@@ -79,6 +87,423 @@
     return jnp.stack(pieces, axis=2).astype(jnp.bfloat16)
 
 
+def turned_over(rows):
+    rows = list(rows)
+    place = lax.broadcasted_iota(jnp.int32, (8, LANES), 0)
+    for shift in (4, 2, 1):
+        low = jnp.bitwise_and(place, shift) == 0
+        for i in range(8):
+            if i & shift == 0:
+                near, far = rows[i], rows[i + shift]
+                rows[i] = jnp.where(low, near, pltpu.roll(far, shift, 0))
+                rows[i + shift] = jnp.where(low, pltpu.roll(near, 8 - shift, 0), far)
+    return rows
+
+
+def frames_of(v_ref, begin):
+    groups = []
+    for group in range(UBLK // 8):
+        groups.append(turned_over([v_ref[begin + group * 8 + i] for i in range(8)]))
+    return [[group[t].astype(jnp.float32) for group in groups] for t in range(8)]
+
+
+def history_kernel(v_ref, out_ref):
+    def some_inputs(step, carry):
+        begin = pl.multiple_of(step * UBLK, UBLK)
+        for t, frame in enumerate(frames_of(v_ref, begin)):
+            out_ref[t, pl.ds(begin, UBLK), :] = jnp.concatenate(frame, axis=0).astype(jnp.bfloat16)
+        return carry
+
+    lax.fori_loop(0, v_ref.shape[0] // UBLK, some_inputs, 0)
+
+
+def last_frames(voltages):
+    inputs, frames, _ = voltages.shape
+    last = frames // TAPS - 1
+    return pl.pallas_call(
+        history_kernel,
+        name="history",
+        grid=(SPF // LANES,),
+        in_specs=[pl.BlockSpec((inputs, TAPS, LANES), lambda i: (0, last, i))],
+        out_specs=pl.BlockSpec((TAPS, inputs, LANES), lambda i: (0, 0, i)),
+        out_shape=jax.ShapeDtypeStruct((TAPS, inputs, SPF), jnp.bfloat16),
+    )(voltages)
+
+
+def filter_kernel(block, *refs):
+    even_ref, odd_ref = refs[-2:]
+    blocks = TBLK // TAPS
+    count = blocks + 1
+    inputs = even_ref.shape[1]
+    groups = UBLK // 8
+
+    def some_inputs(step, carry):
+        begin = pl.multiple_of(step * UBLK, UBLK)
+        here = pl.ds(begin, UBLK)
+        sides = []
+        for side in range(2):
+            sources = refs[side * count : (side + 1) * count]
+            weights = refs[2 * count + side][...].astype(jnp.float32)
+            taps = [jnp.broadcast_to(weights[k : k + 1], (8, LANES)) for k in range(TAPS)]
+            sides.append((sources, taps))
+        before = []
+        for sources, _ in sides:
+            if block == 0:
+                wide = [sources[0][t, here, :].astype(jnp.float32) for t in range(TAPS)]
+                before.append([[w[g * 8 : (g + 1) * 8] for g in range(groups)] for w in wide])
+            else:
+                before.append(frames_of(sources[0], begin))
+        for part in range(blocks):
+            made = []
+            for side, (sources, taps) in enumerate(sides):
+                now = frames_of(sources[1 + part], begin)
+                window = before[side] + now
+                before[side] = now
+                totals = []
+                for t in range(TAPS):
+                    frame = []
+                    for g in range(groups):
+                        total = taps[0] * window[TAPS + t][g]
+                        for k in range(1, TAPS):
+                            total = total + taps[k] * window[TAPS + t - k][g]
+                        frame.append(total)
+                    totals.append(jnp.concatenate(frame, axis=0))
+                made.append(totals)
+            for t in range(TAPS):
+                at = part * TAPS + t
+                even_ref[at, here, :] = (made[0][t] + made[1][t]).astype(jnp.bfloat16)
+                odd_ref[at, here, :] = (made[0][t] - made[1][t]).astype(jnp.bfloat16)
+        return carry
+
+    lax.fori_loop(0, inputs // UBLK, some_inputs, 0)
+
+
+def filtered_frames(block, voltages, coeffs, history=None):
+    inputs, frames, _ = voltages.shape
+    half = SPF // 2
+    steps = half // LANES
+    first = block * (TBLK // TAPS)
+    in_specs, operands = [], []
+    for side in range(2):
+        for place in range(first - 1, first + TBLK // TAPS):
+            if place < 0:
+                in_specs.append(
+                    pl.BlockSpec((TAPS, inputs, LANES), lambda i, side=side: (0, 0, i + side * steps))
+                )
+                operands.append(history)
+            else:
+                in_specs.append(
+                    pl.BlockSpec(
+                        (inputs, TAPS, LANES),
+                        lambda i, side=side, place=place: (0, place, i + side * steps),
+                    )
+                )
+                operands.append(voltages)
+    for side in range(2):
+        in_specs.append(pl.BlockSpec((TAPS, LANES), lambda i, side=side: (0, i + side * steps)))
+        operands.append(coeffs)
+    shape = jax.ShapeDtypeStruct((TBLK, inputs, half), jnp.bfloat16)
+    out_spec = pl.BlockSpec((TBLK, inputs, LANES), lambda i: (0, 0, i))
+
+    def kernel(*refs):
+        filter_kernel(block, *refs)
+
+    return pl.pallas_call(
+        kernel,
+        name=f"filter_{block}",
+        grid=(steps,),
+        in_specs=in_specs,
+        out_specs=[out_spec, out_spec],
+        out_shape=[shape, shape],
+        compiler_params=pltpu.CompilerParams(vmem_limit_bytes=24 * 2**20),
+    )(*operands)
+
+
+def parity_tables(parts, width):
+    tables = []
+    for parity in range(2):
+        within = np.arange(parity, width, 2)
+        channel = (np.arange(parts)[:, None] * width + within[None, :]).reshape(-1) + CH0
+        phase = channel[:, None].astype(np.int64) * np.arange(SPF // 2)[None, :] % SPF
+        angle = phase.astype(np.float32) * np.float32(2.0 * math.pi / SPF)
+        wide = angle.astype(np.float64)
+        both = np.stack([np.cos(wide), -np.sin(wide)], axis=1)
+        both = both.reshape(-1, SPF // 2).astype(np.float32)
+        tables.append(jnp.asarray(both.astype(ml_dtypes.bfloat16)))
+    return tables
+
+
+def transform_kernel(parts, splits, me_ref, late_ref, early_ref, table_ref, *refs):
+    outs, power_ref, turned = refs[:-2], refs[-2], refs[-1]
+    rows = table_ref.shape[0]
+    own = rows // parts
+    step = pl.program_id(0)
+    me = me_ref[0]
+
+    def work(x_ref):
+        spectrum = lax.dot_general(
+            table_ref[...],
+            x_ref[...].reshape(-1, SPF // 2),
+            (((1,), (1,)), ((), ())),
+            preferred_element_type=jnp.float32,
+        )
+        square = jnp.zeros((8, BLK), jnp.float32)
+        for t in range(TBLK):
+            frame = spectrum[:, t * BLK : (t + 1) * BLK]
+            turned[pl.ds(t, rows, stride=PITCH), :] = frame
+            square = square + jnp.sum((frame * frame).reshape(rows // 8, 8, BLK), axis=0)
+        for s in range(parts):
+            there = jnp.bitwise_xor(me, s)
+            begin = there * (own * PITCH)
+            for split, (first, depth) in enumerate(splits):
+                out = outs[split * parts + s]
+                for channel in range(depth):
+                    for half in range(2):
+                        row = (first + channel) * 2 + half
+                        value = turned[pl.ds(begin + row * PITCH, TBLK), :]
+                        out[0, channel, half * TBLK : (half + 1) * TBLK, :] = value.astype(
+                            jnp.bfloat16
+                        )
+        return square
+
+    @pl.when(step == 0)
+    def _():
+        power_ref[...] = work(late_ref)
+
+    @pl.when(step == 1)
+    def _():
+        power_ref[...] += work(early_ref)
+
+
+def transformed(name, parts, me, late, early, table, splits):
+    frames, inputs, _ = late.shape
+    rows = table.shape[0]
+    shapes, specs = [], []
+    for _, depth in splits:
+        shapes += [jax.ShapeDtypeStruct((2, depth, 2 * TBLK, BLK), jnp.bfloat16)] * parts
+        specs += [
+            pl.BlockSpec((1, depth, 2 * TBLK, BLK), lambda i, me: (i, 0, 0, 0))
+            for _ in range(parts)
+        ]
+
+    def kernel(me_ref, *refs):
+        transform_kernel(parts, splits, me_ref, *refs)
+
+    out = pl.pallas_call(
+        kernel,
+        name=name,
+        grid_spec=pltpu.PrefetchScalarGridSpec(
+            num_scalar_prefetch=1,
+            grid=(2,),
+            in_specs=[
+                pl.BlockSpec((TBLK, inputs, SPF // 2), lambda i, me: (0, 0, 0)),
+                pl.BlockSpec((TBLK, inputs, SPF // 2), lambda i, me: (0, 0, 0)),
+                pl.BlockSpec((rows, SPF // 2), lambda i, me: (0, 0)),
+            ],
+            out_specs=specs + [pl.BlockSpec((8, BLK), lambda i, me: (0, 0))],
+            scratch_shapes=[pltpu.VMEM((rows * PITCH + 8, BLK), jnp.float32)],
+        ),
+        out_shape=shapes + [jax.ShapeDtypeStruct((8, BLK), jnp.float32)],
+        compiler_params=pltpu.CompilerParams(vmem_limit_bytes=44 * 2**20),
+    )(me, late, early, table)
+    messages = [out[split * parts : (split + 1) * parts] for split in range(len(splits))]
+    return messages, out[-1]
+
+
+def correlate_kernel(parts, steps, me_ref, *refs):
+    messages = refs[:parts]
+    row_ref = refs[parts]
+    out_ref, token_ref, plain, other, columns = refs[-5:]
+    blocks = INPUTS // BLK
+    freq = parts // blocks
+    span = steps * 2 * TBLK
+    me = me_ref[0]
+
+    @pl.when(pl.program_id(0) == 0)
+    def _():
+        token_ref[...] = jnp.zeros_like(token_ref)
+        for r in range(blocks):
+            wide = jnp.broadcast_to(row_ref[r : r + 1, :], (BLK, BLK))
+            columns[r * BLK : (r + 1) * BLK, :] = wide.T
+
+    for s in range(parts):
+        source = jnp.bitwise_xor(me, s)
+        block, place = source // freq, source % freq
+        for step in range(steps):
+            begin = pl.multiple_of(place * span + step * 2 * TBLK, 2 * TBLK)
+            real = messages[s][step, 0, :TBLK, :]
+            imag = messages[s][step, 0, TBLK:, :]
+            plain[block, pl.ds(begin, TBLK), :] = real
+            plain[block, pl.ds(begin + TBLK, TBLK), :] = imag
+            other[block, pl.ds(begin, TBLK), :] = -imag
+            other[block, pl.ds(begin + TBLK, TBLK), :] = real
+
+    sides = [plain[r].T for r in range(blocks)]
+    for c in range(blocks):
+        weights = jnp.concatenate([plain[c], other[c]], axis=1)
+        lhs = sides[0] if c == 0 else jnp.concatenate(sides[: c + 1], axis=0)
+        both = jnp.dot(lhs, weights, preferred_element_type=jnp.float32)
+        row_gain = row_ref[c : c + 1, :]
+        for r in range(c + 1):
+            pair = r * blocks - r * (r - 1) // 2 + (c - r)
+            gain = columns[r * BLK : (r + 1) * BLK, :] * (row_gain * (1.0 / (freq * steps * TBLK)))
+            for part in range(2):
+                piece = both[r * BLK : (r + 1) * BLK, part * BLK : (part + 1) * BLK]
+                out_ref[0, part, pair] = (piece * gain).astype(jnp.bfloat16)
+
+
+def correlated(name, me, messages, gains, first, count, place, width, before=None):
+    parts = len(messages)
+    steps = messages[0].shape[0]
+    blocks = INPUTS // BLK
+    pairs = blocks * (blocks + 1) // 2
+    span = parts // blocks * steps * 2 * TBLK
+    in_specs = [
+        pl.BlockSpec((steps, 1, 2 * TBLK, BLK), lambda i, me: (0, first + i, 0, 0))
+        for _ in range(parts)
+    ] + [pl.BlockSpec((blocks, BLK), lambda i, me: (0, 0))]
+    operands = [me, *messages, gains]
+    aliases = {}
+    if before is not None:
+        aliases[len(operands)] = 0
+        in_specs.append(pl.BlockSpec(memory_space=pl.ANY))
+        operands.append(before)
+
+    def kernel(me_ref, *refs):
+        correlate_kernel(parts, steps, me_ref, *refs)
+
+    return pl.pallas_call(
+        kernel,
+        name=name,
+        grid_spec=pltpu.PrefetchScalarGridSpec(
+            num_scalar_prefetch=1,
+            grid=(count,),
+            in_specs=in_specs,
+            out_specs=[
+                pl.BlockSpec(
+                    (1, 2, pairs, BLK, BLK), lambda i, me: (place + 2 * i, 0, 0, 0, 0)
+                ),
+                pl.BlockSpec((8, BLK), lambda i, me: (0, 0)),
+            ],
+            scratch_shapes=[
+                pltpu.VMEM((blocks, span, BLK), jnp.bfloat16),
+                pltpu.VMEM((blocks, span, BLK), jnp.bfloat16),
+                pltpu.VMEM((INPUTS, BLK), jnp.float32),
+            ],
+        ),
+        out_shape=[
+            jax.ShapeDtypeStruct((width, 2, pairs, BLK, BLK), jnp.bfloat16),
+            jax.ShapeDtypeStruct((8, BLK), jnp.float32),
+        ],
+        input_output_aliases=aliases,
+        compiler_params=pltpu.CompilerParams(vmem_limit_bytes=24 * 2**20),
+    )(*operands)
+
+
+def nothing_kernel(*refs):
+    del refs
+
+
+def gated(name, messages, after):
+    spec = pl.BlockSpec(memory_space=pl.ANY)
+    return pl.pallas_call(
+        nothing_kernel,
+        name=name,
+        in_specs=[spec] * (len(messages) + len(after)),
+        out_specs=[spec] * len(messages),
+        out_shape=[jax.ShapeDtypeStruct(m.shape, m.dtype) for m in messages],
+        input_output_aliases={i: i for i in range(len(messages))},
+    )(*messages, *after)
+
+
+def per_device(voltages, coeffs):
+    freq_count = lax.axis_size("freq")
+    parts = lax.axis_size("inp") * freq_count
+    inputs, frames, _ = voltages.shape
+    width = CH // parts
+    fits = (
+        inputs == BLK
+        and frames == 2 * TBLK
+        and TBLK % TAPS == 0
+        and parts & (parts - 1) == 0
+        and parts >= 16
+        and width % 16 == 0
+        and parts * BLK == INPUTS * freq_count
+        and freq_count * frames * 2 == LANES
+    )
+    if not fits:
+        return any_sizes(voltages, coeffs)
+    axes = ("inp", "freq")
+    me = lax.axis_index("inp") * freq_count + lax.axis_index("freq")
+    me = me.astype(jnp.int32).reshape(1)
+    history = passed_along(last_frames(voltages), "freq", 1)
+    late = filtered_frames(1, voltages, coeffs)
+    early = filtered_frames(0, voltages, coeffs, history)
+    tables = parity_tables(parts, width)
+
+    far, near = list(range(parts // 2, parts)), list(range(1, parts // 2))
+    order = [s for pair in zip(far, near + [0]) for s in pair if s > 0]
+
+    def send(message, s):
+        return lax.ppermute(message, axes, [(i, i ^ s) for i in range(parts)])
+
+    class Chunk:
+        def __init__(self, name, messages):
+            self.name = name
+            self.messages = messages
+            self.arrived = {0: messages[0]}
+            self.sent = 0
+
+        def go(self, count, after=()):
+            which = order[self.sent : self.sent + count]
+            chosen = [self.messages[s] for s in which]
+            if after:
+                chosen = gated(f"gate_{self.name}_{self.sent}", chosen, list(after))
+            for s, message in zip(which, chosen):
+                self.arrived[s] = send(message, s)
+            self.sent += len(which)
+
+        def all(self):
+            return [self.arrived[s] for s in range(parts)]
+
+    half = width // 2
+    quarter = half // 2
+    piece = half // 4
+    sets, squares = transformed("spectra_even", parts, me, late[0], early[0], tables[0], [(0, half)])
+    first = Chunk("a", sets[0])
+    first.go(5)
+    sets, more = transformed(
+        "spectra_odd",
+        parts,
+        me,
+        late[1],
+        early[1],
+        tables[1],
+        [(0, quarter), (quarter, quarter)],
+    )
+    second, third = Chunk("b", sets[0]), Chunk("c", sets[1])
+    shared = lax.all_gather(jnp.sum(squares + more, axis=0), axes)
+    shared = jnp.sum(shared.reshape(parts // freq_count, freq_count, BLK), axis=1)
+    gains = 1.0 / jnp.sqrt(shared / (frames * freq_count * CH) + 1e-06)
+    first.go(len(order) - 5, [gains])
+    second.go(5, [first.arrived[order[9]]])
+    out = None
+    for step, count in enumerate((3, 3, 4, 0)):
+        out, token = correlated(
+            f"correlate_a{step}", me, first.all(), gains, step * piece, piece, 2 * step * piece, width, out
+        )
+        second.go(count, [token]) if count else third.go(4, [token])
+    for step, count in enumerate((4, len(order) - 8)):
+        out, token = correlated(
+            f"correlate_b{step}", me, second.all(), gains, step * piece, piece, 2 * step * piece + 1, width, out
+        )
+        third.go(count, [token])
+    out, _ = correlated(
+        "correlate_c", me, third.all(), gains, 0, quarter, 2 * quarter + 1, width, out
+    )
+    return out
+
+
 def solution(mesh):
     in_specs = (P(("grp", "inp"), "freq", None), P())
     out_specs = P(("grp", "inp", "freq"), None, None, None, None)

time: 869 us -> 364 us (0.42)
  local copies, waits for them, and re-layouts: 299 us -> 30.7 us
  other arithmetic: 214 us -> 0.64 us
  blocking collectives: 192 us -> 22.4 us
  matrix products: 152 us -> 0 us
  Pallas kernels: 0 us -> 122 us
  starting transfers between devices: 2.9 us -> 99.5 us
  waiting for transfers between devices: 0.01 us -> 87 us
    all_to_all x1 -> x0, blocking collectives: 189 us -> none  [per_device(): lax.all_to_all(scaled[None], ('inp', 'freq'), split_axis=2, concat_axis=0...]
    dot_general x17 -> x0, matrix products: 152 us -> none  [the longest x8 75.3 us: per_device(): jnp.einsum('cut,cmt->cum', row_panel, other[:, row_index * BLK:], preferr...]
    convert_element_type x4 -> x0, other arithmetic: 141 us -> none  [the longest x1 109 us: per_device(): summed.astype(jnp.bfloat16).reshape(inputs_here * frames_here, SPF)]
    pallas_call x0 -> x20, Pallas kernels: none -> 122 us  [the longest x7 53.8 us: correlated(): pl.pallas_call(kernel, name=name, grid_spec=pltpu.PrefetchScalarGridSpec(...]
    ppermute x0 -> x45, starting transfers between devices: none -> 95.1 us  [send(): return lax.ppermute(message, axes, [(i, i ^ s) for i in range(parts)])]
    another operation x3 -> x0, local copies, waits for them, and re-layouts: 92.4 us -> none  [the longest x1 49.6 us: per_device(): return jnp.stack(pieces, axis=2).astype(jnp.bfloat16)]
    ppermute x0 -> x45, waiting for transfers between devices: none -> 87 us  [send(): return lax.ppermute(message, axes, [(i, i ^ s) for i in range(parts)])]
    another operation x10 -> x0, other arithmetic: 64.1 us -> none
  transfers between devices with their start and end apart: 1 -> 46, of which waited for: 0 -> 13; matrix products, arithmetic and copies ran while one was open for 5% -> 0% of each run, Pallas kernels for 0% -> 17%
where the time goes in v2:
time: 364 us; the launch traced here: 363 us
  Pallas kernels  122 us (34%)
  starting transfers between devices  99.5 us (27%)
  waiting for transfers between devices  87 us (24%)
  local copies, waits for them, and re-layouts  30.7 us (8%)
  blocking collectives  22.4 us (6%)
    ppermute x45, starting transfers between devices, send(): return lax.ppermute(message, axes, [(i, i ^ s) for i in range(parts)])  95.1 us
    ppermute x45, waiting for transfers between devices, send(): return lax.ppermute(message, axes, [(i, i ^ s) for i in range(parts)])  87 us
    pallas_call x7, Pallas kernels, correlated(): pl.pallas_call(kernel, name=name, grid_spec=pltpu.PrefetchScalarGridSpec(...  53.8 us
    pallas_call x2, Pallas kernels, filtered_frames(): pl.pallas_call(kernel, name=f'filter_{block}', grid=(steps,), in_specs=in...  40.1 us
    unnamed x140, local copies, waits for them, and re-layouts  30.7 us
    all_gather x1, blocking collectives, per_device(): shared = lax.all_gather(jnp.sum(squares + more, axis=0), axes)  22.4 us
    pallas_call x2, Pallas kernels, transformed(): pl.pallas_call(kernel, name=name, grid_spec=pltpu.PrefetchScalarGridSpec(...  16.2 us
    pallas_call x1, Pallas kernels, last_frames(): pl.pallas_call(history_kernel, name='history', grid=(SPF // LANES,), in_s...  12.1 us
  transfers between devices with their start and end apart: 46, of which 13 were waited for; matrix products, arithmetic and copies ran while one was open for 0% of the time, Pallas kernels for 17%

profile of v2, /device:TPU:0, one launch (start us, length us, event | category | flops | bytes accessed | tf_op | source)
XLA Modules:
  0.0 363.0 jit_solution(1021498450220383532)
XLA Ops:
  0.0 12.1 %history.1 = bf16[8,128,2048]{2,1,0:T(8,128)(2,1)} custom-call(s32[128,32,2048]{2,1,0:T(8,128)} %refs_5_.3), custom_call_target="tpu_custom_call" | custom-call | tf_op jit(solution)/shard_map/history/pallas_call | solution.py:123
  17.4 20.5 %filter_1.1 = (bf16[16,128,1024]{2,1,0:T(8,128)(2,1)S(1)}, bf16[16,128,1024]{2,1,0:T(8,128)(2,1)S(1)}) custom-call(s32[128,32,2048]{2,1,0:T(8,128)} %refs_5_.3, s32[128,32,2048]{2,1,0:T(8,128)} %refs_5_.3, s32[128,32,2048]{2,1,0:T(8,128)} %refs_5_.3, s32[128,32,2048]{2,1,0:T(8,128)} %refs_5_.3, s32[128,32,2048]{2,1,0:T(8,128)} %refs_5_.3, ...), custom_call_target="tpu_custom_call" | custom-call | tf_op jit(solution)/shard_map/filter_1/pallas_call | solution.py:211
  42.0 19.6 %filter_0.1 = (bf16[16,128,1024]{2,1,0:T(8,128)(2,1)S(1)}, bf16[16,128,1024]{2,1,0:T(8,128)(2,1)S(1)}) custom-call(bf16[8,128,2048]{2,1,0:T(8,128)(2,1)} %collective-permute-done.refs_0_.refs_3_, s32[128,32,2048]{2,1,0:T(8,128)} %refs_5_.3, s32[128,32,2048]{2,1,0:T(8,128)} %refs_5_.3, bf16[8,128,2048]{2,1,0:T(8,128)(2,1)} %collective-permute-done.refs_0_.refs_3_, ...), custom_call_target="tpu_custom_call" | custom-call | tf_op jit(solution)/shard_map/filter_0/pallas_call | solution.py:211
  65.7 7.4 %spectra_odd.1 = (bf16[2,8,32,128]{3,2,1,0:T(8,128)(2,1)S(1)}, bf16[2,8,32,128]{3,2,1,0:T(8,128)(2,1)S(1)}, bf16[2,8,32,128]{3,2,1,0:T(8,128)(2,1)S(1)}, bf16[2,...) custom-call(s32[1]{0:T(128)} %bitcast.me_ref, ...), custom_call_target="tpu_custom_call" | custom-call | tf_op jit(solution)/shard_map/spectra_odd/pallas_call | solution.py:292
  79.8 8.8 %spectra_even.1 = (bf16[2,16,32,128]{3,2,1,0:T(8,128)(2,1)S(1)}, bf16[2,16,32,128]{3,2,1,0:T(8,128)(2,1)}, bf16[2,16,32,128]{3,2,1,0:T(8,128)(2,1)S(1)}, bf16[2,...) custom-call(s32[1]{0:T(128)} %bitcast.me_ref, ...), custom_call_target="tpu_custom_call" | custom-call | tf_op jit(solution)/shard_map/spectra_even/pallas_call | solution.py:292
  98.6 22.4 %all-gather.1 = f32[16,1,128]{2,1,0:T(1,128)S(1)} all-gather(f32[1,1,128]{2,1,0:T(1,128)S(1)} %bitcast.4), channel_id=2, replica_groups=mesh['grp'=2,'inp'=8,'freq'=2] {'inp','freq'}, dimensions={0}, use_global_device_ids=true | all-gather | bytes 8704 | tf_op jit(solution)/shard_map/all_gather | solution.py:485
  131.1 10.0 %collective-permute-done.5.refs_5_ = bf16[2,16,32,128]{3,2,1,0:T(8,128)(2,1)S(1)} collective-permute-done((bf16[2,16,32,128]{3,2,1,0:T(8,128)(2,1)}, bf16[2,16,32,128]{3,2,1,0:T(8,128)(2,1)S(1)}, u32[]{:S(2)}, u32[]{:S(2)}) %collective-permute-start.5) | collective-permute-done | bytes 262176 | tf_op jit(solution)/shard_map/ppermute | solution.py:448
  141.5 7.8 %collective-permute-done.6.refs_6_ = bf16[2,16,32,128]{3,2,1,0:T(8,128)(2,1)S(1)} collective-permute-done((bf16[2,16,32,128]{3,2,1,0:T(8,128)(2,1)}, bf16[2,16,32,128]{3,2,1,0:T(8,128)(2,1)S(1)}, u32[]{:S(2)}, u32[]{:S(2)}) %collective-permute-start.6) | collective-permute-done | bytes 262176 | tf_op jit(solution)/shard_map/ppermute | solution.py:448
  153.5 20.2 %collective-permute-start.1 = (bf16[2,16,32,128]{3,2,1,0:T(8,128)(2,1)}, bf16[2,16,32,128]{3,2,1,0:T(8,128)(2,1)S(1)}, u32[]{:S(2)}, u32[]{:S(2)}) collective-permute-start(bf16[2,16,32,128]{3,2,1,0:T(8,128)(2,1)} %get-tuple-element.122), channel_id=1, source_target_pairs={{0,1},{1,0},{2,3},{3,2},{4,5},{5,4},{6,7},{7,6},{8,9},{9,8},{10,11... | collective-permute-start | bytes 786440 | tf_op jit(solution)/shard_map/ppermute | solution.py:448
  176.4 12.7 %collective-permute-start.9 = (bf16[2,16,32,128]{3,2,1,0:T(8,128)(2,1)}, bf16[2,16,32,128]{3,2,1,0:T(8,128)(2,1)}, u32[]{:S(2)}, u32[]{:S(2)}) collective-permute-start(bf16[2,16,32,128]{3,2,1,0:T(8,128)(2,1)} %copy-done.67), channel_id=1, source_target_pairs={{0,9},{1,8},{2,11},{3,10},{4,13},{5,12},{6,15},{7,14},{8,1},{9,0},... | collective-permute-start | bytes 786440 | tf_op jit(solution)/shard_map/ppermute | solution.py:448
  189.1 13.9 %collective-permute-start.10 = (bf16[2,16,32,128]{3,2,1,0:T(8,128)(2,1)}, bf16[2,16,32,128]{3,2,1,0:T(8,128)(2,1)}, u32[]{:S(2)}, u32[]{:S(2)}) collective-permute-start(bf16[2,16,32,128]{3,2,1,0:T(8,128)(2,1)} %copy-done.66), channel_id=1, source_target_pairs={{0,10},{1,11},{2,8},{3,9},{4,14},{5,15},{6,12},{7,13},{8,2},{9,3},... | collective-permute-start | bytes 786440 | tf_op jit(solution)/shard_map/ppermute | solution.py:448
  203.2 11.5 %collective-permute-done.8.refs_8_ = bf16[2,16,32,128]{3,2,1,0:T(8,128)(2,1)} collective-permute-done((bf16[2,16,32,128]{3,2,1,0:T(8,128)(2,1)}, bf16[2,16,32,128]{3,2,1,0:T(8,128)(2,1)}, u32[]{:S(2)}, u32[]{:S(2)}) %collective-permute-start.8) | collective-permute-done | bytes 262176 | tf_op jit(solution)/shard_map/ppermute | solution.py:448
  214.8 8.7 %collective-permute-done.9.refs_9_ = bf16[2,16,32,128]{3,2,1,0:T(8,128)(2,1)} collective-permute-done((bf16[2,16,32,128]{3,2,1,0:T(8,128)(2,1)}, bf16[2,16,32,128]{3,2,1,0:T(8,128)(2,1)}, u32[]{:S(2)}, u32[]{:S(2)}) %collective-permute-start.9) | collective-permute-done | bytes 262176 | tf_op jit(solution)/shard_map/ppermute | solution.py:448
  223.5 10.8 %collective-permute-done.10.refs_10_ = bf16[2,16,32,128]{3,2,1,0:T(8,128)(2,1)} collective-permute-done((bf16[2,16,32,128]{3,2,1,0:T(8,128)(2,1)}, bf16[2,16,32,128]{3,2,1,0:T(8,128)(2,1)}, u32[]{:S(2)}, u32[]{:S(2)}) %collective-permute-start.10) | collective-permute-done | bytes 262176 | tf_op jit(solution)/shard_map/ppermute | solution.py:448
  235.9 7.0 %correlate_a0.1 = (bf16[32,2,36,128,128]{4,3,2,1,0:T(8,128)(2,1)}, f32[8,128]{1,0:T(8,128)S(1)}) custom-call(s32[1]{0:T(128)} %bitcast.me_ref, bf16[2,16,32,128]{3,2,1,0:T(8,128)(2,1)S(1)} %get-tuple-element.121.refs_0_, bf16[2,16,32,128]{3,2,1,0:T(8,128)(2,1)S(1)} %collective-permute-done.1.refs_1_, ...), custom_call_target="tpu_custom_call" | custom-call | tf_op jit(solution)/shard_map/correlate_a0/pallas_call | solution.py:375
  243.5 6.9 %correlate_a1.1 = (bf16[32,2,36,128,128]{4,3,2,1,0:T(8,128)(2,1)}, f32[8,128]{1,0:T(8,128)S(1)}) custom-call(s32[1]{0:T(128)} %bitcast.me_ref, bf16[2,16,32,128]{3,2,1,0:T(8,128)(2,1)S(1)} %get-tuple-element.121.refs_0_, bf16[2,16,32,128]{3,2,1,0:T(8,128)(2,1)S(1)} %collective-permute-done.1.refs_1_, ...), custom_call_target="tpu_custom_call", output_to_operand_aliasing={{0}: (18, {})} | custom-call | tf_op jit(solution)/shard_map/correlate_a1/pallas_call | solution.py:375
  251.0 7.0 %correlate_a2.1 = (bf16[32,2,36,128,128]{4,3,2,1,0:T(8,128)(2,1)}, f32[8,128]{1,0:T(8,128)S(1)}) custom-call(s32[1]{0:T(128)} %bitcast.me_ref, bf16[2,16,32,128]{3,2,1,0:T(8,128)(2,1)S(1)} %get-tuple-element.121.refs_0_, bf16[2,16,32,128]{3,2,1,0:T(8,128)(2,1)S(1)} %collective-permute-done.1.refs_1_, ...), custom_call_target="tpu_custom_call", output_to_operand_aliasing={{0}: (18, {})} | custom-call | tf_op jit(solution)/shard_map/correlate_a2/pallas_call | solution.py:375
  273.7 7.4 %collective-permute-start.21 = (bf16[2,8,32,128]{3,2,1,0:T(8,128)(2,1)}, bf16[2,8,32,128]{3,2,1,0:T(8,128)(2,1)}, u32[]{:S(2)}, u32[]{:S(2)}) collective-permute-start(bf16[2,8,32,128]{3,2,1,0:T(8,128)(2,1)} %get-tuple-element.172), channel_id=1, source_target_pairs={{0,4},{1,5},{2,6},{3,7},{4,0},{5,1},{6,2},{7,3},{8,12},{9,13},{10,... | collective-permute-start | bytes 393224 | tf_op jit(solution)/shard_map/ppermute | solution.py:448
  283.6 6.9 %correlate_a3.1 = (bf16[32,2,36,128,128]{4,3,2,1,0:T(8,128)(2,1)}, f32[8,128]{1,0:T(8,128)S(1)}) custom-call(s32[1]{0:T(128)} %bitcast.me_ref, bf16[2,16,32,128]{3,2,1,0:T(8,128)(2,1)S(1)} %get-tuple-element.121.refs_0_, bf16[2,16,32,128]{3,2,1,0:T(8,128)(2,1)S(1)} %collective-permute-done.1.refs_1_, ...), custom_call_target="tpu_custom_call", output_to_operand_aliasing={{0}: (18, {})} | custom-call | tf_op jit(solution)/shard_map/correlate_a3/pallas_call | solution.py:375
  296.4 7.3 %correlate_b0.1 = (bf16[32,2,36,128,128]{4,3,2,1,0:T(8,128)(2,1)}, f32[8,128]{1,0:T(8,128)S(1)}) custom-call(s32[1]{0:T(128)} %bitcast.me_ref, bf16[2,8,32,128]{3,2,1,0:T(8,128)(2,1)S(1)} %get-tuple-element.159.refs_0_, bf16[2,8,32,128]{3,2,1,0:T(8,128)(2,1)} %collective-permute-done.18.refs_1_, ...), custom_call_target="tpu_custom_call", output_to_operand_aliasing={{0}: (18, {})} | custom-call | tf_op jit(solution)/shard_map/correlate_b0/pallas_call | solution.py:375
  305.9 7.3 %correlate_b1.1 = (bf16[32,2,36,128,128]{4,3,2,1,0:T(8,128)(2,1)}, f32[8,128]{1,0:T(8,128)S(1)}) custom-call(s32[1]{0:T(128)} %bitcast.me_ref, bf16[2,8,32,128]{3,2,1,0:T(8,128)(2,1)S(1)} %get-tuple-element.159.refs_0_, bf16[2,8,32,128]{3,2,1,0:T(8,128)(2,1)} %collective-permute-done.18.refs_1_, ...), custom_call_target="tpu_custom_call", output_to_operand_aliasing={{0}: (18, {})} | custom-call | tf_op jit(solution)/shard_map/correlate_b1/pallas_call | solution.py:375
  335.0 9.2 %collective-permute-done.36.refs_6_ = bf16[2,8,32,128]{3,2,1,0:T(8,128)(2,1)S(1)} collective-permute-done((bf16[2,8,32,128]{3,2,1,0:T(8,128)(2,1)}, bf16[2,8,32,128]{3,2,1,0:T(8,128)(2,1)S(1)}, u32[]{:S(2)}, u32[]{:S(2)}) %collective-permute-start.36) | collective-permute-done | bytes 131104 | tf_op jit(solution)/shard_map/ppermute | solution.py:448
  344.2 7.4 %collective-permute-done.45.refs_15_ = bf16[2,8,32,128]{3,2,1,0:T(8,128)(2,1)S(1)} collective-permute-done((bf16[2,8,32,128]{3,2,1,0:T(8,128)(2,1)}, bf16[2,8,32,128]{3,2,1,0:T(8,128)(2,1)S(1)}, u32[]{:S(2)}, u32[]{:S(2)}) %collective-permute-start.45) | collective-permute-done | bytes 131104 | tf_op jit(solution)/shard_map/ppermute | solution.py:448
  351.6 11.4 %correlate_c.1 = (bf16[32,2,36,128,128]{4,3,2,1,0:T(8,128)(2,1)}, f32[8,128]{1,0:T(8,128)}) custom-call(s32[1]{0:T(128)} %bitcast.me_ref, bf16[2,8,32,128]{3,2,1,0:T(8,128)(2,1)S(1)} %copy-done.26, bf16[2,8,32,128]{3,2,1,0:T(8,128)(2,1)S(1)} %collective-permute-done.16.refs_1_, ...), custom_call_target="tpu_custom_call", output_to_operand_aliasing={{0}: (18, {})} | custom-call | tf_op jit(solution)/shard_map/correlate_c/pallas_call | solution.py:375
  (232 shorter events, 98.3 us)
Async XLA Ops:
  12.1 29.8 %collective-permute-start = (bf16[8,128,2048]{2,1,0:T(8,128)(2,1)}, bf16[8,128,2048]{2,1,0:T(8,128)(2,1)}, u32[]{:S(2)}, u32[]{:S(2)}) collective-permute-start(bf16[8,128,2048]{2,1,0:T(8,128)(2,1)} %history.1), channel_id=1, source_target_pairs={{0,1},{2,3},{4,5},{6,7},{8,9},{10,11},{12,13},{14,15},{16,17},{18,... | collective-permute-start | bytes 12582920 | tf_op jit(solution)/shard_map/ppermute | solution.py:27
  123.4 25.9 %collective-permute-start.6 = (bf16[2,16,32,128]{3,2,1,0:T(8,128)(2,1)}, bf16[2,16,32,128]{3,2,1,0:T(8,128)(2,1)S(1)}, u32[]{:S(2)}, u32[]{:S(2)}) collective-permute-start(bf16[2,16,32,128]{3,2,1,0:T(8,128)(2,1)} %get-tuple-element.139), channel_id=1, source_target_pairs={{0,6},{1,7},{2,4},{3,5},{4,2},{5,3},{6,0},{7,1},{8,14},{9,15},{10,... | collective-permute-start | bytes 786440 | tf_op jit(solution)/shard_map/ppermute | solution.py:448
  125.1 28.3 %collective-permute-start.7 = (bf16[2,16,32,128]{3,2,1,0:T(8,128)(2,1)}, bf16[2,16,32,128]{3,2,1,0:T(8,128)(2,1)S(1)}, u32[]{:S(2)}, u32[]{:S(2)}) collective-permute-start(bf16[2,16,32,128]{3,2,1,0:T(8,128)(2,1)} %get-tuple-element.140), channel_id=1, source_target_pairs={{0,7},{1,6},{2,5},{3,4},{4,3},{5,2},{6,1},{7,0},{8,15},{9,14},{10,... | collective-permute-start | bytes 786440 | tf_op jit(solution)/shard_map/ppermute | solution.py:448
  130.1 23.4 %collective-permute-start.11 = (bf16[2,16,32,128]{3,2,1,0:T(8,128)(2,1)}, bf16[2,16,32,128]{3,2,1,0:T(8,128)(2,1)S(1)}, u32[]{:S(2)}, u32[]{:S(2)}) collective-permute-start(bf16[2,16,32,128]{3,2,1,0:T(8,128)(2,1)} %get-tuple-element.144), channel_id=1, source_target_pairs={{0,11},{1,10},{2,9},{3,8},{4,15},{5,14},{6,13},{7,12},{8,3},{9,2},... | collective-permute-start | bytes 786440 | tf_op jit(solution)/shard_map/ppermute | solution.py:448
  131.1 42.6 %collective-permute-start.12 = (bf16[2,16,32,128]{3,2,1,0:T(8,128)(2,1)}, bf16[2,16,32,128]{3,2,1,0:T(8,128)(2,1)S(1)}, u32[]{:S(2)}, u32[]{:S(2)}) collective-permute-start(bf16[2,16,32,128]{3,2,1,0:T(8,128)(2,1)} %get-tuple-element.145), channel_id=1, source_target_pairs={{0,12},{1,13},{2,14},{3,15},{4,8},{5,9},{6,10},{7,11},{8,4},{9,5},... | collective-permute-start | bytes 786440 | tf_op jit(solution)/shard_map/ppermute | solution.py:448
  141.1 32.8 %collective-permute-start.13 = (bf16[2,16,32,128]{3,2,1,0:T(8,128)(2,1)}, bf16[2,16,32,128]{3,2,1,0:T(8,128)(2,1)S(1)}, u32[]{:S(2)}, u32[]{:S(2)}) collective-permute-start(bf16[2,16,32,128]{3,2,1,0:T(8,128)(2,1)} %get-tuple-element.146), channel_id=1, source_target_pairs={{0,13},{1,12},{2,15},{3,14},{4,9},{5,8},{6,11},{7,10},{8,5},{9,4},... | collective-permute-start | bytes 786440 | tf_op jit(solution)/shard_map/ppermute | solution.py:448
  149.3 27.0 %collective-permute-start.14 = (bf16[2,16,32,128]{3,2,1,0:T(8,128)(2,1)}, bf16[2,16,32,128]{3,2,1,0:T(8,128)(2,1)S(1)}, u32[]{:S(2)}, u32[]{:S(2)}) collective-permute-start(bf16[2,16,32,128]{3,2,1,0:T(8,128)(2,1)} %get-tuple-element.147), channel_id=1, source_target_pairs={{0,14},{1,15},{2,12},{3,13},{4,10},{5,11},{6,8},{7,9},{8,6},{9,7},... | collective-permute-start | bytes 786440 | tf_op jit(solution)/shard_map/ppermute | solution.py:448
  153.5 35.6 %collective-permute-start.15 = (bf16[2,16,32,128]{3,2,1,0:T(8,128)(2,1)}, bf16[2,16,32,128]{3,2,1,0:T(8,128)(2,1)S(1)}, u32[]{:S(2)}, u32[]{:S(2)}) collective-permute-start(bf16[2,16,32,128]{3,2,1,0:T(8,128)(2,1)} %get-tuple-element.148), channel_id=1, source_target_pairs={{0,15},{1,14},{2,13},{3,12},{4,11},{5,10},{6,9},{7,8},{8,7},{9,6},... | collective-permute-start | bytes 786440 | tf_op jit(solution)/shard_map/ppermute | solution.py:448
  153.5 49.5 %collective-permute-start.1 = (bf16[2,16,32,128]{3,2,1,0:T(8,128)(2,1)}, bf16[2,16,32,128]{3,2,1,0:T(8,128)(2,1)S(1)}, u32[]{:S(2)}, u32[]{:S(2)}) collective-permute-start(bf16[2,16,32,128]{3,2,1,0:T(8,128)(2,1)} %get-tuple-element.122), channel_id=1, source_target_pairs={{0,1},{1,0},{2,3},{3,2},{4,5},{5,4},{6,7},{7,6},{8,9},{9,8},{10,11... | collective-permute-start | bytes 786440 | tf_op jit(solution)/shard_map/ppermute | solution.py:448
  173.7 29.3 %collective-permute-start.2 = (bf16[2,16,32,128]{3,2,1,0:T(8,128)(2,1)}, bf16[2,16,32,128]{3,2,1,0:T(8,128)(2,1)S(1)}, u32[]{:S(2)}, u32[]{:S(2)}) collective-permute-start(bf16[2,16,32,128]{3,2,1,0:T(8,128)(2,1)} %copy-done.69), channel_id=1, source_target_pairs={{0,2},{1,3},{2,0},{3,1},{4,6},{5,7},{6,4},{7,5},{8,10},{9,11},{10,... | collective-permute-start | bytes 786440 | tf_op jit(solution)/shard_map/ppermute | solution.py:448
  173.9 40.9 %collective-permute-start.8 = (bf16[2,16,32,128]{3,2,1,0:T(8,128)(2,1)}, bf16[2,16,32,128]{3,2,1,0:T(8,128)(2,1)}, u32[]{:S(2)}, u32[]{:S(2)}) collective-permute-start(bf16[2,16,32,128]{3,2,1,0:T(8,128)(2,1)} %copy-done.68), channel_id=1, source_target_pairs={{0,8},{1,9},{2,10},{3,11},{4,12},{5,13},{6,14},{7,15},{8,0},{9,1},... | collective-permute-start | bytes 786440 | tf_op jit(solution)/shard_map/ppermute | solution.py:448
  176.4 47.1 %collective-permute-start.9 = (bf16[2,16,32,128]{3,2,1,0:T(8,128)(2,1)}, bf16[2,16,32,128]{3,2,1,0:T(8,128)(2,1)}, u32[]{:S(2)}, u32[]{:S(2)}) collective-permute-start(bf16[2,16,32,128]{3,2,1,0:T(8,128)(2,1)} %copy-done.67), channel_id=1, source_target_pairs={{0,9},{1,8},{2,11},{3,10},{4,13},{5,12},{6,15},{7,14},{8,1},{9,0},... | collective-permute-start | bytes 786440 | tf_op jit(solution)/shard_map/ppermute | solution.py:448
  189.1 45.2 %collective-permute-start.10 = (bf16[2,16,32,128]{3,2,1,0:T(8,128)(2,1)}, bf16[2,16,32,128]{3,2,1,0:T(8,128)(2,1)}, u32[]{:S(2)}, u32[]{:S(2)}) collective-permute-start(bf16[2,16,32,128]{3,2,1,0:T(8,128)(2,1)} %copy-done.66), channel_id=1, source_target_pairs={{0,10},{1,11},{2,8},{3,9},{4,14},{5,15},{6,12},{7,13},{8,2},{9,3},... | collective-permute-start | bytes 786440 | tf_op jit(solution)/shard_map/ppermute | solution.py:448
  203.0 55.6 %collective-permute-start.18 = (bf16[2,8,32,128]{3,2,1,0:T(8,128)(2,1)}, bf16[2,8,32,128]{3,2,1,0:T(8,128)(2,1)}, u32[]{:S(2)}, u32[]{:S(2)}) collective-permute-start(bf16[2,8,32,128]{3,2,1,0:T(8,128)(2,1)} %get-tuple-element.165), channel_id=1, source_target_pairs={{0,1},{1,0},{2,3},{3,2},{4,5},{5,4},{6,7},{7,6},{8,9},{9,8},{10,11... | collective-permute-start | bytes 393224 | tf_op jit(solution)/shard_map/ppermute | solution.py:448
  203.0 55.6 %collective-permute-start.19 = (bf16[2,8,32,128]{3,2,1,0:T(8,128)(2,1)}, bf16[2,8,32,128]{3,2,1,0:T(8,128)(2,1)}, u32[]{:S(2)}, u32[]{:S(2)}) collective-permute-start(bf16[2,8,32,128]{3,2,1,0:T(8,128)(2,1)} %get-tuple-element.166), channel_id=1, source_target_pairs={{0,2},{1,3},{2,0},{3,1},{4,6},{5,7},{6,4},{7,5},{8,10},{9,11},{10,... | collective-permute-start | bytes 393224 | tf_op jit(solution)/shard_map/ppermute | solution.py:448
  214.8 44.9 %collective-permute-start.25 = (bf16[2,8,32,128]{3,2,1,0:T(8,128)(2,1)}, bf16[2,8,32,128]{3,2,1,0:T(8,128)(2,1)}, u32[]{:S(2)}, u32[]{:S(2)}) collective-permute-start(bf16[2,8,32,128]{3,2,1,0:T(8,128)(2,1)} %get-tuple-element.185), channel_id=1, source_target_pairs={{0,8},{1,9},{2,10},{3,11},{4,12},{5,13},{6,14},{7,15},{8,0},{9,1},... | collective-permute-start | bytes 393224 | tf_op jit(solution)/shard_map/ppermute | solution.py:448
  223.5 40.1 %collective-permute-start.26 = (bf16[2,8,32,128]{3,2,1,0:T(8,128)(2,1)}, bf16[2,8,32,128]{3,2,1,0:T(8,128)(2,1)}, u32[]{:S(2)}, u32[]{:S(2)}) collective-permute-start(bf16[2,8,32,128]{3,2,1,0:T(8,128)(2,1)} %get-tuple-element.186), channel_id=1, source_target_pairs={{0,9},{1,8},{2,11},{3,10},{4,13},{5,12},{6,15},{7,14},{8,1},{9,0},... | collective-permute-start | bytes 393224 | tf_op jit(solution)/shard_map/ppermute | solution.py:448
  234.3 31.4 %collective-permute-start.27 = (bf16[2,8,32,128]{3,2,1,0:T(8,128)(2,1)}, bf16[2,8,32,128]{3,2,1,0:T(8,128)(2,1)}, u32[]{:S(2)}, u32[]{:S(2)}) collective-permute-start(bf16[2,8,32,128]{3,2,1,0:T(8,128)(2,1)} %get-tuple-element.187), channel_id=1, source_target_pairs={{0,10},{1,11},{2,8},{3,9},{4,14},{5,15},{6,12},{7,13},{8,2},{9,3},... | collective-permute-start | bytes 393224 | tf_op jit(solution)/shard_map/ppermute | solution.py:448
  265.7 25.4 %collective-permute-start.29 = (bf16[2,8,32,128]{3,2,1,0:T(8,128)(2,1)}, bf16[2,8,32,128]{3,2,1,0:T(8,128)(2,1)}, u32[]{:S(2)}, u32[]{:S(2)}) collective-permute-start(bf16[2,8,32,128]{3,2,1,0:T(8,128)(2,1)} %get-tuple-element.189), channel_id=1, source_target_pairs={{0,12},{1,13},{2,14},{3,15},{4,8},{5,9},{6,10},{7,11},{8,4},{9,5},... | collective-permute-start | bytes 393224 | tf_op jit(solution)/shard_map/ppermute | solution.py:448
  268.2 25.1 %collective-permute-start.30 = (bf16[2,8,32,128]{3,2,1,0:T(8,128)(2,1)}, bf16[2,8,32,128]{3,2,1,0:T(8,128)(2,1)}, u32[]{:S(2)}, u32[]{:S(2)}) collective-permute-start(bf16[2,8,32,128]{3,2,1,0:T(8,128)(2,1)} %get-tuple-element.190), channel_id=1, source_target_pairs={{0,13},{1,12},{2,15},{3,14},{4,9},{5,8},{6,11},{7,10},{8,5},{9,4},... | collective-permute-start | bytes 393224 | tf_op jit(solution)/shard_map/ppermute | solution.py:448
  291.2 22.6 %collective-permute-start.16 = (bf16[2,8,32,128]{3,2,1,0:T(8,128)(2,1)}, bf16[2,8,32,128]{3,2,1,0:T(8,128)(2,1)S(1)}, u32[]{:S(2)}, u32[]{:S(2)}) collective-permute-start(bf16[2,8,32,128]{3,2,1,0:T(8,128)(2,1)} %get-tuple-element.153), channel_id=1, source_target_pairs={{0,1},{1,0},{2,3},{3,2},{4,5},{5,4},{6,7},{7,6},{8,9},{9,8},{10,11... | collective-permute-start | bytes 393224 | tf_op jit(solution)/shard_map/ppermute | solution.py:448
  293.4 22.5 %collective-permute-start.17 = (bf16[2,8,32,128]{3,2,1,0:T(8,128)(2,1)}, bf16[2,8,32,128]{3,2,1,0:T(8,128)(2,1)S(1)}, u32[]{:S(2)}, u32[]{:S(2)}) collective-permute-start(bf16[2,8,32,128]{3,2,1,0:T(8,128)(2,1)} %get-tuple-element.154), channel_id=1, source_target_pairs={{0,2},{1,3},{2,0},{3,1},{4,6},{5,7},{6,4},{7,5},{8,10},{9,11},{10,... | collective-permute-start | bytes 393224 | tf_op jit(solution)/shard_map/ppermute | solution.py:448
  294.4 23.8 %collective-permute-start.39 = (bf16[2,8,32,128]{3,2,1,0:T(8,128)(2,1)}, bf16[2,8,32,128]{3,2,1,0:T(8,128)(2,1)S(1)}, u32[]{:S(2)}, u32[]{:S(2)}) collective-permute-start(bf16[2,8,32,128]{3,2,1,0:T(8,128)(2,1)} %get-tuple-element.210), channel_id=1, source_target_pairs={{0,9},{1,8},{2,11},{3,10},{4,13},{5,12},{6,15},{7,14},{8,1},{9,0},... | collective-permute-start | bytes 393224 | tf_op jit(solution)/shard_map/ppermute | solution.py:448
  319.5 24.7 %collective-permute-start.36 = (bf16[2,8,32,128]{3,2,1,0:T(8,128)(2,1)}, bf16[2,8,32,128]{3,2,1,0:T(8,128)(2,1)S(1)}, u32[]{:S(2)}, u32[]{:S(2)}) collective-permute-start(bf16[2,8,32,128]{3,2,1,0:T(8,128)(2,1)} %get-tuple-element.207), channel_id=1, source_target_pairs={{0,6},{1,7},{2,4},{3,5},{4,2},{5,3},{6,0},{7,1},{8,14},{9,15},{10,... | collective-permute-start | bytes 393224 | tf_op jit(solution)/shard_map/ppermute | solution.py:448
  (92 other events, 1525.5 us)

commit v3 on v0

--- a/solution.py
+++ b/solution.py
@@ -2,7 +2,11 @@
 
 import jax
 import jax.numpy as jnp
+import ml_dtypes
+import numpy as np
 from jax import lax
+from jax.experimental import pallas as pl
+from jax.experimental.pallas import tpu as pltpu
 from jax.sharding import PartitionSpec as P
 
 SPF = 2048
@@ -11,6 +15,11 @@
 CH0 = 256
 INPUTS = 1024
 BLK = 128
+LANES = 128
+UBLK = 16
+TBLK = 16
+FLIGHT = 5
+PITCH = TBLK + 1
 
 
 def passed_along(x, axis, by):
@@ -27,7 +36,7 @@
     return jnp.concatenate([jnp.cos(angle), -jnp.sin(angle)], axis=1).astype(jnp.bfloat16)
 
 
-def per_device(voltages, coeffs):
+def any_sizes(voltages, coeffs):
     inputs_here = voltages.shape[0]
     frames_here = voltages.shape[1]
     inp_count = lax.axis_size("inp")
@@ -79,6 +88,434 @@
     return jnp.stack(pieces, axis=2).astype(jnp.bfloat16)
 
 
+def turned_over(rows):
+    rows = list(rows)
+    place = lax.broadcasted_iota(jnp.int32, (8, LANES), 0)
+    for shift in (4, 2, 1):
+        low = jnp.bitwise_and(place, shift) == 0
+        for i in range(8):
+            if i & shift == 0:
+                near, far = rows[i], rows[i + shift]
+                rows[i] = jnp.where(low, near, pltpu.roll(far, shift, 0))
+                rows[i + shift] = jnp.where(low, pltpu.roll(near, 8 - shift, 0), far)
+    return rows
+
+
+def frames_of(v_ref, cols):
+    groups = []
+    for group in range(UBLK // 8):
+        groups.append(turned_over([v_ref[group * 8 + i, :, cols] for i in range(8)]))
+    return [[group[t].astype(jnp.float32) for group in groups] for t in range(8)]
+
+
+def history_kernel(v_ref, *refs):
+    out_ref = refs[-1]
+
+    def column(step, carry):
+        cols = pl.ds(pl.multiple_of(step * LANES, LANES), LANES)
+        for t, frame in enumerate(frames_of(v_ref, cols)):
+            out_ref[t, :, cols] = jnp.concatenate(frame, axis=0).astype(jnp.bfloat16)
+        return carry
+
+    lax.fori_loop(0, SPF // LANES, column, 0)
+
+
+def last_frames(voltages, after):
+    inputs, frames, _ = voltages.shape
+    last = frames // TAPS - 1
+    return pl.pallas_call(
+        history_kernel,
+        name="history",
+        grid=(inputs // UBLK,),
+        in_specs=[pl.BlockSpec((UBLK, TAPS, SPF), lambda i: (i, last, 0))]
+        + [pl.BlockSpec(memory_space=pl.ANY)] * len(after),
+        out_specs=pl.BlockSpec((TAPS, UBLK, SPF), lambda i: (0, i, 0)),
+        out_shape=jax.ShapeDtypeStruct((TAPS, inputs, SPF), jnp.bfloat16),
+    )(voltages, *after)
+
+
+def parity_tables(parts, width):
+    tables = []
+    for parity in range(2):
+        within = np.arange(parity, width, 2)
+        channel = (np.arange(parts)[:, None] * width + within[None, :]).reshape(-1) + CH0
+        phase = channel[:, None].astype(np.int64) * np.arange(SPF // 2)[None, :] % SPF
+        angle = phase.astype(np.float32) * np.float32(2.0 * math.pi / SPF)
+        wide = angle.astype(np.float64)
+        both = np.stack([np.cos(wide), -np.sin(wide)], axis=1)
+        both = both.reshape(-1, SPF // 2).astype(np.float32)
+        tables.append(jnp.asarray(both.astype(ml_dtypes.bfloat16)))
+    return tables
+
+
+def filter_step(block, sources, c_ref, even, odd):
+    half = SPF // 2
+    groups = UBLK // 8
+    here = pl.ds(pl.multiple_of(pl.program_id(0) * UBLK, UBLK), UBLK)
+
+    def column(step, carry):
+        sides = []
+        before = []
+        for side in range(2):
+            cols = pl.ds(pl.multiple_of(step * LANES + side * half, LANES), LANES)
+            weights = c_ref[:, cols].astype(jnp.float32)
+            taps = [jnp.broadcast_to(weights[k : k + 1], (8, LANES)) for k in range(TAPS)]
+            sides.append((cols, taps))
+            if block == 0:
+                wide = [sources[0][t, :, cols].astype(jnp.float32) for t in range(TAPS)]
+                before.append([[w[g * 8 : (g + 1) * 8] for g in range(groups)] for w in wide])
+            else:
+                before.append(frames_of(sources[0], cols))
+        out = pl.ds(pl.multiple_of(step * LANES, LANES), LANES)
+        for part in range(TBLK // TAPS):
+            made = []
+            for side, (cols, taps) in enumerate(sides):
+                now = frames_of(sources[1 + part], cols)
+                window = before[side] + now
+                before[side] = now
+                totals = []
+                for t in range(TAPS):
+                    frame = []
+                    for g in range(groups):
+                        total = taps[0] * window[TAPS + t][g]
+                        for k in range(1, TAPS):
+                            total = total + taps[k] * window[TAPS + t - k][g]
+                        frame.append(total)
+                    totals.append(jnp.concatenate(frame, axis=0))
+                made.append(totals)
+            for t in range(TAPS):
+                at = part * TAPS + t
+                even[at, here, out] = (made[0][t] + made[1][t]).astype(jnp.bfloat16)
+                odd[at, here, out] = (made[0][t] - made[1][t]).astype(jnp.bfloat16)
+        return carry
+
+    lax.fori_loop(0, half // LANES, column, 0)
+
+
+def front_kernel(block, parts, where, me_ref, *refs):
+    count = 1 + TBLK // TAPS
+    sources, c_ref, tables = refs[:count], refs[count], refs[count + 1 : count + 3]
+    earlier_ref = refs[count + 3] if block == 0 else None
+    outs = refs[count + (4 if block == 0 else 3) : -4]
+    power_ref, even, odd, turned = refs[-4:]
+    filter_step(block, sources, c_ref, even, odd)
+
+    @pl.when(pl.program_id(0) == pl.num_programs(0) - 1)
+    def _():
+        me = me_ref[0]
+        square = jnp.zeros((8, BLK), jnp.float32)
+        for parity, filtered in enumerate((even, odd)):
+            rows = tables[parity].shape[0]
+            own = rows // parts
+            spectrum = lax.dot_general(
+                tables[parity][...],
+                filtered[...].reshape(-1, SPF // 2),
+                (((1,), (1,)), ((), ())),
+                preferred_element_type=jnp.float32,
+            )
+            for t in range(TBLK):
+                frame = spectrum[:, t * BLK : (t + 1) * BLK]
+                turned[pl.ds(t, rows, stride=PITCH), :] = frame
+                square = square + jnp.sum((frame * frame).reshape(rows // 8, 8, BLK), axis=0)
+            for s in range(parts):
+                begin = jnp.bitwise_xor(me, s) * (own * PITCH)
+                for channel in range(own // 2):
+                    index, place = where(s, parity, channel)
+                    for half in range(2):
+                        row = channel * 2 + half
+                        value = turned[pl.ds(begin + row * PITCH, TBLK), :].astype(jnp.bfloat16)
+                        to = (place * 2 + half) * TBLK
+                        outs[index][to : to + TBLK, :] = value
+        if block == 0:
+            square = square + earlier_ref[...]
+            rest = jnp.sum(square, axis=0, keepdims=True)
+            terms = []
+            for _ in range(3):
+                term = rest.astype(jnp.bfloat16).astype(jnp.float32)
+                terms.append(term)
+                rest = rest - term
+            terms.append(jnp.zeros((TBLK - 3, BLK), jnp.float32))
+            tail = jnp.concatenate(terms, axis=0).astype(jnp.bfloat16)
+            for s in range(parts):
+                size = outs[s].shape[0]
+                outs[s][size - TBLK :, :] = tail
+        power_ref[...] = square
+
+
+def front(block, parts, me, voltages, coeffs, tables, shapes, where, history=None, earlier=None):
+    inputs, frames, _ = voltages.shape
+    half = SPF // 2
+    first = block * (TBLK // TAPS)
+    in_specs, operands = [], []
+    for place in range(first - 1, first + TBLK // TAPS):
+        if place < 0:
+            in_specs.append(pl.BlockSpec((TAPS, UBLK, SPF), lambda i, me: (0, i, 0)))
+            operands.append(history)
+        else:
+            in_specs.append(
+                pl.BlockSpec((UBLK, TAPS, SPF), lambda i, me, place=place: (i, place, 0))
+            )
+            operands.append(voltages)
+    operands += [coeffs, *tables]
+    if block == 0:
+        operands.append(earlier)
+    for array in operands[len(in_specs) :]:
+        in_specs.append(pl.BlockSpec(array.shape, lambda i, me: (0, 0)))
+    shapes = [jax.ShapeDtypeStruct(shape, jnp.bfloat16) for shape in shapes]
+    shapes.append(jax.ShapeDtypeStruct((8, BLK), jnp.float32))
+
+    def kernel(me_ref, *refs):
+        front_kernel(block, parts, where, me_ref, *refs)
+
+    return pl.pallas_call(
+        kernel,
+        name=f"front_{block}",
+        grid_spec=pltpu.PrefetchScalarGridSpec(
+            num_scalar_prefetch=1,
+            grid=(inputs // UBLK,),
+            in_specs=in_specs,
+            out_specs=[pl.BlockSpec(shape.shape, lambda i, me: (0, 0)) for shape in shapes],
+            scratch_shapes=[
+                pltpu.VMEM((TBLK, inputs, half), jnp.bfloat16),
+                pltpu.VMEM((TBLK, inputs, half), jnp.bfloat16),
+                pltpu.VMEM((tables[0].shape[0] * PITCH + 8, BLK), jnp.float32),
+            ],
+        ),
+        out_shape=shapes,
+        compiler_params=pltpu.CompilerParams(vmem_limit_bytes=50 * 2**20),
+    )(me, *operands)
+
+
+def correlate_kernel(parts, me_ref, *refs):
+    late, early, powers = refs[:parts], refs[parts : 2 * parts], refs[2 * parts : 3 * parts]
+    out_ref, token_ref, plain, other, columns, lines, shares = refs[-7:]
+    blocks = INPUTS // BLK
+    freq = parts // blocks
+    me = me_ref[0]
+
+    @pl.when(pl.program_id(0) == 0)
+    def _():
+        token_ref[...] = jnp.zeros_like(token_ref)
+        for s in range(parts):
+            terms = powers[s][...].astype(jnp.float32)
+            power = terms[0:1] + terms[1:2] + terms[2:3]
+            shares[jnp.bitwise_xor(me, s)] = jnp.broadcast_to(power, (8, BLK))
+        for r in range(blocks):
+            power = shares[r * freq]
+            for f in range(1, freq):
+                power = power + shares[r * freq + f]
+            gain = 1.0 / jnp.sqrt(power / (freq * 2 * TBLK * CH) + 1e-06)
+            lines[r] = gain
+            columns[r * BLK : (r + 1) * BLK, :] = jnp.broadcast_to(gain[0:1], (BLK, BLK)).T
+
+    for s in range(parts):
+        source = jnp.bitwise_xor(me, s)
+        block, place = source // freq, source % freq
+        for half, ref in enumerate((late[s], early[s])):
+            begin = pl.multiple_of((place * 2 + half) * 2 * TBLK, 2 * TBLK)
+            real = ref[:TBLK, :]
+            imag = ref[TBLK:, :]
+            plain[block, pl.ds(begin, TBLK), :] = real
+            plain[block, pl.ds(begin + TBLK, TBLK), :] = imag
+            other[block, pl.ds(begin, TBLK), :] = -imag
+            other[block, pl.ds(begin + TBLK, TBLK), :] = real
+
+    sides = [plain[r].T for r in range(blocks)]
+    for c in range(blocks):
+        weights = jnp.concatenate([plain[c], other[c]], axis=1)
+        line = lines[c][0:1] * (1.0 / (freq * 2 * TBLK))
+        for r in range(c + 1):
+            both = jnp.dot(sides[r], weights, preferred_element_type=jnp.float32)
+            pair = r * blocks - r * (r - 1) // 2 + (c - r)
+            gain = columns[r * BLK : (r + 1) * BLK, :] * line
+            for part in range(2):
+                piece = both[:, part * BLK : (part + 1) * BLK]
+                out_ref[0, part, pair] = (piece * gain).astype(jnp.bfloat16)
+
+
+def correlated(name, me, late, early, powers, spot, count, place, width, before, after=()):
+    parts = len(late)
+    blocks = INPUTS // BLK
+    pairs = blocks * (blocks + 1) // 2
+    span = parts // blocks * 4 * TBLK
+    first, second = spot
+    last = powers[0].shape[0] // TBLK - 1
+    in_specs = (
+        [pl.BlockSpec((2 * TBLK, BLK), lambda i, me: (first + i, 0))] * parts
+        + [pl.BlockSpec((2 * TBLK, BLK), lambda i, me: (second + i, 0))] * parts
+        + [pl.BlockSpec((TBLK, BLK), lambda i, me: (last, 0))] * parts
+    )
+    operands = [me, *late, *early, *powers]
+    aliases = {}
+    if before is not None:
+        aliases[len(operands)] = 0
+        operands.append(before)
+    operands += list(after)
+    in_specs += [pl.BlockSpec(memory_space=pl.ANY)] * (len(operands) - 1 - len(in_specs))
+
+    def kernel(me_ref, *refs):
+        correlate_kernel(parts, me_ref, *refs)
+
+    return pl.pallas_call(
+        kernel,
+        name=name,
+        grid_spec=pltpu.PrefetchScalarGridSpec(
+            num_scalar_prefetch=1,
+            grid=(count,),
+            in_specs=in_specs,
+            out_specs=[
+                pl.BlockSpec(
+                    (1, 2, pairs, BLK, BLK), lambda i, me: (place + 2 * i, 0, 0, 0, 0)
+                ),
+                pl.BlockSpec((8, BLK), lambda i, me: (0, 0)),
+            ],
+            scratch_shapes=[
+                pltpu.VMEM((blocks, span, BLK), jnp.bfloat16),
+                pltpu.VMEM((blocks, span, BLK), jnp.bfloat16),
+                pltpu.VMEM((INPUTS, BLK), jnp.float32),
+                pltpu.VMEM((blocks, 8, BLK), jnp.float32),
+                pltpu.VMEM((parts, 8, BLK), jnp.float32),
+            ],
+        ),
+        out_shape=[
+            jax.ShapeDtypeStruct((width, 2, pairs, BLK, BLK), jnp.bfloat16),
+            jax.ShapeDtypeStruct((8, BLK), jnp.float32),
+        ],
+        input_output_aliases=aliases,
+        compiler_params=pltpu.CompilerParams(vmem_limit_bytes=24 * 2**20),
+    )(*operands)
+
+
+def nothing_kernel(*refs):
+    del refs
+
+
+def gated(name, messages, after):
+    spec = pl.BlockSpec(memory_space=pl.ANY)
+    return pl.pallas_call(
+        nothing_kernel,
+        name=name,
+        in_specs=[spec] * (len(messages) + len(after)),
+        out_specs=[spec] * len(messages),
+        out_shape=[jax.ShapeDtypeStruct(m.shape, m.dtype) for m in messages],
+        input_output_aliases={i: i for i in range(len(messages))},
+    )(*messages, *after)
+
+
+def per_device(voltages, coeffs):
+    freq_count = lax.axis_size("freq")
+    parts = lax.axis_size("inp") * freq_count
+    inputs, frames, _ = voltages.shape
+    width = CH // parts
+    fits = (
+        inputs == BLK
+        and frames == 2 * TBLK
+        and TBLK % TAPS == 0
+        and parts & (parts - 1) == 0
+        and parts >= 16
+        and width % 16 == 0
+        and parts * BLK == INPUTS * freq_count
+        and freq_count * frames * 2 == LANES
+    )
+    if not fits:
+        return any_sizes(voltages, coeffs)
+    axes = ("inp", "freq")
+    me = lax.axis_index("inp") * freq_count + lax.axis_index("freq")
+    me = me.astype(jnp.int32).reshape(1)
+    half = width // 2
+    extra = half // 4
+    tables = parity_tables(parts, width)
+
+    far, near = list(range(parts // 2, parts)), list(range(1, parts // 2))
+    far = [s for pair in zip(far[: parts // 4], far[parts // 4 :]) for s in pair]
+    log = []
+
+    def send(name, messages, order, arrived, after=()):
+        for s in order:
+            waits = list(after) + (log[-FLIGHT:][:1] if len(log) >= FLIGHT else [])
+            message = messages[s]
+            if waits:
+                (message,) = gated(f"gate_{name}_{s}", [message], waits)
+            arrived[s] = lax.ppermute(message, axes, [(i, i ^ s) for i in range(parts)])
+            log.append(arrived[s])
+
+    def mixed(some_far, some_near):
+        out = []
+        while some_far or some_near:
+            out += some_far[:2] + some_near[:1] if some_far else some_near
+            some_near = some_near[1:] if some_far else []
+            some_far = some_far[2:]
+        return out
+
+    made = front(
+        1,
+        parts,
+        me,
+        voltages,
+        coeffs,
+        tables,
+        [(width * 2 * TBLK, BLK)] * parts,
+        lambda s, parity, channel: (s, parity * half + channel),
+    )
+    late, earlier = {0: made[0]}, made[parts]
+    ahead = FLIGHT - 1
+    send("late", made, near[:1] + far[:ahead], late)
+
+    history = passed_along(last_frames(voltages, [late[1]]), "freq", 1)
+    made_early = front(
+        0,
+        parts,
+        me,
+        voltages,
+        coeffs,
+        tables,
+        [((half + extra) * 2 * TBLK + TBLK, BLK)] * parts + [((half - extra) * 2 * TBLK, BLK)] * parts,
+        lambda s, parity, channel: (
+            (s, parity * half + channel)
+            if parity == 0 or channel < extra
+            else (parts + s, channel - extra)
+        ),
+        history,
+        earlier,
+    )
+    send("late", made, mixed(far[ahead:], near[1:]), late, [made_early[-1]])
+    one, two = made_early[:parts], made_early[parts : 2 * parts]
+    early, rest = {0: one[0]}, {0: two[0]}
+    send("one", one, mixed(far, near), early)
+
+    def every(found):
+        return [found[s] for s in range(parts)]
+
+    send("two", two, far[:FLIGHT], rest)
+    late, early = every(late), every(early)
+    left_far, left_near = far[FLIGHT:], list(near)
+    out, after = None, []
+    pieces = [(parity, i) for parity, size in ((0, half), (1, extra)) for i in range(0, size, extra)]
+    for parity, i in pieces:
+        spot = (parity * half + i, parity * half + i)
+        out, token = correlated(
+            f"correlate_{parity}_{i}", me, late, early, early, spot, extra, 2 * i + parity, width, out, after
+        )
+        final = (parity, i) == pieces[-1]
+        now = left_near if final else left_near[:1]
+        send("two", two, now + left_far[: len(left_far) if final else 1], rest, [token])
+        after = [rest[now[0]]] if now else []
+        left_near, left_far = left_near[1:], left_far[1:]
+    out, _ = correlated(
+        "correlate_rest",
+        me,
+        late,
+        every(rest),
+        early,
+        (half + extra, 0),
+        half - extra,
+        2 * extra + 1,
+        width,
+        out,
+    )
+    return out
+
+
 def solution(mesh):
     in_specs = (P(("grp", "inp"), "freq", None), P())
     out_specs = P(("grp", "inp", "freq"), None, None, None, None)

time: 869 us -> 415 us (0.48)
  other arithmetic: 214 us -> 0 us
  blocking collectives: 192 us -> 0 us
  matrix products: 152 us -> 0 us
  local copies, waits for them, and re-layouts: 299 us -> 153 us
  Pallas kernels: 0 us -> 105 us
  starting transfers between devices: 2.9 us -> 87.3 us
  waiting for transfers between devices: 0.01 us -> 64.7 us
    all_to_all x1 -> x0, blocking collectives: 189 us -> none  [per_device(): lax.all_to_all(scaled[None], ('inp', 'freq'), split_axis=2, concat_axis=0...]
    dot_general x17 -> x0, matrix products: 152 us -> none  [the longest x8 75.3 us: per_device(): jnp.einsum('cut,cmt->cum', row_panel, other[:, row_index * BLK:], preferr...]
    convert_element_type x4 -> x0, other arithmetic: 141 us -> none  [the longest x1 109 us: per_device(): summed.astype(jnp.bfloat16).reshape(inputs_here * frames_here, SPF)]
    pallas_call x0 -> x49, Pallas kernels: none -> 105 us  [the longest x2 49 us: front(): pl.pallas_call(kernel, name=f'front_{block}', grid_spec=pltpu.PrefetchSca...]
    another operation x3 -> x0, local copies, waits for them, and re-layouts: 92.4 us -> none  [the longest x1 49.6 us: per_device(): return jnp.stack(pieces, axis=2).astype(jnp.bfloat16)]
    ppermute x0 -> x45, starting transfers between devices: none -> 84.5 us  [send(): arrived[s] = lax.ppermute(message, axes, [(i, i ^ s) for i in range(parts)])]
    unnamed x103 -> x410, local copies, waits for them, and re-layouts: 81.1 us -> 153 us
    ppermute x0 -> x45, waiting for transfers between devices: none -> 64.7 us  [send(): arrived[s] = lax.ppermute(message, axes, [(i, i ^ s) for i in range(parts)])]
  transfers between devices with their start and end apart: 1 -> 46, of which waited for: 0 -> 15; matrix products, arithmetic and copies ran while one was open for 5% -> 0% of each run, Pallas kernels for 0% -> 13%
where the time goes in v3:
time: 415 us; the launch traced here: 411 us
  local copies, waits for them, and re-layouts  153 us (37%)
  Pallas kernels  105 us (25%)
  starting transfers between devices  87.3 us (21%)
  waiting for transfers between devices  64.7 us (16%)
    unnamed x410, local copies, waits for them, and re-layouts  153 us
    ppermute x45, starting transfers between devices, send(): arrived[s] = lax.ppermute(message, axes, [(i, i ^ s) for i in range(parts)])  84.5 us
    ppermute x45, waiting for transfers between devices, send(): arrived[s] = lax.ppermute(message, axes, [(i, i ^ s) for i in range(parts)])  64.7 us
    pallas_call x2, Pallas kernels, front(): pl.pallas_call(kernel, name=f'front_{block}', grid_spec=pltpu.PrefetchSca...  49 us
    pallas_call x6, Pallas kernels, correlated(): pl.pallas_call(kernel, name=name, grid_spec=pltpu.PrefetchScalarGridSpec(...  47.5 us
    pallas_call x1, Pallas kernels, last_frames(): pl.pallas_call(history_kernel, name='history', grid=(inputs // UBLK,), in...  8.79 us
  transfers between devices with their start and end apart: 46, of which 15 were waited for; matrix products, arithmetic and copies ran while one was open for 0% of the time, Pallas kernels for 13%

profile of v3, /device:TPU:0, one launch (start us, length us, event | category | flops | bytes accessed | tf_op | source)
XLA Modules:
  0.0 411.1 jit_solution(17390146509365782739)
XLA Ops:
  0.8 25.1 %front_1.1 = (bf16[1024,128]{1,0:T(8,128)(2,1)S(1)}, bf16[1024,128]{1,0:T(8,128)(2,1)S(1)}, bf16[1024,128]{1,0:T(8,128)(2,1)S(1)}, bf16[1024,128]{1,0:T(8,128)(2...) custom-call(s32[1]{0:T(128)} %bitcast.me_ref, ...), custom_call_target="tpu_custom_call" | custom-call | tf_op jit(solution)/shard_map/front_1/pallas_call | solution.py:270
  35.4 8.8 %history.1 = bf16[8,128,2048]{2,1,0:T(8,128)(2,1)} custom-call(s32[128,32,2048]{2,1,0:T(8,128)} %refs_2_.3, bf16[1024,128]{1,0:T(8,128)(2,1)} %copy-done.56), custom_call_target="tpu_custom_call" | custom-call | tf_op jit(solution)/shard_map/history/pallas_call | solution.py:126
  47.0 4.8 %collective-permute-start.2 = (bf16[1024,128]{1,0:T(8,128)(2,1)S(1)}, bf16[1024,128]{1,0:T(8,128)(2,1)S(1)}, u32[]{:S(2)}, u32[]{:S(2)}) collective-permute-start(bf16[1024,128]{1,0:T(8,128)(2,1)S(1)} %get-tuple-element.71), channel_id=1, source_target_pairs={{0,12},{1,13},{2,14},{3,15},{4,8},{5,9},{6,10},{7,11},{8,4},{9,5},... | collective-permute-start | bytes 786440 | tf_op jit(solution)/shard_map/ppermute | solution.py:439
  56.6 23.9 %front_0.1 = (bf16[656,128]{1,0:T(8,128)(2,1)S(1)}, bf16[656,128]{1,0:T(8,128)(2,1)S(1)}, bf16[656,128]{1,0:T(8,128)(2,1)S(1)}, bf16[656,128]{1,0:T(8,128)(2,1)S...) custom-call(s32[1]{0:T(128)} %bitcast.me_ref, ...), custom_call_target="tpu_custom_call" | custom-call | tf_op jit(solution)/shard_map/front_0/pallas_call | solution.py:270
  100.0 3.6 collective-permute-start.4
  111.9 21.7 %collective-permute-done.4.refs_2_.refs_10_ = bf16[1024,128]{1,0:T(8,128)(2,1)S(1)} collective-permute-done((bf16[1024,128]{1,0:T(8,128)(2,1)}, bf16[1024,128]{1,0:T(8,128)(2,1)S(1)}, u32[]{:S(2)}, u32[]{:S(2)}) %collective-permute-start.4) | collective-permute-done | bytes 262176 | tf_op jit(solution)/shard_map/ppermute | solution.py:439
  136.5 4.1 collective-permute-start.8
  140.5 3.6 collective-permute-done.11.refs_2_.refs_11_
  146.8 5.3 %collective-permute-start.15 = (bf16[1024,128]{1,0:T(8,128)(2,1)}, bf16[1024,128]{1,0:T(8,128)(2,1)S(1)}, u32[]{:S(2)}, u32[]{:S(2)}) collective-permute-start(bf16[1024,128]{1,0:T(8,128)(2,1)} %gate_late_7.1), channel_id=1, source_target_pairs={{0,7},{1,6},{2,5},{3,4},{4,3},{5,2},{6,1},{7,0},{8,15},{9,14},{10,... | collective-permute-start | bytes 786440 | tf_op jit(solution)/shard_map/ppermute | solution.py:439
  156.6 3.4 collective-permute-start.21
  160.0 4.9 %collective-permute-done.12.refs_1_.refs_6_ = bf16[1024,128]{1,0:T(8,128)(2,1)S(1)} collective-permute-done((bf16[1024,128]{1,0:T(8,128)(2,1)}, bf16[1024,128]{1,0:T(8,128)(2,1)S(1)}, u32[]{:S(2)}, u32[]{:S(2)}) %collective-permute-start.12) | collective-permute-done | bytes 262176 | tf_op jit(solution)/shard_map/ppermute | solution.py:439
  165.6 4.8 %collective-permute-start.19 = (bf16[656,128]{1,0:T(8,128)(2,1)}, bf16[656,128]{1,0:T(8,128)(2,1)S(1)}, u32[]{:S(2)}, u32[]{:S(2)}) collective-permute-start(bf16[656,128]{1,0:T(8,128)(2,1)} %gate_one_9.1), channel_id=1, source_target_pairs={{0,9},{1,8},{2,11},{3,10},{4,13},{5,12},{6,15},{7,14},{8,1},{9,0},... | collective-permute-start | bytes 503816 | tf_op jit(solution)/shard_map/ppermute | solution.py:439
  170.4 6.6 %collective-permute-done.15.refs_1_.refs_7_ = bf16[1024,128]{1,0:T(8,128)(2,1)S(1)} collective-permute-done((bf16[1024,128]{1,0:T(8,128)(2,1)}, bf16[1024,128]{1,0:T(8,128)(2,1)S(1)}, u32[]{:S(2)}, u32[]{:S(2)}) %collective-permute-start.15) | collective-permute-done | bytes 262176 | tf_op jit(solution)/shard_map/ppermute | solution.py:439
  186.8 10.2 %collective-permute-start.28 = (bf16[656,128]{1,0:T(8,128)(2,1)}, bf16[656,128]{1,0:T(8,128)(2,1)S(1)}, u32[]{:S(2)}, u32[]{:S(2)}) collective-permute-start(bf16[656,128]{1,0:T(8,128)(2,1)} %gate_one_11.1), channel_id=1, source_target_pairs={{0,11},{1,10},{2,9},{3,8},{4,15},{5,14},{6,13},{7,12},{8,3},{9,2},... | collective-permute-start | bytes 503816 | tf_op jit(solution)/shard_map/ppermute | solution.py:439
  199.9 9.3 %collective-permute-done.22.refs_1_.refs_26_.refs_42_ = bf16[656,128]{1,0:T(8,128)(2,1)S(1)} collective-permute-done((bf16[656,128]{1,0:T(8,128)(2,1)}, bf16[656,128]{1,0:T(8,128)(2,1)S(1)}, u32[]{:S(2)}, u32[]{:S(2)}) %collective-permute-start.22) | collective-permute-done | bytes 167968 | tf_op jit(solution)/shard_map/ppermute | solution.py:439
  214.1 4.9 %collective-permute-start.31 = (bf16[384,128]{1,0:T(8,128)(2,1)}, bf16[384,128]{1,0:T(8,128)(2,1)}, u32[]{:S(2)}, u32[]{:S(2)}) collective-permute-start(bf16[384,128]{1,0:T(8,128)(2,1)} %gate_two_8.1), channel_id=1, source_target_pairs={{0,8},{1,9},{2,10},{3,11},{4,12},{5,13},{6,14},{7,15},{8,0},{9,1},... | collective-permute-start | bytes 294920 | tf_op jit(solution)/shard_map/ppermute | solution.py:439
  219.0 6.4 %collective-permute-done.26.refs_22_.refs_38_.refs_1_ = bf16[656,128]{1,0:T(8,128)(2,1)S(1)} collective-permute-done((bf16[656,128]{1,0:T(8,128)(2,1)}, bf16[656,128]{1,0:T(8,128)(2,1)S(1)}, u32[]{:S(2)}, u32[]{:S(2)}) %collective-permute-start.26) | collective-permute-done | bytes 167968 | tf_op jit(solution)/shard_map/ppermute | solution.py:439
  252.1 6.1 %correlate_0_0.1 = (bf16[32,2,36,128,128]{4,3,2,1,0:T(8,128)(2,1)}, f32[8,128]{1,0:T(8,128)S(1)}) custom-call(s32[1]{0:T(128)} %bitcast.me_ref, bf16[1024,128]{1,0:T(8,128)(2,1)S(1)} %copy-done.151, bf16[1024,128]{1,0:T(8,128)(2,1)S(1)} %copy-done.57, bf16[1024,128]{1,0:T(8,128)(2,1)S(1)} %copy-done.88, bf16[1024,128]{1,0:T(8,128)(2,1)S(1)} %copy-done.116, ...), custom_call_target="tpu_custom_call" | custom-call | tf_op jit(solution)/shard_map/correlate_0_0/pallas_call | solution.py:359
  286.9 6.1 %correlate_0_4.1 = (bf16[32,2,36,128,128]{4,3,2,1,0:T(8,128)(2,1)}, f32[8,128]{1,0:T(8,128)S(1)}) custom-call(s32[1]{0:T(128)} %bitcast.me_ref, bf16[1024,128]{1,0:T(8,128)(2,1)S(1)} %copy-done.152, bf16[1024,128]{1,0:T(8,128)(2,1)S(1)} %copy-done.57, bf16[1024,128]{1,0:T(8,128)(2,1)S(1)} %copy-done.89, ...), custom_call_target="tpu_custom_call", output_to_operand_aliasing={{0}: (49, {})} | custom-call | tf_op jit(solution)/shard_map/correlate_0_4/pallas_call | solution.py:359
  313.7 6.1 %correlate_0_8.1 = (bf16[32,2,36,128,128]{4,3,2,1,0:T(8,128)(2,1)}, f32[8,128]{1,0:T(8,128)S(1)}) custom-call(s32[1]{0:T(128)} %bitcast.me_ref, bf16[1024,128]{1,0:T(8,128)(2,1)S(1)} %copy-done.153, bf16[1024,128]{1,0:T(8,128)(2,1)S(1)} %copy-done.57, bf16[1024,128]{1,0:T(8,128)(2,1)S(1)} %copy-done.90, ...), custom_call_target="tpu_custom_call", output_to_operand_aliasing={{0}: (49, {})} | custom-call | tf_op jit(solution)/shard_map/correlate_0_8/pallas_call | solution.py:359
  338.6 6.1 %correlate_0_12.1 = (bf16[32,2,36,128,128]{4,3,2,1,0:T(8,128)(2,1)}, f32[8,128]{1,0:T(8,128)S(1)}) custom-call(s32[1]{0:T(128)} %bitcast.me_ref, bf16[1024,128]{1,0:T(8,128)(2,1)S(1)} %copy-done.154, bf16[1024,128]{1,0:T(8,128)(2,1)S(1)} %copy-done.57, bf16[1024,128]{1,0:T(8,128)(2,1)S(1)} %copy-done.91, ...), custom_call_target="tpu_custom_call", output_to_operand_aliasing={{0}: (49, {})} | custom-call | tf_op jit(solution)/shard_map/correlate_0_12/pallas_call | solution.py:359
  363.2 6.1 %correlate_1_0.1 = (bf16[32,2,36,128,128]{4,3,2,1,0:T(8,128)(2,1)}, f32[8,128]{1,0:T(8,128)S(1)}) custom-call(s32[1]{0:T(128)} %bitcast.me_ref, bf16[1024,128]{1,0:T(8,128)(2,1)S(1)} %copy-done.155, bf16[1024,128]{1,0:T(8,128)(2,1)S(1)} %copy-done.57, bf16[1024,128]{1,0:T(8,128)(2,1)S(1)} %copy-done.92, ...), custom_call_target="tpu_custom_call", output_to_operand_aliasing={{0}: (49, {})} | custom-call | tf_op jit(solution)/shard_map/correlate_1_0/pallas_call | solution.py:359
  374.4 5.9 %collective-permute-done.43.refs_22_ = bf16[384,128]{1,0:T(8,128)(2,1)} collective-permute-done((bf16[384,128]{1,0:T(8,128)(2,1)}, bf16[384,128]{1,0:T(8,128)(2,1)}, u32[]{:S(2)}, u32[]{:S(2)}) %collective-permute-start.43) | collective-permute-done | bytes 98336 | tf_op jit(solution)/shard_map/ppermute | solution.py:439
  394.0 16.9 %correlate_rest.1 = (bf16[32,2,36,128,128]{4,3,2,1,0:T(8,128)(2,1)}, f32[8,128]{1,0:T(8,128)}) custom-call(s32[1]{0:T(128)} %bitcast.me_ref, bf16[1024,128]{1,0:T(8,128)(2,1)S(1)} %copy-done.156, bf16[1024,128]{1,0:T(8,128)(2,1)S(1)} %copy-done.57, bf16[1024,128]{1,0:T(8,128)(2,1)S(1)} %copy-done.93, ...), custom_call_target="tpu_custom_call", output_to_operand_aliasing={{0}: (49, {})} | custom-call | tf_op jit(solution)/shard_map/correlate_rest/pallas_call | solution.py:359
  (527 shorter events, 205.7 us)
Async XLA Ops:
  47.0 56.6 %collective-permute-start.2 = (bf16[1024,128]{1,0:T(8,128)(2,1)S(1)}, bf16[1024,128]{1,0:T(8,128)(2,1)S(1)}, u32[]{:S(2)}, u32[]{:S(2)}) collective-permute-start(bf16[1024,128]{1,0:T(8,128)(2,1)S(1)} %get-tuple-element.71), channel_id=1, source_target_pairs={{0,12},{1,13},{2,14},{3,15},{4,8},{5,9},{6,10},{7,11},{8,4},{9,5},... | collective-permute-start | bytes 786440 | tf_op jit(solution)/shard_map/ppermute | solution.py:439
  51.8 53.1 %collective-permute-start.6 = (bf16[1024,128]{1,0:T(8,128)(2,1)S(1)}, bf16[1024,128]{1,0:T(8,128)(2,1)S(1)}, u32[]{:S(2)}, u32[]{:S(2)}) collective-permute-start(bf16[1024,128]{1,0:T(8,128)(2,1)S(1)} %get-tuple-element.76), channel_id=1, source_target_pairs={{0,8},{1,9},{2,10},{3,11},{4,12},{5,13},{6,14},{7,15},{8,0},{9,1},... | collective-permute-start | bytes 786440 | tf_op jit(solution)/shard_map/ppermute | solution.py:439
  51.8 56.1 %collective-permute-start.10 = (bf16[1024,128]{1,0:T(8,128)(2,1)S(1)}, bf16[1024,128]{1,0:T(8,128)(2,1)S(1)}, u32[]{:S(2)}, u32[]{:S(2)}) collective-permute-start(bf16[1024,128]{1,0:T(8,128)(2,1)S(1)} %get-tuple-element.80), channel_id=1, source_target_pairs={{0,9},{1,8},{2,11},{3,10},{4,13},{5,12},{6,15},{7,14},{8,1},{9,0},... | collective-permute-start | bytes 786440 | tf_op jit(solution)/shard_map/ppermute | solution.py:439
  52.9 56.5 %collective-permute-start.13 = (bf16[1024,128]{1,0:T(8,128)(2,1)S(1)}, bf16[1024,128]{1,0:T(8,128)(2,1)S(1)}, u32[]{:S(2)}, u32[]{:S(2)}) collective-permute-start(bf16[1024,128]{1,0:T(8,128)(2,1)S(1)} %get-tuple-element.83), channel_id=1, source_target_pairs={{0,13},{1,12},{2,15},{3,14},{4,9},{5,8},{6,11},{7,10},{8,5},{9,4},... | collective-permute-start | bytes 786440 | tf_op jit(solution)/shard_map/ppermute | solution.py:439
  100.0 33.6 %collective-permute-start.4 = (bf16[1024,128]{1,0:T(8,128)(2,1)}, bf16[1024,128]{1,0:T(8,128)(2,1)S(1)}, u32[]{:S(2)}, u32[]{:S(2)}) collective-permute-start(bf16[1024,128]{1,0:T(8,128)(2,1)} %gate_late_10.1), channel_id=1, source_target_pairs={{0,10},{1,11},{2,8},{3,9},{4,14},{5,15},{6,12},{7,13},{8,2},{9,3},... | collective-permute-start | bytes 786440 | tf_op jit(solution)/shard_map/ppermute | solution.py:439
  104.4 30.2 %collective-permute-start.3 = (bf16[1024,128]{1,0:T(8,128)(2,1)}, bf16[1024,128]{1,0:T(8,128)(2,1)S(1)}, u32[]{:S(2)}, u32[]{:S(2)}) collective-permute-start(bf16[1024,128]{1,0:T(8,128)(2,1)} %gate_late_2.1), channel_id=1, source_target_pairs={{0,2},{1,3},{2,0},{3,1},{4,6},{5,7},{6,4},{7,5},{8,10},{9,11},{10,... | collective-permute-start | bytes 786440 | tf_op jit(solution)/shard_map/ppermute | solution.py:439
  105.6 30.1 %collective-permute-start.7 = (bf16[1024,128]{1,0:T(8,128)(2,1)}, bf16[1024,128]{1,0:T(8,128)(2,1)S(1)}, u32[]{:S(2)}, u32[]{:S(2)}) collective-permute-start(bf16[1024,128]{1,0:T(8,128)(2,1)} %gate_late_14.1), channel_id=1, source_target_pairs={{0,14},{1,15},{2,12},{3,13},{4,10},{5,11},{6,8},{7,9},{8,6},{9,7},... | collective-permute-start | bytes 786440 | tf_op jit(solution)/shard_map/ppermute | solution.py:439
  108.6 35.5 %collective-permute-start.11 = (bf16[1024,128]{1,0:T(8,128)(2,1)}, bf16[1024,128]{1,0:T(8,128)(2,1)S(1)}, u32[]{:S(2)}, u32[]{:S(2)}) collective-permute-start(bf16[1024,128]{1,0:T(8,128)(2,1)} %gate_late_11.1), channel_id=1, source_target_pairs={{0,11},{1,10},{2,9},{3,8},{4,15},{5,14},{6,13},{7,12},{8,3},{9,2},... | collective-permute-start | bytes 786440 | tf_op jit(solution)/shard_map/ppermute | solution.py:439
  110.1 35.9 %collective-permute-start.14 = (bf16[1024,128]{1,0:T(8,128)(2,1)}, bf16[1024,128]{1,0:T(8,128)(2,1)S(1)}, u32[]{:S(2)}, u32[]{:S(2)}) collective-permute-start(bf16[1024,128]{1,0:T(8,128)(2,1)} %gate_late_15.1), channel_id=1, source_target_pairs={{0,15},{1,14},{2,13},{3,12},{4,11},{5,10},{6,9},{7,8},{8,7},{9,6},... | collective-permute-start | bytes 786440 | tf_op jit(solution)/shard_map/ppermute | solution.py:439
  146.8 30.2 %collective-permute-start.15 = (bf16[1024,128]{1,0:T(8,128)(2,1)}, bf16[1024,128]{1,0:T(8,128)(2,1)S(1)}, u32[]{:S(2)}, u32[]{:S(2)}) collective-permute-start(bf16[1024,128]{1,0:T(8,128)(2,1)} %gate_late_7.1), channel_id=1, source_target_pairs={{0,7},{1,6},{2,5},{3,4},{4,3},{5,2},{6,1},{7,0},{8,15},{9,14},{10,... | collective-permute-start | bytes 786440 | tf_op jit(solution)/shard_map/ppermute | solution.py:439
  152.8 25.3 %collective-permute-start.17 = (bf16[656,128]{1,0:T(8,128)(2,1)}, bf16[656,128]{1,0:T(8,128)(2,1)S(1)}, u32[]{:S(2)}, u32[]{:S(2)}) collective-permute-start(bf16[656,128]{1,0:T(8,128)(2,1)} %gate_one_8.1), channel_id=1, source_target_pairs={{0,8},{1,9},{2,10},{3,11},{4,12},{5,13},{6,14},{7,15},{8,0},{9,1},... | collective-permute-start | bytes 503816 | tf_op jit(solution)/shard_map/ppermute | solution.py:439
  154.9 25.4 %collective-permute-start.16 = (bf16[656,128]{1,0:T(8,128)(2,1)}, bf16[656,128]{1,0:T(8,128)(2,1)S(1)}, u32[]{:S(2)}, u32[]{:S(2)}) collective-permute-start(bf16[656,128]{1,0:T(8,128)(2,1)} %gate_one_1.1), channel_id=1, source_target_pairs={{0,1},{1,0},{2,3},{3,2},{4,5},{5,4},{6,7},{7,6},{8,9},{9,8},{10,11... | collective-permute-start | bytes 503816 | tf_op jit(solution)/shard_map/ppermute | solution.py:439
  156.6 27.5 %collective-permute-start.21 = (bf16[656,128]{1,0:T(8,128)(2,1)}, bf16[656,128]{1,0:T(8,128)(2,1)S(1)}, u32[]{:S(2)}, u32[]{:S(2)}) collective-permute-start(bf16[656,128]{1,0:T(8,128)(2,1)} %gate_one_12.1), channel_id=1, source_target_pairs={{0,12},{1,13},{2,14},{3,15},{4,8},{5,9},{6,10},{7,11},{8,4},{9,5},... | collective-permute-start | bytes 503816 | tf_op jit(solution)/shard_map/ppermute | solution.py:439
  184.8 24.4 %collective-permute-start.22 = (bf16[656,128]{1,0:T(8,128)(2,1)}, bf16[656,128]{1,0:T(8,128)(2,1)S(1)}, u32[]{:S(2)}, u32[]{:S(2)}) collective-permute-start(bf16[656,128]{1,0:T(8,128)(2,1)} %gate_one_10.1), channel_id=1, source_target_pairs={{0,10},{1,11},{2,8},{3,9},{4,14},{5,15},{6,12},{7,13},{8,2},{9,3},... | collective-permute-start | bytes 503816 | tf_op jit(solution)/shard_map/ppermute | solution.py:439
  185.5 24.5 %collective-permute-start.20 = (bf16[656,128]{1,0:T(8,128)(2,1)}, bf16[656,128]{1,0:T(8,128)(2,1)S(1)}, u32[]{:S(2)}, u32[]{:S(2)}) collective-permute-start(bf16[656,128]{1,0:T(8,128)(2,1)} %gate_one_3.1), channel_id=1, source_target_pairs={{0,3},{1,2},{2,1},{3,0},{4,7},{5,6},{6,5},{7,4},{8,11},{9,10},{10,... | collective-permute-start | bytes 503816 | tf_op jit(solution)/shard_map/ppermute | solution.py:439
  186.8 25.8 %collective-permute-start.28 = (bf16[656,128]{1,0:T(8,128)(2,1)}, bf16[656,128]{1,0:T(8,128)(2,1)S(1)}, u32[]{:S(2)}, u32[]{:S(2)}) collective-permute-start(bf16[656,128]{1,0:T(8,128)(2,1)} %gate_one_11.1), channel_id=1, source_target_pairs={{0,11},{1,10},{2,9},{3,8},{4,15},{5,14},{6,13},{7,12},{8,3},{9,2},... | collective-permute-start | bytes 503816 | tf_op jit(solution)/shard_map/ppermute | solution.py:439
  214.1 44.7 %collective-permute-start.31 = (bf16[384,128]{1,0:T(8,128)(2,1)}, bf16[384,128]{1,0:T(8,128)(2,1)}, u32[]{:S(2)}, u32[]{:S(2)}) collective-permute-start(bf16[384,128]{1,0:T(8,128)(2,1)} %gate_two_8.1), channel_id=1, source_target_pairs={{0,8},{1,9},{2,10},{3,11},{4,12},{5,13},{6,14},{7,15},{8,0},{9,1},... | collective-permute-start | bytes 294920 | tf_op jit(solution)/shard_map/ppermute | solution.py:439
  259.4 34.3 %collective-permute-start.33 = (bf16[384,128]{1,0:T(8,128)(2,1)}, bf16[384,128]{1,0:T(8,128)(2,1)}, u32[]{:S(2)}, u32[]{:S(2)}) collective-permute-start(bf16[384,128]{1,0:T(8,128)(2,1)} %gate_two_9.1), channel_id=1, source_target_pairs={{0,9},{1,8},{2,11},{3,10},{4,13},{5,12},{6,15},{7,14},{8,1},{9,0},... | collective-permute-start | bytes 294920 | tf_op jit(solution)/shard_map/ppermute | solution.py:439
  294.3 26.1 %collective-permute-start.35 = (bf16[384,128]{1,0:T(8,128)(2,1)}, bf16[384,128]{1,0:T(8,128)(2,1)}, u32[]{:S(2)}, u32[]{:S(2)}) collective-permute-start(bf16[384,128]{1,0:T(8,128)(2,1)} %gate_two_10.1), channel_id=1, source_target_pairs={{0,10},{1,11},{2,8},{3,9},{4,14},{5,15},{6,12},{7,13},{8,2},{9,3},... | collective-permute-start | bytes 294920 | tf_op jit(solution)/shard_map/ppermute | solution.py:439
  296.6 24.6 %collective-permute-start.37 = (bf16[384,128]{1,0:T(8,128)(2,1)}, bf16[384,128]{1,0:T(8,128)(2,1)}, u32[]{:S(2)}, u32[]{:S(2)}) collective-permute-start(bf16[384,128]{1,0:T(8,128)(2,1)} %gate_two_12.1), channel_id=1, source_target_pairs={{0,12},{1,13},{2,14},{3,15},{4,8},{5,9},{6,10},{7,11},{8,4},{9,5},... | collective-permute-start | bytes 294920 | tf_op jit(solution)/shard_map/ppermute | solution.py:439
  321.2 24.2 %collective-permute-start.38 = (bf16[384,128]{1,0:T(8,128)(2,1)}, bf16[384,128]{1,0:T(8,128)(2,1)}, u32[]{:S(2)}, u32[]{:S(2)}) collective-permute-start(bf16[384,128]{1,0:T(8,128)(2,1)} %gate_two_14.1), channel_id=1, source_target_pairs={{0,14},{1,15},{2,12},{3,13},{4,10},{5,11},{6,8},{7,9},{8,6},{9,7},... | collective-permute-start | bytes 294920 | tf_op jit(solution)/shard_map/ppermute | solution.py:439
  324.1 22.0 %collective-permute-start.41 = (bf16[384,128]{1,0:T(8,128)(2,1)}, bf16[384,128]{1,0:T(8,128)(2,1)}, u32[]{:S(2)}, u32[]{:S(2)}) collective-permute-start(bf16[384,128]{1,0:T(8,128)(2,1)} %gate_two_13.1), channel_id=1, source_target_pairs={{0,13},{1,12},{2,15},{3,14},{4,9},{5,8},{6,11},{7,10},{8,5},{9,4},... | collective-permute-start | bytes 294920 | tf_op jit(solution)/shard_map/ppermute | solution.py:439
  346.2 25.5 %collective-permute-start.42 = (bf16[384,128]{1,0:T(8,128)(2,1)}, bf16[384,128]{1,0:T(8,128)(2,1)}, u32[]{:S(2)}, u32[]{:S(2)}) collective-permute-start(bf16[384,128]{1,0:T(8,128)(2,1)} %gate_two_11.1), channel_id=1, source_target_pairs={{0,11},{1,10},{2,9},{3,8},{4,15},{5,14},{6,13},{7,12},{8,3},{9,2},... | collective-permute-start | bytes 294920 | tf_op jit(solution)/shard_map/ppermute | solution.py:439
  348.5 25.8 %collective-permute-start.45 = (bf16[384,128]{1,0:T(8,128)(2,1)}, bf16[384,128]{1,0:T(8,128)(2,1)}, u32[]{:S(2)}, u32[]{:S(2)}) collective-permute-start(bf16[384,128]{1,0:T(8,128)(2,1)} %gate_two_15.1), channel_id=1, source_target_pairs={{0,15},{1,14},{2,13},{3,12},{4,11},{5,10},{6,9},{7,8},{8,7},{9,6},... | collective-permute-start | bytes 294920 | tf_op jit(solution)/shard_map/ppermute | solution.py:439
  (227 other events, 2195.3 us)

commit v4 on v3

--- a/solution.py
+++ b/solution.py
@@ -18,6 +18,7 @@
 LANES = 128
 UBLK = 16
 TBLK = 16
+VMEM_BYTES = 64 * 2**20 - 2**16
 FLIGHT = 5
 PITCH = TBLK + 1
 
@@ -108,30 +109,8 @@
     return [[group[t].astype(jnp.float32) for group in groups] for t in range(8)]
 
 
-def history_kernel(v_ref, *refs):
-    out_ref = refs[-1]
-
-    def column(step, carry):
-        cols = pl.ds(pl.multiple_of(step * LANES, LANES), LANES)
-        for t, frame in enumerate(frames_of(v_ref, cols)):
-            out_ref[t, :, cols] = jnp.concatenate(frame, axis=0).astype(jnp.bfloat16)
-        return carry
-
-    lax.fori_loop(0, SPF // LANES, column, 0)
-
-
-def last_frames(voltages, after):
-    inputs, frames, _ = voltages.shape
-    last = frames // TAPS - 1
-    return pl.pallas_call(
-        history_kernel,
-        name="history",
-        grid=(inputs // UBLK,),
-        in_specs=[pl.BlockSpec((UBLK, TAPS, SPF), lambda i: (i, last, 0))]
-        + [pl.BlockSpec(memory_space=pl.ANY)] * len(after),
-        out_specs=pl.BlockSpec((TAPS, UBLK, SPF), lambda i: (0, i, 0)),
-        out_shape=jax.ShapeDtypeStruct((TAPS, inputs, SPF), jnp.bfloat16),
-    )(voltages, *after)
+def kept(array):
+    return pltpu.with_memory_space_constraint(array, pltpu.HBM)
 
 
 def parity_tables(parts, width):
@@ -148,7 +127,7 @@
     return tables
 
 
-def filter_step(block, sources, c_ref, even, odd):
+def filter_step(block, sources, c_ref, even, odd, last_ref):
     half = SPF // 2
     groups = UBLK // 8
     here = pl.ds(pl.multiple_of(pl.program_id(0) * UBLK, UBLK), UBLK)
@@ -183,6 +162,10 @@
                         frame.append(total)
                     totals.append(jnp.concatenate(frame, axis=0))
                 made.append(totals)
+                if last_ref is not None and part == TBLK // TAPS - 1:
+                    for t in range(TAPS):
+                        frame = jnp.concatenate(now[t], axis=0)
+                        last_ref[t, :, cols] = frame.astype(jnp.bfloat16)
             for t in range(TAPS):
                 at = part * TAPS + t
                 even[at, here, out] = (made[0][t] + made[1][t]).astype(jnp.bfloat16)
@@ -197,8 +180,9 @@
     sources, c_ref, tables = refs[:count], refs[count], refs[count + 1 : count + 3]
     earlier_ref = refs[count + 3] if block == 0 else None
     outs = refs[count + (4 if block == 0 else 3) : -4]
+    last_ref = None if block == 0 else outs[-1]
     power_ref, even, odd, turned = refs[-4:]
-    filter_step(block, sources, c_ref, even, odd)
+    filter_step(block, sources, c_ref, even, odd, last_ref)
 
     @pl.when(pl.program_id(0) == pl.num_programs(0) - 1)
     def _():
@@ -250,7 +234,7 @@
     for place in range(first - 1, first + TBLK // TAPS):
         if place < 0:
             in_specs.append(pl.BlockSpec((TAPS, UBLK, SPF), lambda i, me: (0, i, 0)))
-            operands.append(history)
+            operands.append(kept(history))
         else:
             in_specs.append(
                 pl.BlockSpec((UBLK, TAPS, SPF), lambda i, me, place=place: (i, place, 0))
@@ -261,8 +245,13 @@
         operands.append(earlier)
     for array in operands[len(in_specs) :]:
         in_specs.append(pl.BlockSpec(array.shape, lambda i, me: (0, 0)))
-    shapes = [jax.ShapeDtypeStruct(shape, jnp.bfloat16) for shape in shapes]
-    shapes.append(jax.ShapeDtypeStruct((8, BLK), jnp.float32))
+    out_shapes = [pltpu.HBM(shape, jnp.bfloat16) for shape in shapes]
+    out_specs = [pl.BlockSpec(shape, lambda i, me: (0, 0)) for shape in shapes]
+    if block == 1:
+        out_shapes.append(pltpu.HBM((TAPS, inputs, SPF), jnp.bfloat16))
+        out_specs.append(pl.BlockSpec((TAPS, UBLK, SPF), lambda i, me: (0, i, 0)))
+    out_shapes.append(jax.ShapeDtypeStruct((8, BLK), jnp.float32))
+    out_specs.append(pl.BlockSpec((8, BLK), lambda i, me: (0, 0)))
 
     def kernel(me_ref, *refs):
         front_kernel(block, parts, where, me_ref, *refs)
@@ -274,15 +263,15 @@
             num_scalar_prefetch=1,
             grid=(inputs // UBLK,),
             in_specs=in_specs,
-            out_specs=[pl.BlockSpec(shape.shape, lambda i, me: (0, 0)) for shape in shapes],
+            out_specs=out_specs,
             scratch_shapes=[
                 pltpu.VMEM((TBLK, inputs, half), jnp.bfloat16),
                 pltpu.VMEM((TBLK, inputs, half), jnp.bfloat16),
                 pltpu.VMEM((tables[0].shape[0] * PITCH + 8, BLK), jnp.float32),
             ],
         ),
-        out_shape=shapes,
-        compiler_params=pltpu.CompilerParams(vmem_limit_bytes=50 * 2**20),
+        out_shape=out_shapes,
+        compiler_params=pltpu.CompilerParams(vmem_limit_bytes=VMEM_BYTES),
     )(me, *operands)
 
 
@@ -345,12 +334,12 @@
         + [pl.BlockSpec((2 * TBLK, BLK), lambda i, me: (second + i, 0))] * parts
         + [pl.BlockSpec((TBLK, BLK), lambda i, me: (last, 0))] * parts
     )
-    operands = [me, *late, *early, *powers]
+    operands = [me, *map(kept, late), *map(kept, early), *map(kept, powers)]
     aliases = {}
     if before is not None:
         aliases[len(operands)] = 0
         operands.append(before)
-    operands += list(after)
+    operands += map(kept, after)
     in_specs += [pl.BlockSpec(memory_space=pl.ANY)] * (len(operands) - 1 - len(in_specs))
 
     def kernel(me_ref, *refs):
@@ -382,7 +371,7 @@
             jax.ShapeDtypeStruct((8, BLK), jnp.float32),
         ],
         input_output_aliases=aliases,
-        compiler_params=pltpu.CompilerParams(vmem_limit_bytes=24 * 2**20),
+        compiler_params=pltpu.CompilerParams(vmem_limit_bytes=VMEM_BYTES),
     )(*operands)
 
 
@@ -397,9 +386,10 @@
         name=name,
         in_specs=[spec] * (len(messages) + len(after)),
         out_specs=[spec] * len(messages),
-        out_shape=[jax.ShapeDtypeStruct(m.shape, m.dtype) for m in messages],
+        out_shape=[pltpu.HBM(m.shape, m.dtype) for m in messages],
         input_output_aliases={i: i for i in range(len(messages))},
-    )(*messages, *after)
+        compiler_params=pltpu.CompilerParams(vmem_limit_bytes=VMEM_BYTES),
+    )(*map(kept, messages), *map(kept, after))
 
 
 def per_device(voltages, coeffs):
@@ -457,11 +447,12 @@
         [(width * 2 * TBLK, BLK)] * parts,
         lambda s, parity, channel: (s, parity * half + channel),
     )
-    late, earlier = {0: made[0]}, made[parts]
+    late, earlier = {0: made[0]}, made[parts + 1]
+    history = passed_along(made[parts], "freq", 1)
+    log.append(history)
     ahead = FLIGHT - 1
-    send("late", made, near[:1] + far[:ahead], late)
-
-    history = passed_along(last_frames(voltages, [late[1]]), "freq", 1)
+    send("late", made, far[:ahead], late)
+
     made_early = front(
         0,
         parts,
@@ -478,7 +469,7 @@
         history,
         earlier,
     )
-    send("late", made, mixed(far[ahead:], near[1:]), late, [made_early[-1]])
+    send("late", made, mixed(far[ahead:], near), late, [made_early[-1]])
     one, two = made_early[:parts], made_early[parts : 2 * parts]
     early, rest = {0: one[0]}, {0: two[0]}
     send("one", one, mixed(far, near), early)

time: 415 us -> 297 us (0.72)
  local copies, waits for them, and re-layouts: 153 us -> 0 us
  starting transfers between devices: 87.3 us -> 121 us
    unnamed x410 -> x0, local copies, waits for them, and re-layouts: 153 us -> none
    ppermute x45, starting transfers between devices: 84.5 us -> 116 us  [send(): arrived[s] = lax.ppermute(message, axes, [(i, i ^ s) for i in range(parts)])]
    pallas_call x1 -> x0, Pallas kernels: 8.79 us -> none  [last_frames(): pl.pallas_call(history_kernel, name='history', grid=(inputs // UBLK,), in...]
    pallas_call x6, Pallas kernels: 47.5 us -> 55.9 us  [correlated(): pl.pallas_call(kernel, name=name, grid_spec=pltpu.PrefetchScalarGridSpec(...]
    pallas_call x2, Pallas kernels: 49 us -> 53.4 us  [front(): pl.pallas_call(kernel, name=f'front_{block}', grid_spec=pltpu.PrefetchSca...]
  transfers between devices with their start and end apart: 46 -> 46, of which waited for: 15 -> 15; matrix products, arithmetic and copies ran while one was open for 0% -> 0% of each run, Pallas kernels for 13% -> 22%
where the time goes in v4:
time: 297 us; the launch traced here: 295 us
  starting transfers between devices  121 us (41%)
  Pallas kernels  109 us (37%)
  waiting for transfers between devices  64.6 us (22%)
    ppermute x45, starting transfers between devices, send(): arrived[s] = lax.ppermute(message, axes, [(i, i ^ s) for i in range(parts)])  116 us
    ppermute x45, waiting for transfers between devices, send(): arrived[s] = lax.ppermute(message, axes, [(i, i ^ s) for i in range(parts)])  64.6 us
    pallas_call x6, Pallas kernels, correlated(): pl.pallas_call(kernel, name=name, grid_spec=pltpu.PrefetchScalarGridSpec(...  55.9 us
    pallas_call x2, Pallas kernels, front(): pl.pallas_call(kernel, name=f'front_{block}', grid_spec=pltpu.PrefetchSca...  53.4 us
  transfers between devices with their start and end apart: 46, of which 15 were waited for; matrix products, arithmetic and copies ran while one was open for 0% of the time, Pallas kernels for 22%

profile of v4, /device:TPU:0, one launch (start us, length us, event | category | flops | bytes accessed | tf_op | source)
XLA Modules:
  0.0 294.9 jit_solution(4233561834881302285)
XLA Ops:
  0.0 27.5 %front_1.1 = (bf16[1024,128]{1,0:T(8,128)(2,1)}, bf16[1024,128]{1,0:T(8,128)(2,1)}, bf16[1024,128]{1,0:T(8,128)(2,1)}, bf16[1024,128]{1,0:T(8,128)(2,1)}, bf16[1...) custom-call(s32[1]{0:T(128)} %bitcast.me_ref, ...), custom_call_target="tpu_custom_call" | custom-call | tf_op jit(solution)/shard_map/front_1/pallas_call | solution.py:259
  27.5 4.3 %collective-permute-start = (bf16[8,128,2048]{2,1,0:T(8,128)(2,1)}, bf16[8,128,2048]{2,1,0:T(8,128)(2,1)}, u32[]{:S(2)}, u32[]{:S(2)}) collective-permute-start(bf16[8,128,2048]{2,1,0:T(8,128)(2,1)} %get-tuple-element.69), channel_id=1, source_target_pairs={{0,1},{2,3},{4,5},{6,7},{8,9},{10,11},{12,13},{14,15},{16,17},{18,... | collective-permute-start | bytes 12582920 | tf_op jit(solution)/shard_map/ppermute | solution.py:29
  39.0 25.9 %front_0.1 = (bf16[656,128]{1,0:T(8,128)(2,1)}, bf16[656,128]{1,0:T(8,128)(2,1)}, bf16[656,128]{1,0:T(8,128)(2,1)}, bf16[656,128]{1,0:T(8,128)(2,1)}, bf16[656,1...) custom-call(s32[1]{0:T(128)} %bitcast.me_ref, ...), custom_call_target="tpu_custom_call" | custom-call | tf_op jit(solution)/shard_map/front_0/pallas_call | solution.py:259
  69.1 14.2 %collective-permute-done.9.refs_2_.refs_9_ = bf16[1024,128]{1,0:T(8,128)(2,1)} collective-permute-done((bf16[1024,128]{1,0:T(8,128)(2,1)}, bf16[1024,128]{1,0:T(8,128)(2,1)}, u32[]{:S(2)}, u32[]{:S(2)}) %collective-permute-start.9) | collective-permute-done | bytes 262176 | tf_op jit(solution)/shard_map/ppermute | solution.py:429
  83.6 5.1 %collective-permute-start.13 = (bf16[1024,128]{1,0:T(8,128)(2,1)}, bf16[1024,128]{1,0:T(8,128)(2,1)}, u32[]{:S(2)}, u32[]{:S(2)}) collective-permute-start(bf16[1024,128]{1,0:T(8,128)(2,1)} %gate_late_15.1), channel_id=1, source_target_pairs={{0,15},{1,14},{2,13},{3,12},{4,11},{5,10},{6,9},{7,8},{8,7},{9,6},... | collective-permute-start | bytes 786440 | tf_op jit(solution)/shard_map/ppermute | solution.py:429
  88.7 20.5 %collective-permute-done.3.refs_2_.refs_10_ = bf16[1024,128]{1,0:T(8,128)(2,1)} collective-permute-done((bf16[1024,128]{1,0:T(8,128)(2,1)}, bf16[1024,128]{1,0:T(8,128)(2,1)}, u32[]{:S(2)}, u32[]{:S(2)}) %collective-permute-start.3) | collective-permute-done | bytes 262176 | tf_op jit(solution)/shard_map/ppermute | solution.py:429
  109.7 5.7 %collective-permute-start.8 = (bf16[1024,128]{1,0:T(8,128)(2,1)}, bf16[1024,128]{1,0:T(8,128)(2,1)}, u32[]{:S(2)}, u32[]{:S(2)}) collective-permute-start(bf16[1024,128]{1,0:T(8,128)(2,1)} %gate_late_4.1), channel_id=1, source_target_pairs={{0,4},{1,5},{2,6},{3,7},{4,0},{5,1},{6,2},{7,3},{8,12},{9,13},{10,... | collective-permute-start | bytes 786440 | tf_op jit(solution)/shard_map/ppermute | solution.py:429
  118.7 7.0 %collective-permute-start.14 = (bf16[1024,128]{1,0:T(8,128)(2,1)}, bf16[1024,128]{1,0:T(8,128)(2,1)}, u32[]{:S(2)}, u32[]{:S(2)}) collective-permute-start(bf16[1024,128]{1,0:T(8,128)(2,1)} %gate_late_6.1), channel_id=1, source_target_pairs={{0,6},{1,7},{2,4},{3,5},{4,2},{5,3},{6,0},{7,1},{8,14},{9,15},{10,... | collective-permute-start | bytes 786440 | tf_op jit(solution)/shard_map/ppermute | solution.py:429
  125.7 5.1 %collective-permute-start.17 = (bf16[656,128]{1,0:T(8,128)(2,1)}, bf16[656,128]{1,0:T(8,128)(2,1)}, u32[]{:S(2)}, u32[]{:S(2)}) collective-permute-start(bf16[656,128]{1,0:T(8,128)(2,1)} %gate_one_8.1), channel_id=1, source_target_pairs={{0,8},{1,9},{2,10},{3,11},{4,12},{5,13},{6,14},{7,15},{8,0},{9,1},... | collective-permute-start | bytes 503816 | tf_op jit(solution)/shard_map/ppermute | solution.py:429
  130.7 13.6 %collective-permute-start.21 = (bf16[656,128]{1,0:T(8,128)(2,1)}, bf16[656,128]{1,0:T(8,128)(2,1)}, u32[]{:S(2)}, u32[]{:S(2)}) collective-permute-start(bf16[656,128]{1,0:T(8,128)(2,1)} %gate_one_12.1), channel_id=1, source_target_pairs={{0,12},{1,13},{2,14},{3,15},{4,8},{5,9},{6,10},{7,11},{8,4},{9,5},... | collective-permute-start | bytes 503816 | tf_op jit(solution)/shard_map/ppermute | solution.py:429
  146.9 6.5 %collective-permute-done.21.refs_1_.refs_28_.refs_44_ = bf16[656,128]{1,0:T(8,128)(2,1)} collective-permute-done((bf16[656,128]{1,0:T(8,128)(2,1)}, bf16[656,128]{1,0:T(8,128)(2,1)}, u32[]{:S(2)}, u32[]{:S(2)}) %collective-permute-start.21) | collective-permute-done | bytes 167968 | tf_op jit(solution)/shard_map/ppermute | solution.py:429
  153.4 10.8 %collective-permute-start.22 = (bf16[656,128]{1,0:T(8,128)(2,1)}, bf16[656,128]{1,0:T(8,128)(2,1)}, u32[]{:S(2)}, u32[]{:S(2)}) collective-permute-start(bf16[656,128]{1,0:T(8,128)(2,1)} %gate_one_10.1), channel_id=1, source_target_pairs={{0,10},{1,11},{2,8},{3,9},{4,14},{5,15},{6,12},{7,13},{8,2},{9,3},... | collective-permute-start | bytes 503816 | tf_op jit(solution)/shard_map/ppermute | solution.py:429
  171.2 11.7 %collective-permute-start.30 = (bf16[656,128]{1,0:T(8,128)(2,1)}, bf16[656,128]{1,0:T(8,128)(2,1)}, u32[]{:S(2)}, u32[]{:S(2)}) collective-permute-start(bf16[656,128]{1,0:T(8,128)(2,1)} %gate_one_15.1), channel_id=1, source_target_pairs={{0,15},{1,14},{2,13},{3,12},{4,11},{5,10},{6,9},{7,8},{8,7},{9,6},... | collective-permute-start | bytes 503816 | tf_op jit(solution)/shard_map/ppermute | solution.py:429
  183.5 6.3 %collective-permute-start.25 = (bf16[656,128]{1,0:T(8,128)(2,1)}, bf16[656,128]{1,0:T(8,128)(2,1)}, u32[]{:S(2)}, u32[]{:S(2)}) collective-permute-start(bf16[656,128]{1,0:T(8,128)(2,1)} %gate_one_5.1), channel_id=1, source_target_pairs={{0,5},{1,4},{2,7},{3,6},{4,1},{5,0},{6,3},{7,2},{8,13},{9,12},{10,... | collective-permute-start | bytes 503816 | tf_op jit(solution)/shard_map/ppermute | solution.py:429
  189.8 3.8 %collective-permute-start.26 = (bf16[656,128]{1,0:T(8,128)(2,1)}, bf16[656,128]{1,0:T(8,128)(2,1)}, u32[]{:S(2)}, u32[]{:S(2)}) collective-permute-start(bf16[656,128]{1,0:T(8,128)(2,1)} %gate_one_6.1), channel_id=1, source_target_pairs={{0,6},{1,7},{2,4},{3,5},{4,2},{5,3},{6,0},{7,1},{8,14},{9,15},{10,... | collective-permute-start | bytes 503816 | tf_op jit(solution)/shard_map/ppermute | solution.py:429
  193.6 5.1 %collective-permute-start.31 = (bf16[384,128]{1,0:T(8,128)(2,1)}, bf16[384,128]{1,0:T(8,128)(2,1)}, u32[]{:S(2)}, u32[]{:S(2)}) collective-permute-start(bf16[384,128]{1,0:T(8,128)(2,1)} %gate_two_8.1), channel_id=1, source_target_pairs={{0,8},{1,9},{2,10},{3,11},{4,12},{5,13},{6,14},{7,15},{8,0},{9,1},... | collective-permute-start | bytes 294920 | tf_op jit(solution)/shard_map/ppermute | solution.py:429
  198.8 5.3 %collective-permute-done.25.refs_21_.refs_37_.refs_1_ = bf16[656,128]{1,0:T(8,128)(2,1)} collective-permute-done((bf16[656,128]{1,0:T(8,128)(2,1)}, bf16[656,128]{1,0:T(8,128)(2,1)}, u32[]{:S(2)}, u32[]{:S(2)}) %collective-permute-start.25) | collective-permute-done | bytes 167968 | tf_op jit(solution)/shard_map/ppermute | solution.py:429
  205.4 7.6 %correlate_0_0.1 = (bf16[32,2,36,128,128]{4,3,2,1,0:T(8,128)(2,1)}, f32[8,128]{1,0:T(8,128)}) custom-call(s32[1]{0:T(128)} %bitcast.me_ref, bf16[1024,128]{1,0:T(8,128)(2,1)} %get-tuple-element.67.refs_0_, bf16[1024,128]{1,0:T(8,128)(2,1)} %collective-permute-done.2.refs_2_.refs_1_, bf16[1024,128]{1,0:T(8,128)(2,1)} %collective-permute-done.4.refs_2_, ...), custom_call_target="tpu_custom_call" | custom-call | tf_op jit(solution)/shard_map/correlate_0_0/pallas_call | solution.py:348
  214.4 3.9 %collective-permute-start.33 = (bf16[384,128]{1,0:T(8,128)(2,1)}, bf16[384,128]{1,0:T(8,128)(2,1)}, u32[]{:S(2)}, u32[]{:S(2)}) collective-permute-start(bf16[384,128]{1,0:T(8,128)(2,1)} %gate_two_9.1), channel_id=1, source_target_pairs={{0,9},{1,8},{2,11},{3,10},{4,13},{5,12},{6,15},{7,14},{8,1},{9,0},... | collective-permute-start | bytes 294920 | tf_op jit(solution)/shard_map/ppermute | solution.py:429
  218.3 7.6 %correlate_0_4.1 = (bf16[32,2,36,128,128]{4,3,2,1,0:T(8,128)(2,1)}, f32[8,128]{1,0:T(8,128)}) custom-call(s32[1]{0:T(128)} %bitcast.me_ref, bf16[1024,128]{1,0:T(8,128)(2,1)} %get-tuple-element.67.refs_0_, bf16[1024,128]{1,0:T(8,128)(2,1)} %collective-permute-done.2.refs_2_.refs_1_, ...), custom_call_target="tpu_custom_call", output_to_operand_aliasing={{0}: (49, {})} | custom-call | tf_op jit(solution)/shard_map/correlate_0_4/pallas_call | solution.py:348
  232.4 7.6 %correlate_0_8.1 = (bf16[32,2,36,128,128]{4,3,2,1,0:T(8,128)(2,1)}, f32[8,128]{1,0:T(8,128)}) custom-call(s32[1]{0:T(128)} %bitcast.me_ref, bf16[1024,128]{1,0:T(8,128)(2,1)} %get-tuple-element.67.refs_0_, bf16[1024,128]{1,0:T(8,128)(2,1)} %collective-permute-done.2.refs_2_.refs_1_, ...), custom_call_target="tpu_custom_call", output_to_operand_aliasing={{0}: (49, {})} | custom-call | tf_op jit(solution)/shard_map/correlate_0_8/pallas_call | solution.py:348
  245.2 7.6 %correlate_0_12.1 = (bf16[32,2,36,128,128]{4,3,2,1,0:T(8,128)(2,1)}, f32[8,128]{1,0:T(8,128)}) custom-call(s32[1]{0:T(128)} %bitcast.me_ref, bf16[1024,128]{1,0:T(8,128)(2,1)} %get-tuple-element.67.refs_0_, bf16[1024,128]{1,0:T(8,128)(2,1)} %collective-permute-done.2.refs_2_.refs_1_, ...), custom_call_target="tpu_custom_call", output_to_operand_aliasing={{0}: (49, {})} | custom-call | tf_op jit(solution)/shard_map/correlate_0_12/pallas_call | solution.py:348
  259.6 7.6 %correlate_1_0.1 = (bf16[32,2,36,128,128]{4,3,2,1,0:T(8,128)(2,1)}, f32[8,128]{1,0:T(8,128)}) custom-call(s32[1]{0:T(128)} %bitcast.me_ref, bf16[1024,128]{1,0:T(8,128)(2,1)} %get-tuple-element.67.refs_0_, bf16[1024,128]{1,0:T(8,128)(2,1)} %collective-permute-done.2.refs_2_.refs_1_, ...), custom_call_target="tpu_custom_call", output_to_operand_aliasing={{0}: (49, {})} | custom-call | tf_op jit(solution)/shard_map/correlate_1_0/pallas_call | solution.py:348
  276.9 17.8 %correlate_rest.1 = (bf16[32,2,36,128,128]{4,3,2,1,0:T(8,128)(2,1)}, f32[8,128]{1,0:T(8,128)}) custom-call(s32[1]{0:T(128)} %bitcast.me_ref, bf16[1024,128]{1,0:T(8,128)(2,1)} %get-tuple-element.67.refs_0_, bf16[1024,128]{1,0:T(8,128)(2,1)} %collective-permute-done.2.refs_2_.refs_1_, ...), custom_call_target="tpu_custom_call", output_to_operand_aliasing={{0}: (49, {})} | custom-call | tf_op jit(solution)/shard_map/correlate_rest/pallas_call | solution.py:348
  (117 shorter events, 56.5 us)
Async XLA Ops:
  31.9 35.9 %collective-permute-start.5 = (bf16[1024,128]{1,0:T(8,128)(2,1)}, bf16[1024,128]{1,0:T(8,128)(2,1)}, u32[]{:S(2)}, u32[]{:S(2)}) collective-permute-start(bf16[1024,128]{1,0:T(8,128)(2,1)} %get-tuple-element.77), channel_id=1, source_target_pairs={{0,8},{1,9},{2,10},{3,11},{4,12},{5,13},{6,14},{7,15},{8,0},{9,1},... | collective-permute-start | bytes 786440 | tf_op jit(solution)/shard_map/ppermute | solution.py:429
  35.3 33.8 %collective-permute-start.1 = (bf16[1024,128]{1,0:T(8,128)(2,1)}, bf16[1024,128]{1,0:T(8,128)(2,1)}, u32[]{:S(2)}, u32[]{:S(2)}) collective-permute-start(bf16[1024,128]{1,0:T(8,128)(2,1)} %get-tuple-element.72), channel_id=1, source_target_pairs={{0,12},{1,13},{2,14},{3,15},{4,8},{5,9},{6,10},{7,11},{8,4},{9,5},... | collective-permute-start | bytes 786440 | tf_op jit(solution)/shard_map/ppermute | solution.py:429
  36.6 46.6 %collective-permute-start.9 = (bf16[1024,128]{1,0:T(8,128)(2,1)}, bf16[1024,128]{1,0:T(8,128)(2,1)}, u32[]{:S(2)}, u32[]{:S(2)}) collective-permute-start(bf16[1024,128]{1,0:T(8,128)(2,1)} %get-tuple-element.81), channel_id=1, source_target_pairs={{0,9},{1,8},{2,11},{3,10},{4,13},{5,12},{6,15},{7,14},{8,1},{9,0},... | collective-permute-start | bytes 786440 | tf_op jit(solution)/shard_map/ppermute | solution.py:429
  36.6 46.9 %collective-permute-start.12 = (bf16[1024,128]{1,0:T(8,128)(2,1)}, bf16[1024,128]{1,0:T(8,128)(2,1)}, u32[]{:S(2)}, u32[]{:S(2)}) collective-permute-start(bf16[1024,128]{1,0:T(8,128)(2,1)} %get-tuple-element.84), channel_id=1, source_target_pairs={{0,13},{1,12},{2,15},{3,14},{4,9},{5,8},{6,11},{7,10},{8,5},{9,4},... | collective-permute-start | bytes 786440 | tf_op jit(solution)/shard_map/ppermute | solution.py:429
  64.8 44.3 %collective-permute-start.3 = (bf16[1024,128]{1,0:T(8,128)(2,1)}, bf16[1024,128]{1,0:T(8,128)(2,1)}, u32[]{:S(2)}, u32[]{:S(2)}) collective-permute-start(bf16[1024,128]{1,0:T(8,128)(2,1)} %gate_late_10.1), channel_id=1, source_target_pairs={{0,10},{1,11},{2,8},{3,9},{4,14},{5,15},{6,12},{7,13},{8,2},{9,3},... | collective-permute-start | bytes 786440 | tf_op jit(solution)/shard_map/ppermute | solution.py:429
  67.8 41.9 %collective-permute-start.6 = (bf16[1024,128]{1,0:T(8,128)(2,1)}, bf16[1024,128]{1,0:T(8,128)(2,1)}, u32[]{:S(2)}, u32[]{:S(2)}) collective-permute-start(bf16[1024,128]{1,0:T(8,128)(2,1)} %gate_late_14.1), channel_id=1, source_target_pairs={{0,14},{1,15},{2,12},{3,13},{4,10},{5,11},{6,8},{7,9},{8,6},{9,7},... | collective-permute-start | bytes 786440 | tf_op jit(solution)/shard_map/ppermute | solution.py:429
  69.1 40.6 %collective-permute-start.2 = (bf16[1024,128]{1,0:T(8,128)(2,1)}, bf16[1024,128]{1,0:T(8,128)(2,1)}, u32[]{:S(2)}, u32[]{:S(2)}) collective-permute-start(bf16[1024,128]{1,0:T(8,128)(2,1)} %gate_late_1.1), channel_id=1, source_target_pairs={{0,1},{1,0},{2,3},{3,2},{4,5},{5,4},{6,7},{7,6},{8,9},{9,8},{10,11... | collective-permute-start | bytes 786440 | tf_op jit(solution)/shard_map/ppermute | solution.py:429
  83.3 35.0 %collective-permute-start.10 = (bf16[1024,128]{1,0:T(8,128)(2,1)}, bf16[1024,128]{1,0:T(8,128)(2,1)}, u32[]{:S(2)}, u32[]{:S(2)}) collective-permute-start(bf16[1024,128]{1,0:T(8,128)(2,1)} %gate_late_11.1), channel_id=1, source_target_pairs={{0,11},{1,10},{2,9},{3,8},{4,15},{5,14},{6,13},{7,12},{8,3},{9,2},... | collective-permute-start | bytes 786440 | tf_op jit(solution)/shard_map/ppermute | solution.py:429
  83.6 35.1 %collective-permute-start.13 = (bf16[1024,128]{1,0:T(8,128)(2,1)}, bf16[1024,128]{1,0:T(8,128)(2,1)}, u32[]{:S(2)}, u32[]{:S(2)}) collective-permute-start(bf16[1024,128]{1,0:T(8,128)(2,1)} %gate_late_15.1), channel_id=1, source_target_pairs={{0,15},{1,14},{2,13},{3,12},{4,11},{5,10},{6,9},{7,8},{8,7},{9,6},... | collective-permute-start | bytes 786440 | tf_op jit(solution)/shard_map/ppermute | solution.py:429
  109.7 21.1 %collective-permute-start.8 = (bf16[1024,128]{1,0:T(8,128)(2,1)}, bf16[1024,128]{1,0:T(8,128)(2,1)}, u32[]{:S(2)}, u32[]{:S(2)}) collective-permute-start(bf16[1024,128]{1,0:T(8,128)(2,1)} %gate_late_4.1), channel_id=1, source_target_pairs={{0,4},{1,5},{2,6},{3,7},{4,0},{5,1},{6,2},{7,3},{8,12},{9,13},{10,... | collective-permute-start | bytes 786440 | tf_op jit(solution)/shard_map/ppermute | solution.py:429
  118.2 26.1 %collective-permute-start.11 = (bf16[1024,128]{1,0:T(8,128)(2,1)}, bf16[1024,128]{1,0:T(8,128)(2,1)}, u32[]{:S(2)}, u32[]{:S(2)}) collective-permute-start(bf16[1024,128]{1,0:T(8,128)(2,1)} %gate_late_5.1), channel_id=1, source_target_pairs={{0,5},{1,4},{2,7},{3,6},{4,1},{5,0},{6,3},{7,2},{8,13},{9,12},{10,... | collective-permute-start | bytes 786440 | tf_op jit(solution)/shard_map/ppermute | solution.py:429
  118.7 25.6 %collective-permute-start.14 = (bf16[1024,128]{1,0:T(8,128)(2,1)}, bf16[1024,128]{1,0:T(8,128)(2,1)}, u32[]{:S(2)}, u32[]{:S(2)}) collective-permute-start(bf16[1024,128]{1,0:T(8,128)(2,1)} %gate_late_6.1), channel_id=1, source_target_pairs={{0,6},{1,7},{2,4},{3,5},{4,2},{5,3},{6,0},{7,1},{8,14},{9,15},{10,... | collective-permute-start | bytes 786440 | tf_op jit(solution)/shard_map/ppermute | solution.py:429
  125.7 21.0 %collective-permute-start.15 = (bf16[1024,128]{1,0:T(8,128)(2,1)}, bf16[1024,128]{1,0:T(8,128)(2,1)}, u32[]{:S(2)}, u32[]{:S(2)}) collective-permute-start(bf16[1024,128]{1,0:T(8,128)(2,1)} %gate_late_7.1), channel_id=1, source_target_pairs={{0,7},{1,6},{2,5},{3,4},{4,3},{5,2},{6,1},{7,0},{8,15},{9,14},{10,... | collective-permute-start | bytes 786440 | tf_op jit(solution)/shard_map/ppermute | solution.py:429
  125.7 21.2 %collective-permute-start.17 = (bf16[656,128]{1,0:T(8,128)(2,1)}, bf16[656,128]{1,0:T(8,128)(2,1)}, u32[]{:S(2)}, u32[]{:S(2)}) collective-permute-start(bf16[656,128]{1,0:T(8,128)(2,1)} %gate_one_8.1), channel_id=1, source_target_pairs={{0,8},{1,9},{2,10},{3,11},{4,12},{5,13},{6,14},{7,15},{8,0},{9,1},... | collective-permute-start | bytes 503816 | tf_op jit(solution)/shard_map/ppermute | solution.py:429
  130.7 22.7 %collective-permute-start.21 = (bf16[656,128]{1,0:T(8,128)(2,1)}, bf16[656,128]{1,0:T(8,128)(2,1)}, u32[]{:S(2)}, u32[]{:S(2)}) collective-permute-start(bf16[656,128]{1,0:T(8,128)(2,1)} %gate_one_12.1), channel_id=1, source_target_pairs={{0,12},{1,13},{2,14},{3,15},{4,8},{5,9},{6,10},{7,11},{8,4},{9,5},... | collective-permute-start | bytes 503816 | tf_op jit(solution)/shard_map/ppermute | solution.py:429
  144.3 19.8 %collective-permute-start.16 = (bf16[656,128]{1,0:T(8,128)(2,1)}, bf16[656,128]{1,0:T(8,128)(2,1)}, u32[]{:S(2)}, u32[]{:S(2)}) collective-permute-start(bf16[656,128]{1,0:T(8,128)(2,1)} %gate_one_1.1), channel_id=1, source_target_pairs={{0,1},{1,0},{2,3},{3,2},{4,5},{5,4},{6,7},{7,6},{8,9},{9,8},{10,11... | collective-permute-start | bytes 503816 | tf_op jit(solution)/shard_map/ppermute | solution.py:429
  144.3 24.9 %collective-permute-start.19 = (bf16[656,128]{1,0:T(8,128)(2,1)}, bf16[656,128]{1,0:T(8,128)(2,1)}, u32[]{:S(2)}, u32[]{:S(2)}) collective-permute-start(bf16[656,128]{1,0:T(8,128)(2,1)} %gate_one_9.1), channel_id=1, source_target_pairs={{0,9},{1,8},{2,11},{3,10},{4,13},{5,12},{6,15},{7,14},{8,1},{9,0},... | collective-permute-start | bytes 503816 | tf_op jit(solution)/shard_map/ppermute | solution.py:429
  146.7 22.6 %collective-permute-start.27 = (bf16[656,128]{1,0:T(8,128)(2,1)}, bf16[656,128]{1,0:T(8,128)(2,1)}, u32[]{:S(2)}, u32[]{:S(2)}) collective-permute-start(bf16[656,128]{1,0:T(8,128)(2,1)} %gate_one_13.1), channel_id=1, source_target_pairs={{0,13},{1,12},{2,15},{3,14},{4,9},{5,8},{6,11},{7,10},{8,5},{9,4},... | collective-permute-start | bytes 503816 | tf_op jit(solution)/shard_map/ppermute | solution.py:429
  146.9 24.3 %collective-permute-start.18 = (bf16[656,128]{1,0:T(8,128)(2,1)}, bf16[656,128]{1,0:T(8,128)(2,1)}, u32[]{:S(2)}, u32[]{:S(2)}) collective-permute-start(bf16[656,128]{1,0:T(8,128)(2,1)} %gate_one_2.1), channel_id=1, source_target_pairs={{0,2},{1,3},{2,0},{3,1},{4,6},{5,7},{6,4},{7,5},{8,10},{9,11},{10,... | collective-permute-start | bytes 503816 | tf_op jit(solution)/shard_map/ppermute | solution.py:429
  153.4 29.5 %collective-permute-start.22 = (bf16[656,128]{1,0:T(8,128)(2,1)}, bf16[656,128]{1,0:T(8,128)(2,1)}, u32[]{:S(2)}, u32[]{:S(2)}) collective-permute-start(bf16[656,128]{1,0:T(8,128)(2,1)} %gate_one_10.1), channel_id=1, source_target_pairs={{0,10},{1,11},{2,8},{3,9},{4,14},{5,15},{6,12},{7,13},{8,2},{9,3},... | collective-permute-start | bytes 503816 | tf_op jit(solution)/shard_map/ppermute | solution.py:429
  169.2 20.6 %collective-permute-start.20 = (bf16[656,128]{1,0:T(8,128)(2,1)}, bf16[656,128]{1,0:T(8,128)(2,1)}, u32[]{:S(2)}, u32[]{:S(2)}) collective-permute-start(bf16[656,128]{1,0:T(8,128)(2,1)} %gate_one_3.1), channel_id=1, source_target_pairs={{0,3},{1,2},{2,1},{3,0},{4,7},{5,6},{6,5},{7,4},{8,11},{9,10},{10,... | collective-permute-start | bytes 503816 | tf_op jit(solution)/shard_map/ppermute | solution.py:429
  169.3 24.3 %collective-permute-start.28 = (bf16[656,128]{1,0:T(8,128)(2,1)}, bf16[656,128]{1,0:T(8,128)(2,1)}, u32[]{:S(2)}, u32[]{:S(2)}) collective-permute-start(bf16[656,128]{1,0:T(8,128)(2,1)} %gate_one_11.1), channel_id=1, source_target_pairs={{0,11},{1,10},{2,9},{3,8},{4,15},{5,14},{6,13},{7,12},{8,3},{9,2},... | collective-permute-start | bytes 503816 | tf_op jit(solution)/shard_map/ppermute | solution.py:429
  171.2 22.4 %collective-permute-start.30 = (bf16[656,128]{1,0:T(8,128)(2,1)}, bf16[656,128]{1,0:T(8,128)(2,1)}, u32[]{:S(2)}, u32[]{:S(2)}) collective-permute-start(bf16[656,128]{1,0:T(8,128)(2,1)} %gate_one_15.1), channel_id=1, source_target_pairs={{0,15},{1,14},{2,13},{3,12},{4,11},{5,10},{6,9},{7,8},{8,7},{9,6},... | collective-permute-start | bytes 503816 | tf_op jit(solution)/shard_map/ppermute | solution.py:429
  183.5 20.5 %collective-permute-start.25 = (bf16[656,128]{1,0:T(8,128)(2,1)}, bf16[656,128]{1,0:T(8,128)(2,1)}, u32[]{:S(2)}, u32[]{:S(2)}) collective-permute-start(bf16[656,128]{1,0:T(8,128)(2,1)} %gate_one_5.1), channel_id=1, source_target_pairs={{0,5},{1,4},{2,7},{3,6},{4,1},{5,0},{6,3},{7,2},{8,13},{9,12},{10,... | collective-permute-start | bytes 503816 | tf_op jit(solution)/shard_map/ppermute | solution.py:429
  (22 other events, 253.0 us)

commit v5 on v4

--- a/solution.py
+++ b/solution.py
@@ -322,7 +322,7 @@
                 out_ref[0, part, pair] = (piece * gain).astype(jnp.bfloat16)
 
 
-def correlated(name, me, late, early, powers, spot, count, place, width, before, after=()):
+def correlated(name, me, late, early, powers, spot, count, width, before, after=()):
     parts = len(late)
     blocks = INPUTS // BLK
     pairs = blocks * (blocks + 1) // 2
@@ -354,7 +354,14 @@
             in_specs=in_specs,
             out_specs=[
                 pl.BlockSpec(
-                    (1, 2, pairs, BLK, BLK), lambda i, me: (place + 2 * i, 0, 0, 0, 0)
+                    (1, 2, pairs, BLK, BLK),
+                    lambda i, me: (
+                        2 * lax.rem(first + i, width // 2) + lax.div(first + i, width // 2),
+                        0,
+                        0,
+                        0,
+                        0,
+                    ),
                 ),
                 pl.BlockSpec((8, BLK), lambda i, me: (0, 0)),
             ],
@@ -413,29 +420,23 @@
     me = lax.axis_index("inp") * freq_count + lax.axis_index("freq")
     me = me.astype(jnp.int32).reshape(1)
     half = width // 2
-    extra = half // 4
     tables = parity_tables(parts, width)
+    sizes = [width * 7 // 16, width * 5 // 16, width // 4]
+    starts = [0, sizes[0], sizes[0] + sizes[1]]
 
     far, near = list(range(parts // 2, parts)), list(range(1, parts // 2))
     far = [s for pair in zip(far[: parts // 4], far[parts // 4 :]) for s in pair]
-    log = []
-
-    def send(name, messages, order, arrived, after=()):
-        for s in order:
-            waits = list(after) + (log[-FLIGHT:][:1] if len(log) >= FLIGHT else [])
-            message = messages[s]
-            if waits:
-                (message,) = gated(f"gate_{name}_{s}", [message], waits)
-            arrived[s] = lax.ppermute(message, axes, [(i, i ^ s) for i in range(parts)])
-            log.append(arrived[s])
-
-    def mixed(some_far, some_near):
-        out = []
-        while some_far or some_near:
-            out += some_far[:2] + some_near[:1] if some_far else some_near
-            some_near = some_near[1:] if some_far else []
-            some_far = some_far[2:]
-        return out
+    near = near[parts // 4 - 1 :] + near[: parts // 4 - 1]
+    log, passed = [], []
+
+    def send(chunk, s, after=()):
+        waits = list(after) + (log[-FLIGHT:][:1] if len(log) >= FLIGHT else [])
+        message = messages[chunk][s]
+        if waits:
+            (message,) = gated(f"gate_{chunk}_{s}", [message], waits + passed)
+            passed[:] = [message]
+        arrived[chunk][s] = lax.ppermute(message, axes, [(i, i ^ s) for i in range(parts)])
+        log.append(arrived[chunk][s])
 
     made = front(
         1,
@@ -447,63 +448,88 @@
         [(width * 2 * TBLK, BLK)] * parts,
         lambda s, parity, channel: (s, parity * half + channel),
     )
-    late, earlier = {0: made[0]}, made[parts + 1]
-    history = passed_along(made[parts], "freq", 1)
+    messages, arrived = [made[:parts]], [{0: made[0]}]
+    history, earlier = made[parts], made[parts + 1]
+    history = passed_along(history, "freq", 1)
     log.append(history)
-    ahead = FLIGHT - 1
-    send("late", made, far[:ahead], late)
-
-    made_early = front(
+    for s in far[: FLIGHT - 1]:
+        send(0, s)
+
+    def where(s, parity, channel):
+        place = parity * half + channel
+        chunk = max(i for i in range(len(starts)) if starts[i] <= place)
+        return chunk * parts + s, place - starts[chunk]
+
+    shapes = [(size * 2 * TBLK + (TBLK if i == 0 else 0), BLK) for i, size in enumerate(sizes)]
+    made = front(
         0,
         parts,
         me,
         voltages,
         coeffs,
         tables,
-        [((half + extra) * 2 * TBLK + TBLK, BLK)] * parts + [((half - extra) * 2 * TBLK, BLK)] * parts,
-        lambda s, parity, channel: (
-            (s, parity * half + channel)
-            if parity == 0 or channel < extra
-            else (parts + s, channel - extra)
-        ),
+        [shape for shape in shapes for _ in range(parts)],
+        where,
         history,
         earlier,
     )
-    send("late", made, mixed(far[ahead:], near), late, [made_early[-1]])
-    one, two = made_early[:parts], made_early[parts : 2 * parts]
-    early, rest = {0: one[0]}, {0: two[0]}
-    send("one", one, mixed(far, near), early)
-
-    def every(found):
-        return [found[s] for s in range(parts)]
-
-    send("two", two, far[:FLIGHT], rest)
-    late, early = every(late), every(early)
-    left_far, left_near = far[FLIGHT:], list(near)
-    out, after = None, []
-    pieces = [(parity, i) for parity, size in ((0, half), (1, extra)) for i in range(0, size, extra)]
-    for parity, i in pieces:
-        spot = (parity * half + i, parity * half + i)
-        out, token = correlated(
-            f"correlate_{parity}_{i}", me, late, early, early, spot, extra, 2 * i + parity, width, out, after
-        )
-        final = (parity, i) == pieces[-1]
-        now = left_near if final else left_near[:1]
-        send("two", two, now + left_far[: len(left_far) if final else 1], rest, [token])
-        after = [rest[now[0]]] if now else []
-        left_near, left_far = left_near[1:], left_far[1:]
-    out, _ = correlated(
-        "correlate_rest",
-        me,
-        late,
-        every(rest),
-        early,
-        (half + extra, 0),
-        half - extra,
-        2 * extra + 1,
-        width,
-        out,
-    )
+    for i in range(len(sizes)):
+        messages.append(made[i * parts : (i + 1) * parts])
+        arrived.append({0: made[i * parts]})
+    done = [made[-1]]
+
+    far_left = [(0, s) for s in far[FLIGHT - 1 :]] + [(1, s) for s in far]
+    near_left = [(0, s) for s in near] + [(1, s) for s in near]
+    lead = len(near_left) - len(far_left)
+    while far_left or near_left:
+        take = [near_left.pop(0)] if near_left else []
+        if lead > 0 and near_left and len(far_left) % 4 == 0:
+            take.append(near_left.pop(0))
+            lead -= 1
+        if far_left:
+            take.append(far_left.pop(0))
+        for chunk, s in take:
+            send(chunk, s, done)
+
+    def every(chunk):
+        return [arrived[chunk][s] for s in range(parts)]
+
+    out, token = None, done[0]
+    for chunk in range(1, len(sizes) + 1):
+        size, start = sizes[chunk - 1], starts[chunk - 1]
+        if chunk == len(sizes):
+            pieces = [size]
+        else:
+            pieces = [size - size // 2, size // 2]
+            far_left, near_left = list(far), near[parts // 4 :] + near[: parts // 4]
+            for s in far_left[: FLIGHT - 1]:
+                send(chunk + 1, s, [token])
+            far_left = far_left[FLIGHT - 1 :]
+        after = []
+        for index, count in enumerate(pieces):
+            first = sum(pieces[:index])
+            out, token = correlated(
+                f"correlate_{chunk}_{index}",
+                me,
+                every(0),
+                every(chunk),
+                every(1),
+                (start + first, first),
+                count,
+                width,
+                out,
+                after,
+            )
+            if chunk == len(sizes):
+                break
+            final = index == len(pieces) - 1
+            first_near = near_left[0]
+            for turn in range(len(near_left) if final else 3):
+                if near_left:
+                    send(chunk + 1, near_left.pop(0), [token])
+                if far_left and turn < (len(near) if final else 2):
+                    send(chunk + 1, far_left.pop(0), [token])
+            after = [arrived[chunk + 1][first_near]]
     return out
 
 

time: 297 us -> 276 us (0.929)
  waiting for transfers between devices: 64.6 us -> 52.1 us
  starting transfers between devices: 121 us -> 114 us
    ppermute x45 -> x60, waiting for transfers between devices: 64.6 us -> 52.1 us  [send(): lax.ppermute(message, axes, [(i, i ^ s) for i in range(parts)])]
    ppermute x45 -> x60, starting transfers between devices: 116 us -> 109 us  [send(): lax.ppermute(message, axes, [(i, i ^ s) for i in range(parts)])]
    pallas_call x6 -> x5, Pallas kernels: 55.9 us -> 53.7 us  [correlated(): pl.pallas_call(kernel, name=name, grid_spec=pltpu.PrefetchScalarGridSpec(...]
  transfers between devices with their start and end apart: 46 -> 61, of which waited for: 15 -> 18; matrix products, arithmetic and copies ran while one was open for 0% -> 0% of each run, Pallas kernels for 22% -> 25%
where the time goes in v5:
time: 276 us; the launch traced here: 273 us
  starting transfers between devices  114 us (41%)
  Pallas kernels  107 us (39%)
  waiting for transfers between devices  52.1 us (19%)
    ppermute x60, starting transfers between devices, send(): lax.ppermute(message, axes, [(i, i ^ s) for i in range(parts)])  109 us
    pallas_call x5, Pallas kernels, correlated(): pl.pallas_call(kernel, name=name, grid_spec=pltpu.PrefetchScalarGridSpec(...  53.7 us
    pallas_call x2, Pallas kernels, front(): pl.pallas_call(kernel, name=f'front_{block}', grid_spec=pltpu.PrefetchSca...  53.5 us
    ppermute x60, waiting for transfers between devices, send(): lax.ppermute(message, axes, [(i, i ^ s) for i in range(parts)])  52.1 us
  transfers between devices with their start and end apart: 61, of which 18 were waited for; matrix products, arithmetic and copies ran while one was open for 0% of the time, Pallas kernels for 25%

profile of v5, /device:TPU:0, one launch (start us, length us, event | category | flops | bytes accessed | tf_op | source)
XLA Modules:
  0.0 273.4 jit_solution(11081162807960989965)
XLA Ops:
  0.0 27.5 %front_1.1 = (bf16[1024,128]{1,0:T(8,128)(2,1)}, bf16[1024,128]{1,0:T(8,128)(2,1)}, bf16[1024,128]{1,0:T(8,128)(2,1)}, bf16[1024,128]{1,0:T(8,128)(2,1)}, bf16[1...) custom-call(s32[1]{0:T(128)} %bitcast.me_ref, ...), custom_call_target="tpu_custom_call" | custom-call | tf_op jit(solution)/shard_map/front_1/pallas_call | solution.py:259
  27.5 4.3 %collective-permute-start = (bf16[8,128,2048]{2,1,0:T(8,128)(2,1)}, bf16[8,128,2048]{2,1,0:T(8,128)(2,1)}, u32[]{:S(2)}, u32[]{:S(2)}) collective-permute-start(bf16[8,128,2048]{2,1,0:T(8,128)(2,1)} %get-tuple-element.83), channel_id=1, source_target_pairs={{0,1},{2,3},{4,5},{6,7},{8,9},{10,11},{12,13},{14,15},{16,17},{18,... | collective-permute-start | bytes 12582920 | tf_op jit(solution)/shard_map/ppermute | solution.py:29
  31.9 3.4 %collective-permute-start.2 = (bf16[1024,128]{1,0:T(8,128)(2,1)}, bf16[1024,128]{1,0:T(8,128)(2,1)}, u32[]{:S(2)}, u32[]{:S(2)}) collective-permute-start(bf16[1024,128]{1,0:T(8,128)(2,1)} %get-tuple-element.89), channel_id=1, source_target_pairs={{0,8},{1,9},{2,10},{3,11},{4,12},{5,13},{6,14},{7,15},{8,0},{9,1},... | collective-permute-start | bytes 786440 | tf_op jit(solution)/shard_map/ppermute | solution.py:438
  39.0 26.0 %front_0.1 = (bf16[464,128]{1,0:T(8,128)(2,1)}, bf16[464,128]{1,0:T(8,128)(2,1)}, bf16[464,128]{1,0:T(8,128)(2,1)}, bf16[464,128]{1,0:T(8,128)(2,1)}, bf16[464,1...) custom-call(s32[1]{0:T(128)} %bitcast.me_ref, ...), custom_call_target="tpu_custom_call" | custom-call | tf_op jit(solution)/shard_map/front_0/pallas_call | solution.py:259
  66.6 4.8 %collective-permute-start.3 = (bf16[1024,128]{1,0:T(8,128)(2,1)}, bf16[1024,128]{1,0:T(8,128)(2,1)}, u32[]{:S(2)}, u32[]{:S(2)}) collective-permute-start(bf16[1024,128]{1,0:T(8,128)(2,1)} %gate_0_10.1.refs_3_), channel_id=1, source_target_pairs={{0,10},{1,11},{2,8},{3,9},{4,14},{5,15},{6,12},{7,13},{8,2},{9,3},... | collective-permute-start | bytes 786440 | tf_op jit(solution)/shard_map/ppermute | solution.py:438
  79.8 8.4 %collective-permute-start.12 = (bf16[1024,128]{1,0:T(8,128)(2,1)}, bf16[1024,128]{1,0:T(8,128)(2,1)}, u32[]{:S(2)}, u32[]{:S(2)}) collective-permute-start(bf16[1024,128]{1,0:T(8,128)(2,1)} %gate_0_7.1.refs_3_), channel_id=1, source_target_pairs={{0,7},{1,6},{2,5},{3,4},{4,3},{5,2},{6,1},{7,0},{8,15},{9,14},{10,... | collective-permute-start | bytes 786440 | tf_op jit(solution)/shard_map/ppermute | solution.py:438
  88.2 5.2 %collective-permute-done.3.refs_2_.refs_10_ = bf16[1024,128]{1,0:T(8,128)(2,1)} collective-permute-done((bf16[1024,128]{1,0:T(8,128)(2,1)}, bf16[1024,128]{1,0:T(8,128)(2,1)}, u32[]{:S(2)}, u32[]{:S(2)}) %collective-permute-start.3) | collective-permute-done | bytes 262176 | tf_op jit(solution)/shard_map/ppermute | solution.py:438
  93.5 8.9 %collective-permute-done.10.refs_2_.refs_6_ = bf16[1024,128]{1,0:T(8,128)(2,1)} collective-permute-done((bf16[1024,128]{1,0:T(8,128)(2,1)}, bf16[1024,128]{1,0:T(8,128)(2,1)}, u32[]{:S(2)}, u32[]{:S(2)}) %collective-permute-start.10) | collective-permute-done | bytes 262176 | tf_op jit(solution)/shard_map/ppermute | solution.py:438
  105.9 5.2 %collective-permute-done.12.refs_2_.refs_7_ = bf16[1024,128]{1,0:T(8,128)(2,1)} collective-permute-done((bf16[1024,128]{1,0:T(8,128)(2,1)}, bf16[1024,128]{1,0:T(8,128)(2,1)}, u32[]{:S(2)}, u32[]{:S(2)}) %collective-permute-start.12) | collective-permute-done | bytes 262176 | tf_op jit(solution)/shard_map/ppermute | solution.py:438
  111.7 7.6 %collective-permute-done.14.refs_2_.refs_11_ = bf16[1024,128]{1,0:T(8,128)(2,1)} collective-permute-done((bf16[1024,128]{1,0:T(8,128)(2,1)}, bf16[1024,128]{1,0:T(8,128)(2,1)}, u32[]{:S(2)}, u32[]{:S(2)}) %collective-permute-start.14) | collective-permute-done | bytes 262176 | tf_op jit(solution)/shard_map/ppermute | solution.py:438
  121.8 5.7 %collective-permute-start.19 = (bf16[464,128]{1,0:T(8,128)(2,1)}, bf16[464,128]{1,0:T(8,128)(2,1)}, u32[]{:S(2)}, u32[]{:S(2)}) collective-permute-start(bf16[464,128]{1,0:T(8,128)(2,1)} %gate_1_4.1.refs_3_), channel_id=1, source_target_pairs={{0,4},{1,5},{2,6},{3,7},{4,0},{5,1},{6,2},{7,3},{8,12},{9,13},{10,... | collective-permute-start | bytes 356360 | tf_op jit(solution)/shard_map/ppermute | solution.py:438
  127.4 9.2 %collective-permute-start.17 = (bf16[464,128]{1,0:T(8,128)(2,1)}, bf16[464,128]{1,0:T(8,128)(2,1)}, u32[]{:S(2)}, u32[]{:S(2)}) collective-permute-start(bf16[464,128]{1,0:T(8,128)(2,1)} %gate_1_5.1.refs_3_), channel_id=1, source_target_pairs={{0,5},{1,4},{2,7},{3,6},{4,1},{5,0},{6,3},{7,2},{8,13},{9,12},{10,... | collective-permute-start | bytes 356360 | tf_op jit(solution)/shard_map/ppermute | solution.py:438
  141.6 3.4 %collective-permute-start.25 = (bf16[464,128]{1,0:T(8,128)(2,1)}, bf16[464,128]{1,0:T(8,128)(2,1)}, u32[]{:S(2)}, u32[]{:S(2)}) collective-permute-start(bf16[464,128]{1,0:T(8,128)(2,1)} %gate_1_10.1.refs_3_), channel_id=1, source_target_pairs={{0,10},{1,11},{2,8},{3,9},{4,14},{5,15},{6,12},{7,13},{8,2},{9,3},... | collective-permute-start | bytes 356360 | tf_op jit(solution)/shard_map/ppermute | solution.py:438
  147.0 4.6 %collective-permute-done.23.refs_2_.refs_22_.refs_38_ = bf16[464,128]{1,0:T(8,128)(2,1)} collective-permute-done((bf16[464,128]{1,0:T(8,128)(2,1)}, bf16[464,128]{1,0:T(8,128)(2,1)}, u32[]{:S(2)}, u32[]{:S(2)}) %collective-permute-start.23) | collective-permute-done | bytes 118816 | tf_op jit(solution)/shard_map/ppermute | solution.py:438
  153.6 3.7 %collective-permute-done.25.refs_2_.refs_26_.refs_42_ = bf16[464,128]{1,0:T(8,128)(2,1)} collective-permute-done((bf16[464,128]{1,0:T(8,128)(2,1)}, bf16[464,128]{1,0:T(8,128)(2,1)}, u32[]{:S(2)}, u32[]{:S(2)}) %collective-permute-start.25) | collective-permute-done | bytes 118816 | tf_op jit(solution)/shard_map/ppermute | solution.py:438
  157.4 5.4 %collective-permute-start.27 = (bf16[464,128]{1,0:T(8,128)(2,1)}, bf16[464,128]{1,0:T(8,128)(2,1)}, u32[]{:S(2)}, u32[]{:S(2)}) collective-permute-start(bf16[464,128]{1,0:T(8,128)(2,1)} %gate_1_3.1.refs_3_), channel_id=1, source_target_pairs={{0,3},{1,2},{2,1},{3,0},{4,7},{5,6},{6,5},{7,4},{8,11},{9,10},{10,... | collective-permute-start | bytes 356360 | tf_op jit(solution)/shard_map/ppermute | solution.py:438
  172.2 11.5 %correlate_1_0.1 = (bf16[32,2,36,128,128]{4,3,2,1,0:T(8,128)(2,1)}, f32[8,128]{1,0:T(8,128)}) custom-call(s32[1]{0:T(128)} %bitcast.me_ref, bf16[1024,128]{1,0:T(8,128)(2,1)} %get-tuple-element.81.refs_0_, bf16[1024,128]{1,0:T(8,128)(2,1)} %collective-permute-done.8.refs_2_.refs_1_, bf16[1024,128]{1,0:T(8,128)(2,1)} %collective-permute-done.11.refs_2_, ...), custom_call_target="tpu_custom_call" | custom-call | tf_op jit(solution)/shard_map/correlate_1_0/pallas_call | solution.py:348
  183.9 8.8 %collective-permute-start.39 = (bf16[320,128]{1,0:T(8,128)(2,1)}, bf16[320,128]{1,0:T(8,128)(2,1)}, u32[]{:S(2)}, u32[]{:S(2)}) collective-permute-start(bf16[320,128]{1,0:T(8,128)(2,1)} %gate_2_10.1.refs_3_), channel_id=1, source_target_pairs={{0,10},{1,11},{2,8},{3,9},{4,14},{5,15},{6,12},{7,13},{8,2},{9,3},... | collective-permute-start | bytes 245768 | tf_op jit(solution)/shard_map/ppermute | solution.py:438
  196.1 11.6 %correlate_1_1.1 = (bf16[32,2,36,128,128]{4,3,2,1,0:T(8,128)(2,1)}, f32[8,128]{1,0:T(8,128)}) custom-call(s32[1]{0:T(128)} %bitcast.me_ref, bf16[1024,128]{1,0:T(8,128)(2,1)} %get-tuple-element.81.refs_0_, bf16[1024,128]{1,0:T(8,128)(2,1)} %collective-permute-done.8.refs_2_.refs_1_, ...), custom_call_target="tpu_custom_call", output_to_operand_aliasing={{0}: (49, {})} | custom-call | tf_op jit(solution)/shard_map/correlate_1_1/pallas_call | solution.py:348
  207.8 3.3 %collective-permute-start.44 = (bf16[320,128]{1,0:T(8,128)(2,1)}, bf16[320,128]{1,0:T(8,128)(2,1)}, u32[]{:S(2)}, u32[]{:S(2)}) collective-permute-start(bf16[320,128]{1,0:T(8,128)(2,1)} %gate_2_11.1.refs_3_), channel_id=1, source_target_pairs={{0,11},{1,10},{2,9},{3,8},{4,15},{5,14},{6,13},{7,12},{8,3},{9,2},... | collective-permute-start | bytes 245768 | tf_op jit(solution)/shard_map/ppermute | solution.py:438
  223.3 9.0 %correlate_2_0.1 = (bf16[32,2,36,128,128]{4,3,2,1,0:T(8,128)(2,1)}, f32[8,128]{1,0:T(8,128)}) custom-call(s32[1]{0:T(128)} %bitcast.me_ref, bf16[1024,128]{1,0:T(8,128)(2,1)} %get-tuple-element.81.refs_0_, bf16[1024,128]{1,0:T(8,128)(2,1)} %collective-permute-done.8.refs_2_.refs_1_, ...), custom_call_target="tpu_custom_call", output_to_operand_aliasing={{0}: (49, {})} | custom-call | tf_op jit(solution)/shard_map/correlate_2_0/pallas_call | solution.py:348
  237.8 8.9 %correlate_2_1.1 = (bf16[32,2,36,128,128]{4,3,2,1,0:T(8,128)(2,1)}, f32[8,128]{1,0:T(8,128)}) custom-call(s32[1]{0:T(128)} %bitcast.me_ref, bf16[1024,128]{1,0:T(8,128)(2,1)} %get-tuple-element.81.refs_0_, bf16[1024,128]{1,0:T(8,128)(2,1)} %collective-permute-done.8.refs_2_.refs_1_, ...), custom_call_target="tpu_custom_call", output_to_operand_aliasing={{0}: (49, {})} | custom-call | tf_op jit(solution)/shard_map/correlate_2_1/pallas_call | solution.py:348
  255.2 4.6 %collective-permute-done.57.refs_22_ = bf16[256,128]{1,0:T(8,128)(2,1)} collective-permute-done((bf16[256,128]{1,0:T(8,128)(2,1)}, bf16[256,128]{1,0:T(8,128)(2,1)}, u32[]{:S(2)}, u32[]{:S(2)}) %collective-permute-start.57) | collective-permute-done | bytes 65568 | tf_op jit(solution)/shard_map/ppermute | solution.py:438
  260.6 12.7 %correlate_3_0.1 = (bf16[32,2,36,128,128]{4,3,2,1,0:T(8,128)(2,1)}, f32[8,128]{1,0:T(8,128)}) custom-call(s32[1]{0:T(128)} %bitcast.me_ref, bf16[1024,128]{1,0:T(8,128)(2,1)} %get-tuple-element.81.refs_0_, bf16[1024,128]{1,0:T(8,128)(2,1)} %collective-permute-done.8.refs_2_.refs_1_, ...), custom_call_target="tpu_custom_call", output_to_operand_aliasing={{0}: (49, {})} | custom-call | tf_op jit(solution)/shard_map/correlate_3_0/pallas_call | solution.py:348
  (161 shorter events, 69.1 us)
Async XLA Ops:
  31.9 34.0 %collective-permute-start.2 = (bf16[1024,128]{1,0:T(8,128)(2,1)}, bf16[1024,128]{1,0:T(8,128)(2,1)}, u32[]{:S(2)}, u32[]{:S(2)}) collective-permute-start(bf16[1024,128]{1,0:T(8,128)(2,1)} %get-tuple-element.89), channel_id=1, source_target_pairs={{0,8},{1,9},{2,10},{3,11},{4,12},{5,13},{6,14},{7,15},{8,0},{9,1},... | collective-permute-start | bytes 786440 | tf_op jit(solution)/shard_map/ppermute | solution.py:438
  35.3 31.3 %collective-permute-start.1 = (bf16[1024,128]{1,0:T(8,128)(2,1)}, bf16[1024,128]{1,0:T(8,128)(2,1)}, u32[]{:S(2)}, u32[]{:S(2)}) collective-permute-start(bf16[1024,128]{1,0:T(8,128)(2,1)} %get-tuple-element.87), channel_id=1, source_target_pairs={{0,12},{1,13},{2,14},{3,15},{4,8},{5,9},{6,10},{7,11},{8,4},{9,5},... | collective-permute-start | bytes 786440 | tf_op jit(solution)/shard_map/ppermute | solution.py:438
  36.6 35.7 %collective-permute-start.7 = (bf16[1024,128]{1,0:T(8,128)(2,1)}, bf16[1024,128]{1,0:T(8,128)(2,1)}, u32[]{:S(2)}, u32[]{:S(2)}) collective-permute-start(bf16[1024,128]{1,0:T(8,128)(2,1)} %get-tuple-element.96), channel_id=1, source_target_pairs={{0,9},{1,8},{2,11},{3,10},{4,13},{5,12},{6,15},{7,14},{8,1},{9,0},... | collective-permute-start | bytes 786440 | tf_op jit(solution)/shard_map/ppermute | solution.py:438
  36.6 38.6 %collective-permute-start.6 = (bf16[1024,128]{1,0:T(8,128)(2,1)}, bf16[1024,128]{1,0:T(8,128)(2,1)}, u32[]{:S(2)}, u32[]{:S(2)}) collective-permute-start(bf16[1024,128]{1,0:T(8,128)(2,1)} %get-tuple-element.94), channel_id=1, source_target_pairs={{0,13},{1,12},{2,15},{3,14},{4,9},{5,8},{6,11},{7,10},{8,5},{9,4},... | collective-permute-start | bytes 786440 | tf_op jit(solution)/shard_map/ppermute | solution.py:438
  65.9 22.3 %collective-permute-start.4 = (bf16[1024,128]{1,0:T(8,128)(2,1)}, bf16[1024,128]{1,0:T(8,128)(2,1)}, u32[]{:S(2)}, u32[]{:S(2)}) collective-permute-start(bf16[1024,128]{1,0:T(8,128)(2,1)} %gate_0_5.1.refs_3_), channel_id=1, source_target_pairs={{0,5},{1,4},{2,7},{3,6},{4,1},{5,0},{6,3},{7,2},{8,13},{9,12},{10,... | collective-permute-start | bytes 786440 | tf_op jit(solution)/shard_map/ppermute | solution.py:438
  66.6 26.8 %collective-permute-start.3 = (bf16[1024,128]{1,0:T(8,128)(2,1)}, bf16[1024,128]{1,0:T(8,128)(2,1)}, u32[]{:S(2)}, u32[]{:S(2)}) collective-permute-start(bf16[1024,128]{1,0:T(8,128)(2,1)} %gate_0_10.1.refs_3_), channel_id=1, source_target_pairs={{0,10},{1,11},{2,8},{3,9},{4,14},{5,15},{6,12},{7,13},{8,2},{9,3},... | collective-permute-start | bytes 786440 | tf_op jit(solution)/shard_map/ppermute | solution.py:438
  72.3 30.1 %collective-permute-start.10 = (bf16[1024,128]{1,0:T(8,128)(2,1)}, bf16[1024,128]{1,0:T(8,128)(2,1)}, u32[]{:S(2)}, u32[]{:S(2)}) collective-permute-start(bf16[1024,128]{1,0:T(8,128)(2,1)} %gate_0_6.1.refs_3_), channel_id=1, source_target_pairs={{0,6},{1,7},{2,4},{3,5},{4,2},{5,3},{6,0},{7,1},{8,14},{9,15},{10,... | collective-permute-start | bytes 786440 | tf_op jit(solution)/shard_map/ppermute | solution.py:438
  75.2 29.1 %collective-permute-start.9 = (bf16[1024,128]{1,0:T(8,128)(2,1)}, bf16[1024,128]{1,0:T(8,128)(2,1)}, u32[]{:S(2)}, u32[]{:S(2)}) collective-permute-start(bf16[1024,128]{1,0:T(8,128)(2,1)} %gate_0_14.1.refs_3_), channel_id=1, source_target_pairs={{0,14},{1,15},{2,12},{3,13},{4,10},{5,11},{6,8},{7,9},{8,6},{9,7},... | collective-permute-start | bytes 786440 | tf_op jit(solution)/shard_map/ppermute | solution.py:438
  79.8 31.3 %collective-permute-start.12 = (bf16[1024,128]{1,0:T(8,128)(2,1)}, bf16[1024,128]{1,0:T(8,128)(2,1)}, u32[]{:S(2)}, u32[]{:S(2)}) collective-permute-start(bf16[1024,128]{1,0:T(8,128)(2,1)} %gate_0_7.1.refs_3_), channel_id=1, source_target_pairs={{0,7},{1,6},{2,5},{3,4},{4,3},{5,2},{6,1},{7,0},{8,15},{9,14},{10,... | collective-permute-start | bytes 786440 | tf_op jit(solution)/shard_map/ppermute | solution.py:438
  88.2 31.1 %collective-permute-start.14 = (bf16[1024,128]{1,0:T(8,128)(2,1)}, bf16[1024,128]{1,0:T(8,128)(2,1)}, u32[]{:S(2)}, u32[]{:S(2)}) collective-permute-start(bf16[1024,128]{1,0:T(8,128)(2,1)} %gate_0_11.1.refs_3_), channel_id=1, source_target_pairs={{0,11},{1,10},{2,9},{3,8},{4,15},{5,14},{6,13},{7,12},{8,3},{9,2},... | collective-permute-start | bytes 786440 | tf_op jit(solution)/shard_map/ppermute | solution.py:438
  93.5 28.3 %collective-permute-start.8 = (bf16[1024,128]{1,0:T(8,128)(2,1)}, bf16[1024,128]{1,0:T(8,128)(2,1)}, u32[]{:S(2)}, u32[]{:S(2)}) collective-permute-start(bf16[1024,128]{1,0:T(8,128)(2,1)} %gate_0_1.1.refs_3_), channel_id=1, source_target_pairs={{0,1},{1,0},{2,3},{3,2},{4,5},{5,4},{6,7},{7,6},{8,9},{9,8},{10,11... | collective-permute-start | bytes 786440 | tf_op jit(solution)/shard_map/ppermute | solution.py:438
  102.4 25.0 %collective-permute-start.15 = (bf16[1024,128]{1,0:T(8,128)(2,1)}, bf16[1024,128]{1,0:T(8,128)(2,1)}, u32[]{:S(2)}, u32[]{:S(2)}) collective-permute-start(bf16[1024,128]{1,0:T(8,128)(2,1)} %gate_0_15.1.refs_3_), channel_id=1, source_target_pairs={{0,15},{1,14},{2,13},{3,12},{4,11},{5,10},{6,9},{7,8},{8,7},{9,6},... | collective-permute-start | bytes 786440 | tf_op jit(solution)/shard_map/ppermute | solution.py:438
  104.4 23.1 %collective-permute-start.11 = (bf16[1024,128]{1,0:T(8,128)(2,1)}, bf16[1024,128]{1,0:T(8,128)(2,1)}, u32[]{:S(2)}, u32[]{:S(2)}) collective-permute-start(bf16[1024,128]{1,0:T(8,128)(2,1)} %gate_0_2.1.refs_3_), channel_id=1, source_target_pairs={{0,2},{1,3},{2,0},{3,1},{4,6},{5,7},{6,4},{7,5},{8,10},{9,11},{10,... | collective-permute-start | bytes 786440 | tf_op jit(solution)/shard_map/ppermute | solution.py:438
  111.1 25.6 %collective-permute-start.13 = (bf16[1024,128]{1,0:T(8,128)(2,1)}, bf16[1024,128]{1,0:T(8,128)(2,1)}, u32[]{:S(2)}, u32[]{:S(2)}) collective-permute-start(bf16[1024,128]{1,0:T(8,128)(2,1)} %gate_0_3.1.refs_3_), channel_id=1, source_target_pairs={{0,3},{1,2},{2,1},{3,0},{4,7},{5,6},{6,5},{7,4},{8,11},{9,10},{10,... | collective-permute-start | bytes 786440 | tf_op jit(solution)/shard_map/ppermute | solution.py:438
  119.3 20.6 %collective-permute-start.20 = (bf16[464,128]{1,0:T(8,128)(2,1)}, bf16[464,128]{1,0:T(8,128)(2,1)}, u32[]{:S(2)}, u32[]{:S(2)}) collective-permute-start(bf16[464,128]{1,0:T(8,128)(2,1)} %gate_1_8.1.refs_3_), channel_id=1, source_target_pairs={{0,8},{1,9},{2,10},{3,11},{4,12},{5,13},{6,14},{7,15},{8,0},{9,1},... | collective-permute-start | bytes 356360 | tf_op jit(solution)/shard_map/ppermute | solution.py:438
  121.8 18.1 %collective-permute-start.19 = (bf16[464,128]{1,0:T(8,128)(2,1)}, bf16[464,128]{1,0:T(8,128)(2,1)}, u32[]{:S(2)}, u32[]{:S(2)}) collective-permute-start(bf16[464,128]{1,0:T(8,128)(2,1)} %gate_1_4.1.refs_3_), channel_id=1, source_target_pairs={{0,4},{1,5},{2,6},{3,7},{4,0},{5,1},{6,2},{7,3},{8,12},{9,13},{10,... | collective-permute-start | bytes 356360 | tf_op jit(solution)/shard_map/ppermute | solution.py:438
  164.4 19.5 %collective-permute-start.33 = (bf16[320,128]{1,0:T(8,128)(2,1)}, bf16[320,128]{1,0:T(8,128)(2,1)}, u32[]{:S(2)}, u32[]{:S(2)}) collective-permute-start(bf16[320,128]{1,0:T(8,128)(2,1)} %gate_2_8.1.refs_3_), channel_id=1, source_target_pairs={{0,8},{1,9},{2,10},{3,11},{4,12},{5,13},{6,14},{7,15},{8,0},{9,1},... | collective-permute-start | bytes 245768 | tf_op jit(solution)/shard_map/ppermute | solution.py:438
  164.9 27.9 %collective-permute-start.32 = (bf16[320,128]{1,0:T(8,128)(2,1)}, bf16[320,128]{1,0:T(8,128)(2,1)}, u32[]{:S(2)}, u32[]{:S(2)}) collective-permute-start(bf16[320,128]{1,0:T(8,128)(2,1)} %gate_2_12.1.refs_3_), channel_id=1, source_target_pairs={{0,12},{1,13},{2,14},{3,15},{4,8},{5,9},{6,10},{7,11},{8,4},{9,5},... | collective-permute-start | bytes 245768 | tf_op jit(solution)/shard_map/ppermute | solution.py:438
  166.8 26.0 %collective-permute-start.36 = (bf16[320,128]{1,0:T(8,128)(2,1)}, bf16[320,128]{1,0:T(8,128)(2,1)}, u32[]{:S(2)}, u32[]{:S(2)}) collective-permute-start(bf16[320,128]{1,0:T(8,128)(2,1)} %gate_2_9.1.refs_3_), channel_id=1, source_target_pairs={{0,9},{1,8},{2,11},{3,10},{4,13},{5,12},{6,15},{7,14},{8,1},{9,0},... | collective-permute-start | bytes 245768 | tf_op jit(solution)/shard_map/ppermute | solution.py:438
  171.0 25.0 %collective-permute-start.35 = (bf16[320,128]{1,0:T(8,128)(2,1)}, bf16[320,128]{1,0:T(8,128)(2,1)}, u32[]{:S(2)}, u32[]{:S(2)}) collective-permute-start(bf16[320,128]{1,0:T(8,128)(2,1)} %gate_2_13.1.refs_3_), channel_id=1, source_target_pairs={{0,13},{1,12},{2,15},{3,14},{4,9},{5,8},{6,11},{7,10},{8,5},{9,4},... | collective-permute-start | bytes 245768 | tf_op jit(solution)/shard_map/ppermute | solution.py:438
  183.9 23.9 %collective-permute-start.39 = (bf16[320,128]{1,0:T(8,128)(2,1)}, bf16[320,128]{1,0:T(8,128)(2,1)}, u32[]{:S(2)}, u32[]{:S(2)}) collective-permute-start(bf16[320,128]{1,0:T(8,128)(2,1)} %gate_2_10.1.refs_3_), channel_id=1, source_target_pairs={{0,10},{1,11},{2,8},{3,9},{4,14},{5,15},{6,12},{7,13},{8,2},{9,3},... | collective-permute-start | bytes 245768 | tf_op jit(solution)/shard_map/ppermute | solution.py:438
  192.7 18.4 %collective-permute-start.34 = (bf16[320,128]{1,0:T(8,128)(2,1)}, bf16[320,128]{1,0:T(8,128)(2,1)}, u32[]{:S(2)}, u32[]{:S(2)}) collective-permute-start(bf16[320,128]{1,0:T(8,128)(2,1)} %gate_2_2.1.refs_3_), channel_id=1, source_target_pairs={{0,2},{1,3},{2,0},{3,1},{4,6},{5,7},{6,4},{7,5},{8,10},{9,11},{10,... | collective-permute-start | bytes 245768 | tf_op jit(solution)/shard_map/ppermute | solution.py:438
  192.8 18.4 %collective-permute-start.41 = (bf16[320,128]{1,0:T(8,128)(2,1)}, bf16[320,128]{1,0:T(8,128)(2,1)}, u32[]{:S(2)}, u32[]{:S(2)}) collective-permute-start(bf16[320,128]{1,0:T(8,128)(2,1)} %gate_2_14.1.refs_3_), channel_id=1, source_target_pairs={{0,14},{1,15},{2,12},{3,13},{4,10},{5,11},{6,8},{7,9},{8,6},{9,7},... | collective-permute-start | bytes 245768 | tf_op jit(solution)/shard_map/ppermute | solution.py:438
  216.3 17.3 %collective-permute-start.48 = (bf16[256,128]{1,0:T(8,128)(2,1)}, bf16[256,128]{1,0:T(8,128)(2,1)}, u32[]{:S(2)}, u32[]{:S(2)}) collective-permute-start(bf16[256,128]{1,0:T(8,128)(2,1)} %gate_3_8.1.refs_3_), channel_id=1, source_target_pairs={{0,8},{1,9},{2,10},{3,11},{4,12},{5,13},{6,14},{7,15},{8,0},{9,1},... | collective-permute-start | bytes 196616 | tf_op jit(solution)/shard_map/ppermute | solution.py:438
  (37 other events, 437.2 us)

commit v6 on v5

--- a/solution.py
+++ b/solution.py
@@ -275,14 +275,32 @@
     )(me, *operands)
 
 
-def correlate_kernel(parts, me_ref, *refs):
+def correlate_kernel(parts, first, count, me_ref, *refs):
     late, early, powers = refs[:parts], refs[parts : 2 * parts], refs[2 * parts : 3 * parts]
-    out_ref, token_ref, plain, other, columns, lines, shares = refs[-7:]
+    out_ref, token_ref, plain, other, columns, lines, shares, ready, sems = refs[-9:]
     blocks = INPUTS // BLK
     freq = parts // blocks
     me = me_ref[0]
 
-    @pl.when(pl.program_id(0) == 0)
+    step = pl.program_id(0)
+    slot = lax.rem(step, 2)
+    depth = out_ref.shape[0]
+
+    def writes(step, slot):
+        channel = 2 * lax.rem(first + step, depth // 2) + lax.div(first + step, depth // 2)
+        return [
+            pltpu.make_async_copy(
+                ready.at[slot, part], out_ref.at[channel, part], sems.at[slot, part]
+            )
+            for part in range(2)
+        ]
+
+    @pl.when(step >= 2)
+    def _():
+        for write in writes(step - 2, slot):
+            write.wait()
+
+    @pl.when(step == 0)
     def _():
         token_ref[...] = jnp.zeros_like(token_ref)
         for s in range(parts):
@@ -319,7 +337,18 @@
             gain = columns[r * BLK : (r + 1) * BLK, :] * line
             for part in range(2):
                 piece = both[:, part * BLK : (part + 1) * BLK]
-                out_ref[0, part, pair] = (piece * gain).astype(jnp.bfloat16)
+                ready[slot, part, pair] = (piece * gain).astype(jnp.bfloat16)
+
+    for write in writes(step, slot):
+        write.start()
+
+    @pl.when(step == count - 1)
+    def _():
+        if count > 1:
+            for write in writes(step - 1, 1 - slot):
+                write.wait()
+        for write in writes(step, slot):
+            write.wait()
 
 
 def correlated(name, me, late, early, powers, spot, count, width, before, after=()):
@@ -343,7 +372,7 @@
     in_specs += [pl.BlockSpec(memory_space=pl.ANY)] * (len(operands) - 1 - len(in_specs))
 
     def kernel(me_ref, *refs):
-        correlate_kernel(parts, me_ref, *refs)
+        correlate_kernel(parts, first, count, me_ref, *refs)
 
     return pl.pallas_call(
         kernel,
@@ -353,16 +382,7 @@
             grid=(count,),
             in_specs=in_specs,
             out_specs=[
-                pl.BlockSpec(
-                    (1, 2, pairs, BLK, BLK),
-                    lambda i, me: (
-                        2 * lax.rem(first + i, width // 2) + lax.div(first + i, width // 2),
-                        0,
-                        0,
-                        0,
-                        0,
-                    ),
-                ),
+                pl.BlockSpec(memory_space=pl.ANY),
                 pl.BlockSpec((8, BLK), lambda i, me: (0, 0)),
             ],
             scratch_shapes=[
@@ -371,6 +391,8 @@
                 pltpu.VMEM((INPUTS, BLK), jnp.float32),
                 pltpu.VMEM((blocks, 8, BLK), jnp.float32),
                 pltpu.VMEM((parts, 8, BLK), jnp.float32),
+                pltpu.VMEM((2, 2, pairs, BLK, BLK), jnp.bfloat16),
+                pltpu.SemaphoreType.DMA((2, 2)),
             ],
         ),
         out_shape=[
@@ -421,8 +443,8 @@
     me = me.astype(jnp.int32).reshape(1)
     half = width // 2
     tables = parity_tables(parts, width)
-    sizes = [width * 7 // 16, width * 5 // 16, width // 4]
-    starts = [0, sizes[0], sizes[0] + sizes[1]]
+    sizes = [width * 7 // 16, width * 9 // 16]
+    starts = [0, sizes[0]]
 
     far, near = list(range(parts // 2, parts)), list(range(1, parts // 2))
     far = [s for pair in zip(far[: parts // 4], far[parts // 4 :]) for s in pair]

time: 276 us -> 266 us (0.964)
  starting transfers between devices: 114 us -> 96.3 us
  waiting for transfers between devices: 52.1 us -> 63.7 us
  Pallas kernels: 107 us -> 103 us
    ppermute x60 -> x45, starting transfers between devices: 109 us -> 92 us  [send(): lax.ppermute(message, axes, [(i, i ^ s) for i in range(parts)])]
    ppermute x60 -> x45, waiting for transfers between devices: 52.1 us -> 63.7 us  [send(): lax.ppermute(message, axes, [(i, i ^ s) for i in range(parts)])]
    pallas_call x5 -> x3, Pallas kernels: 53.7 us -> 49.3 us  [correlated(): pl.pallas_call(kernel, name=name, grid_spec=pltpu.PrefetchScalarGridSpec(...]
  transfers between devices with their start and end apart: 61 -> 46, of which waited for: 18 -> 16; matrix products, arithmetic and copies ran while one was open for 0% -> 0% of each run, Pallas kernels for 25% -> 19%
where the time goes in v6:
time: 266 us; the launch traced here: 263 us
  Pallas kernels  103 us (39%)
  starting transfers between devices  96.3 us (36%)
  waiting for transfers between devices  63.7 us (24%)
    ppermute x45, starting transfers between devices, send(): lax.ppermute(message, axes, [(i, i ^ s) for i in range(parts)])  92 us
    ppermute x45, waiting for transfers between devices, send(): lax.ppermute(message, axes, [(i, i ^ s) for i in range(parts)])  63.7 us
    pallas_call x2, Pallas kernels, front(): pl.pallas_call(kernel, name=f'front_{block}', grid_spec=pltpu.PrefetchSca...  53.2 us
    pallas_call x3, Pallas kernels, correlated(): pl.pallas_call(kernel, name=name, grid_spec=pltpu.PrefetchScalarGridSpec(...  49.3 us
  transfers between devices with their start and end apart: 46, of which 16 were waited for; matrix products, arithmetic and copies ran while one was open for 0% of the time, Pallas kernels for 19%

profile of v6, /device:TPU:0, one launch (start us, length us, event | category | flops | bytes accessed | tf_op | source)
XLA Modules:
  0.0 262.9 jit_solution(5285530124080965603)
XLA Ops:
  0.0 27.5 %front_1.1 = (bf16[1024,128]{1,0:T(8,128)(2,1)}, bf16[1024,128]{1,0:T(8,128)(2,1)}, bf16[1024,128]{1,0:T(8,128)(2,1)}, bf16[1024,128]{1,0:T(8,128)(2,1)}, bf16[1...) custom-call(s32[1]{0:T(128)} %bitcast.me_ref, ...), custom_call_target="tpu_custom_call" | custom-call | tf_op jit(solution)/shard_map/front_1/pallas_call | solution.py:259
  27.5 4.3 %collective-permute-start = (bf16[8,128,2048]{2,1,0:T(8,128)(2,1)}, bf16[8,128,2048]{2,1,0:T(8,128)(2,1)}, u32[]{:S(2)}, u32[]{:S(2)}) collective-permute-start(bf16[8,128,2048]{2,1,0:T(8,128)(2,1)} %get-tuple-element.63), channel_id=1, source_target_pairs={{0,1},{2,3},{4,5},{6,7},{8,9},{10,11},{12,13},{14,15},{16,17},{18,... | collective-permute-start | bytes 12582920 | tf_op jit(solution)/shard_map/ppermute | solution.py:29
  31.8 3.4 %collective-permute-start.2 = (bf16[1024,128]{1,0:T(8,128)(2,1)}, bf16[1024,128]{1,0:T(8,128)(2,1)}, u32[]{:S(2)}, u32[]{:S(2)}) collective-permute-start(bf16[1024,128]{1,0:T(8,128)(2,1)} %get-tuple-element.69), channel_id=1, source_target_pairs={{0,8},{1,9},{2,10},{3,11},{4,12},{5,13},{6,14},{7,15},{8,0},{9,1},... | collective-permute-start | bytes 786440 | tf_op jit(solution)/shard_map/ppermute | solution.py:460
  38.9 25.7 %front_0.1 = (bf16[464,128]{1,0:T(8,128)(2,1)}, bf16[464,128]{1,0:T(8,128)(2,1)}, bf16[464,128]{1,0:T(8,128)(2,1)}, bf16[464,128]{1,0:T(8,128)(2,1)}, bf16[464,1...) custom-call(s32[1]{0:T(128)} %bitcast.me_ref, ...), custom_call_target="tpu_custom_call" | custom-call | tf_op jit(solution)/shard_map/front_0/pallas_call | solution.py:259
  66.3 5.1 %collective-permute-start.3 = (bf16[1024,128]{1,0:T(8,128)(2,1)}, bf16[1024,128]{1,0:T(8,128)(2,1)}, u32[]{:S(2)}, u32[]{:S(2)}) collective-permute-start(bf16[1024,128]{1,0:T(8,128)(2,1)} %gate_0_10.1.refs_3_), channel_id=1, source_target_pairs={{0,10},{1,11},{2,8},{3,9},{4,14},{5,15},{6,12},{7,13},{8,2},{9,3},... | collective-permute-start | bytes 786440 | tf_op jit(solution)/shard_map/ppermute | solution.py:460
  79.5 8.8 %collective-permute-start.12 = (bf16[1024,128]{1,0:T(8,128)(2,1)}, bf16[1024,128]{1,0:T(8,128)(2,1)}, u32[]{:S(2)}, u32[]{:S(2)}) collective-permute-start(bf16[1024,128]{1,0:T(8,128)(2,1)} %gate_0_7.1.refs_3_), channel_id=1, source_target_pairs={{0,7},{1,6},{2,5},{3,4},{4,3},{5,2},{6,1},{7,0},{8,15},{9,14},{10,... | collective-permute-start | bytes 786440 | tf_op jit(solution)/shard_map/ppermute | solution.py:460
  88.4 8.9 %collective-permute-done.3.refs_2_.refs_10_ = bf16[1024,128]{1,0:T(8,128)(2,1)} collective-permute-done((bf16[1024,128]{1,0:T(8,128)(2,1)}, bf16[1024,128]{1,0:T(8,128)(2,1)}, u32[]{:S(2)}, u32[]{:S(2)}) %collective-permute-start.3) | collective-permute-done | bytes 262176 | tf_op jit(solution)/shard_map/ppermute | solution.py:460
  97.3 5.0 %collective-permute-done.10.refs_2_.refs_6_ = bf16[1024,128]{1,0:T(8,128)(2,1)} collective-permute-done((bf16[1024,128]{1,0:T(8,128)(2,1)}, bf16[1024,128]{1,0:T(8,128)(2,1)}, u32[]{:S(2)}, u32[]{:S(2)}) %collective-permute-start.10) | collective-permute-done | bytes 262176 | tf_op jit(solution)/shard_map/ppermute | solution.py:460
  109.0 12.8 %collective-permute-done.14.refs_2_.refs_11_ = bf16[1024,128]{1,0:T(8,128)(2,1)} collective-permute-done((bf16[1024,128]{1,0:T(8,128)(2,1)}, bf16[1024,128]{1,0:T(8,128)(2,1)}, u32[]{:S(2)}, u32[]{:S(2)}) %collective-permute-start.14) | collective-permute-done | bytes 262176 | tf_op jit(solution)/shard_map/ppermute | solution.py:460
  122.7 4.9 %collective-permute-start.19 = (bf16[464,128]{1,0:T(8,128)(2,1)}, bf16[464,128]{1,0:T(8,128)(2,1)}, u32[]{:S(2)}, u32[]{:S(2)}) collective-permute-start(bf16[464,128]{1,0:T(8,128)(2,1)} %gate_1_4.1.refs_3_), channel_id=1, source_target_pairs={{0,4},{1,5},{2,6},{3,7},{4,0},{5,1},{6,2},{7,3},{8,12},{9,13},{10,... | collective-permute-start | bytes 356360 | tf_op jit(solution)/shard_map/ppermute | solution.py:460
  127.6 9.2 %collective-permute-start.17 = (bf16[464,128]{1,0:T(8,128)(2,1)}, bf16[464,128]{1,0:T(8,128)(2,1)}, u32[]{:S(2)}, u32[]{:S(2)}) collective-permute-start(bf16[464,128]{1,0:T(8,128)(2,1)} %gate_1_5.1.refs_3_), channel_id=1, source_target_pairs={{0,5},{1,4},{2,7},{3,6},{4,1},{5,0},{6,3},{7,2},{8,13},{9,12},{10,... | collective-permute-start | bytes 356360 | tf_op jit(solution)/shard_map/ppermute | solution.py:460
  141.7 3.1 %collective-permute-start.25 = (bf16[464,128]{1,0:T(8,128)(2,1)}, bf16[464,128]{1,0:T(8,128)(2,1)}, u32[]{:S(2)}, u32[]{:S(2)}) collective-permute-start(bf16[464,128]{1,0:T(8,128)(2,1)} %gate_1_10.1.refs_3_), channel_id=1, source_target_pairs={{0,10},{1,11},{2,8},{3,9},{4,14},{5,15},{6,12},{7,13},{8,2},{9,3},... | collective-permute-start | bytes 356360 | tf_op jit(solution)/shard_map/ppermute | solution.py:460
  147.1 4.3 %collective-permute-done.23.refs_2_.refs_22_.refs_38_ = bf16[464,128]{1,0:T(8,128)(2,1)} collective-permute-done((bf16[464,128]{1,0:T(8,128)(2,1)}, bf16[464,128]{1,0:T(8,128)(2,1)}, u32[]{:S(2)}, u32[]{:S(2)}) %collective-permute-start.23) | collective-permute-done | bytes 118816 | tf_op jit(solution)/shard_map/ppermute | solution.py:460
  153.8 3.7 %collective-permute-done.25.refs_2_.refs_26_.refs_42_ = bf16[464,128]{1,0:T(8,128)(2,1)} collective-permute-done((bf16[464,128]{1,0:T(8,128)(2,1)}, bf16[464,128]{1,0:T(8,128)(2,1)}, u32[]{:S(2)}, u32[]{:S(2)}) %collective-permute-start.25) | collective-permute-done | bytes 118816 | tf_op jit(solution)/shard_map/ppermute | solution.py:460
  157.4 4.7 %collective-permute-start.27 = (bf16[464,128]{1,0:T(8,128)(2,1)}, bf16[464,128]{1,0:T(8,128)(2,1)}, u32[]{:S(2)}, u32[]{:S(2)}) collective-permute-start(bf16[464,128]{1,0:T(8,128)(2,1)} %gate_1_3.1.refs_3_), channel_id=1, source_target_pairs={{0,3},{1,2},{2,1},{3,0},{4,7},{5,6},{6,5},{7,4},{8,11},{9,10},{10,... | collective-permute-start | bytes 356360 | tf_op jit(solution)/shard_map/ppermute | solution.py:460
  172.0 11.8 %correlate_1_0.1 = (bf16[32,2,36,128,128]{4,3,2,1,0:T(8,128)(2,1)}, f32[8,128]{1,0:T(8,128)}) custom-call(s32[1]{0:T(128)} %bitcast.me_ref, bf16[1024,128]{1,0:T(8,128)(2,1)} %get-tuple-element.61.refs_0_, bf16[1024,128]{1,0:T(8,128)(2,1)} %collective-permute-done.8.refs_2_.refs_1_, bf16[1024,128]{1,0:T(8,128)(2,1)} %collective-permute-done.11.refs_2_, ...), custom_call_target="tpu_custom_call" | custom-call | tf_op jit(solution)/shard_map/correlate_1_0/pallas_call | solution.py:377
  184.4 3.8 %collective-permute-done.33.refs_2_.refs_24_ = bf16[576,128]{1,0:T(8,128)(2,1)} collective-permute-done((bf16[576,128]{1,0:T(8,128)(2,1)}, bf16[576,128]{1,0:T(8,128)(2,1)}, u32[]{:S(2)}, u32[]{:S(2)}) %collective-permute-start.33) | collective-permute-done | bytes 147488 | tf_op jit(solution)/shard_map/ppermute | solution.py:460
  188.3 10.5 %collective-permute-start.39 = (bf16[576,128]{1,0:T(8,128)(2,1)}, bf16[576,128]{1,0:T(8,128)(2,1)}, u32[]{:S(2)}, u32[]{:S(2)}) collective-permute-start(bf16[576,128]{1,0:T(8,128)(2,1)} %gate_2_10.1.refs_3_), channel_id=1, source_target_pairs={{0,10},{1,11},{2,8},{3,9},{4,14},{5,15},{6,12},{7,13},{8,2},{9,3},... | collective-permute-start | bytes 442376 | tf_op jit(solution)/shard_map/ppermute | solution.py:460
  198.8 3.3 %collective-permute-start.41 = (bf16[576,128]{1,0:T(8,128)(2,1)}, bf16[576,128]{1,0:T(8,128)(2,1)}, u32[]{:S(2)}, u32[]{:S(2)}) collective-permute-start(bf16[576,128]{1,0:T(8,128)(2,1)} %gate_2_14.1.refs_3_), channel_id=1, source_target_pairs={{0,14},{1,15},{2,12},{3,13},{4,10},{5,11},{6,8},{7,9},{8,6},{9,7},... | collective-permute-start | bytes 442376 | tf_op jit(solution)/shard_map/ppermute | solution.py:460
  202.2 12.0 %correlate_1_1.1 = (bf16[32,2,36,128,128]{4,3,2,1,0:T(8,128)(2,1)}, f32[8,128]{1,0:T(8,128)}) custom-call(s32[1]{0:T(128)} %bitcast.me_ref, bf16[1024,128]{1,0:T(8,128)(2,1)} %get-tuple-element.61.refs_0_, bf16[1024,128]{1,0:T(8,128)(2,1)} %collective-permute-done.8.refs_2_.refs_1_, ...), custom_call_target="tpu_custom_call", output_to_operand_aliasing={{0}: (49, {})} | custom-call | tf_op jit(solution)/shard_map/correlate_1_1/pallas_call | solution.py:377
  214.3 3.3 %collective-permute-start.44 = (bf16[576,128]{1,0:T(8,128)(2,1)}, bf16[576,128]{1,0:T(8,128)(2,1)}, u32[]{:S(2)}, u32[]{:S(2)}) collective-permute-start(bf16[576,128]{1,0:T(8,128)(2,1)} %gate_2_11.1.refs_3_), channel_id=1, source_target_pairs={{0,11},{1,10},{2,9},{3,8},{4,15},{5,14},{6,13},{7,12},{8,3},{9,2},... | collective-permute-start | bytes 442376 | tf_op jit(solution)/shard_map/ppermute | solution.py:460
  223.2 10.6 %collective-permute-done.42.refs_22_ = bf16[576,128]{1,0:T(8,128)(2,1)} collective-permute-done((bf16[576,128]{1,0:T(8,128)(2,1)}, bf16[576,128]{1,0:T(8,128)(2,1)}, u32[]{:S(2)}, u32[]{:S(2)}) %collective-permute-start.42) | collective-permute-done | bytes 147488 | tf_op jit(solution)/shard_map/ppermute | solution.py:460
  233.8 3.5 %collective-permute-done.43.refs_23_ = bf16[576,128]{1,0:T(8,128)(2,1)} collective-permute-done((bf16[576,128]{1,0:T(8,128)(2,1)}, bf16[576,128]{1,0:T(8,128)(2,1)}, u32[]{:S(2)}, u32[]{:S(2)}) %collective-permute-start.43) | collective-permute-done | bytes 147488 | tf_op jit(solution)/shard_map/ppermute | solution.py:460
  237.3 25.4 %correlate_2_0.1 = (bf16[32,2,36,128,128]{4,3,2,1,0:T(8,128)(2,1)}, f32[8,128]{1,0:T(8,128)}) custom-call(s32[1]{0:T(128)} %bitcast.me_ref, bf16[1024,128]{1,0:T(8,128)(2,1)} %get-tuple-element.61.refs_0_, bf16[1024,128]{1,0:T(8,128)(2,1)} %collective-permute-done.8.refs_2_.refs_1_, ...), custom_call_target="tpu_custom_call", output_to_operand_aliasing={{0}: (49, {})} | custom-call | tf_op jit(solution)/shard_map/correlate_2_0/pallas_call | solution.py:377
  (114 shorter events, 46.7 us)
Async XLA Ops:
  31.8 33.8 %collective-permute-start.2 = (bf16[1024,128]{1,0:T(8,128)(2,1)}, bf16[1024,128]{1,0:T(8,128)(2,1)}, u32[]{:S(2)}, u32[]{:S(2)}) collective-permute-start(bf16[1024,128]{1,0:T(8,128)(2,1)} %get-tuple-element.69), channel_id=1, source_target_pairs={{0,8},{1,9},{2,10},{3,11},{4,12},{5,13},{6,14},{7,15},{8,0},{9,1},... | collective-permute-start | bytes 786440 | tf_op jit(solution)/shard_map/ppermute | solution.py:460
  35.3 31.1 %collective-permute-start.1 = (bf16[1024,128]{1,0:T(8,128)(2,1)}, bf16[1024,128]{1,0:T(8,128)(2,1)}, u32[]{:S(2)}, u32[]{:S(2)}) collective-permute-start(bf16[1024,128]{1,0:T(8,128)(2,1)} %get-tuple-element.67), channel_id=1, source_target_pairs={{0,12},{1,13},{2,14},{3,15},{4,8},{5,9},{6,10},{7,11},{8,4},{9,5},... | collective-permute-start | bytes 786440 | tf_op jit(solution)/shard_map/ppermute | solution.py:460
  36.6 35.7 %collective-permute-start.7 = (bf16[1024,128]{1,0:T(8,128)(2,1)}, bf16[1024,128]{1,0:T(8,128)(2,1)}, u32[]{:S(2)}, u32[]{:S(2)}) collective-permute-start(bf16[1024,128]{1,0:T(8,128)(2,1)} %get-tuple-element.76), channel_id=1, source_target_pairs={{0,9},{1,8},{2,11},{3,10},{4,13},{5,12},{6,15},{7,14},{8,1},{9,0},... | collective-permute-start | bytes 786440 | tf_op jit(solution)/shard_map/ppermute | solution.py:460
  36.6 38.6 %collective-permute-start.6 = (bf16[1024,128]{1,0:T(8,128)(2,1)}, bf16[1024,128]{1,0:T(8,128)(2,1)}, u32[]{:S(2)}, u32[]{:S(2)}) collective-permute-start(bf16[1024,128]{1,0:T(8,128)(2,1)} %get-tuple-element.74), channel_id=1, source_target_pairs={{0,13},{1,12},{2,15},{3,14},{4,9},{5,8},{6,11},{7,10},{8,5},{9,4},... | collective-permute-start | bytes 786440 | tf_op jit(solution)/shard_map/ppermute | solution.py:460
  65.6 22.8 %collective-permute-start.4 = (bf16[1024,128]{1,0:T(8,128)(2,1)}, bf16[1024,128]{1,0:T(8,128)(2,1)}, u32[]{:S(2)}, u32[]{:S(2)}) collective-permute-start(bf16[1024,128]{1,0:T(8,128)(2,1)} %gate_0_5.1.refs_3_), channel_id=1, source_target_pairs={{0,5},{1,4},{2,7},{3,6},{4,1},{5,0},{6,3},{7,2},{8,13},{9,12},{10,... | collective-permute-start | bytes 786440 | tf_op jit(solution)/shard_map/ppermute | solution.py:460
  66.3 30.9 %collective-permute-start.3 = (bf16[1024,128]{1,0:T(8,128)(2,1)}, bf16[1024,128]{1,0:T(8,128)(2,1)}, u32[]{:S(2)}, u32[]{:S(2)}) collective-permute-start(bf16[1024,128]{1,0:T(8,128)(2,1)} %gate_0_10.1.refs_3_), channel_id=1, source_target_pairs={{0,10},{1,11},{2,8},{3,9},{4,14},{5,15},{6,12},{7,13},{8,2},{9,3},... | collective-permute-start | bytes 786440 | tf_op jit(solution)/shard_map/ppermute | solution.py:460
  72.3 30.0 %collective-permute-start.10 = (bf16[1024,128]{1,0:T(8,128)(2,1)}, bf16[1024,128]{1,0:T(8,128)(2,1)}, u32[]{:S(2)}, u32[]{:S(2)}) collective-permute-start(bf16[1024,128]{1,0:T(8,128)(2,1)} %gate_0_6.1.refs_3_), channel_id=1, source_target_pairs={{0,6},{1,7},{2,4},{3,5},{4,2},{5,3},{6,0},{7,1},{8,14},{9,15},{10,... | collective-permute-start | bytes 786440 | tf_op jit(solution)/shard_map/ppermute | solution.py:460
  75.2 28.7 %collective-permute-start.9 = (bf16[1024,128]{1,0:T(8,128)(2,1)}, bf16[1024,128]{1,0:T(8,128)(2,1)}, u32[]{:S(2)}, u32[]{:S(2)}) collective-permute-start(bf16[1024,128]{1,0:T(8,128)(2,1)} %gate_0_14.1.refs_3_), channel_id=1, source_target_pairs={{0,14},{1,15},{2,12},{3,13},{4,10},{5,11},{6,8},{7,9},{8,6},{9,7},... | collective-permute-start | bytes 786440 | tf_op jit(solution)/shard_map/ppermute | solution.py:460
  79.5 28.8 %collective-permute-start.12 = (bf16[1024,128]{1,0:T(8,128)(2,1)}, bf16[1024,128]{1,0:T(8,128)(2,1)}, u32[]{:S(2)}, u32[]{:S(2)}) collective-permute-start(bf16[1024,128]{1,0:T(8,128)(2,1)} %gate_0_7.1.refs_3_), channel_id=1, source_target_pairs={{0,7},{1,6},{2,5},{3,4},{4,3},{5,2},{6,1},{7,0},{8,15},{9,14},{10,... | collective-permute-start | bytes 786440 | tf_op jit(solution)/shard_map/ppermute | solution.py:460
  88.4 33.4 %collective-permute-start.14 = (bf16[1024,128]{1,0:T(8,128)(2,1)}, bf16[1024,128]{1,0:T(8,128)(2,1)}, u32[]{:S(2)}, u32[]{:S(2)}) collective-permute-start(bf16[1024,128]{1,0:T(8,128)(2,1)} %gate_0_11.1.refs_3_), channel_id=1, source_target_pairs={{0,11},{1,10},{2,9},{3,8},{4,15},{5,14},{6,13},{7,12},{8,3},{9,2},... | collective-permute-start | bytes 786440 | tf_op jit(solution)/shard_map/ppermute | solution.py:460
  97.3 25.4 %collective-permute-start.8 = (bf16[1024,128]{1,0:T(8,128)(2,1)}, bf16[1024,128]{1,0:T(8,128)(2,1)}, u32[]{:S(2)}, u32[]{:S(2)}) collective-permute-start(bf16[1024,128]{1,0:T(8,128)(2,1)} %gate_0_1.1.refs_3_), channel_id=1, source_target_pairs={{0,1},{1,0},{2,3},{3,2},{4,5},{5,4},{6,7},{7,6},{8,9},{9,8},{10,11... | collective-permute-start | bytes 786440 | tf_op jit(solution)/shard_map/ppermute | solution.py:460
  102.3 25.3 %collective-permute-start.15 = (bf16[1024,128]{1,0:T(8,128)(2,1)}, bf16[1024,128]{1,0:T(8,128)(2,1)}, u32[]{:S(2)}, u32[]{:S(2)}) collective-permute-start(bf16[1024,128]{1,0:T(8,128)(2,1)} %gate_0_15.1.refs_3_), channel_id=1, source_target_pairs={{0,15},{1,14},{2,13},{3,12},{4,11},{5,10},{6,9},{7,8},{8,7},{9,6},... | collective-permute-start | bytes 786440 | tf_op jit(solution)/shard_map/ppermute | solution.py:460
  103.9 23.7 %collective-permute-start.11 = (bf16[1024,128]{1,0:T(8,128)(2,1)}, bf16[1024,128]{1,0:T(8,128)(2,1)}, u32[]{:S(2)}, u32[]{:S(2)}) collective-permute-start(bf16[1024,128]{1,0:T(8,128)(2,1)} %gate_0_2.1.refs_3_), channel_id=1, source_target_pairs={{0,2},{1,3},{2,0},{3,1},{4,6},{5,7},{6,4},{7,5},{8,10},{9,11},{10,... | collective-permute-start | bytes 786440 | tf_op jit(solution)/shard_map/ppermute | solution.py:460
  108.4 28.4 %collective-permute-start.13 = (bf16[1024,128]{1,0:T(8,128)(2,1)}, bf16[1024,128]{1,0:T(8,128)(2,1)}, u32[]{:S(2)}, u32[]{:S(2)}) collective-permute-start(bf16[1024,128]{1,0:T(8,128)(2,1)} %gate_0_3.1.refs_3_), channel_id=1, source_target_pairs={{0,3},{1,2},{2,1},{3,0},{4,7},{5,6},{6,5},{7,4},{8,11},{9,10},{10,... | collective-permute-start | bytes 786440 | tf_op jit(solution)/shard_map/ppermute | solution.py:460
  121.8 17.9 %collective-permute-start.20 = (bf16[464,128]{1,0:T(8,128)(2,1)}, bf16[464,128]{1,0:T(8,128)(2,1)}, u32[]{:S(2)}, u32[]{:S(2)}) collective-permute-start(bf16[464,128]{1,0:T(8,128)(2,1)} %gate_1_8.1.refs_3_), channel_id=1, source_target_pairs={{0,8},{1,9},{2,10},{3,11},{4,12},{5,13},{6,14},{7,15},{8,0},{9,1},... | collective-permute-start | bytes 356360 | tf_op jit(solution)/shard_map/ppermute | solution.py:460
  164.5 23.7 %collective-permute-start.33 = (bf16[576,128]{1,0:T(8,128)(2,1)}, bf16[576,128]{1,0:T(8,128)(2,1)}, u32[]{:S(2)}, u32[]{:S(2)}) collective-permute-start(bf16[576,128]{1,0:T(8,128)(2,1)} %gate_2_8.1.refs_3_), channel_id=1, source_target_pairs={{0,8},{1,9},{2,10},{3,11},{4,12},{5,13},{6,14},{7,15},{8,0},{9,1},... | collective-permute-start | bytes 442376 | tf_op jit(solution)/shard_map/ppermute | solution.py:460
  165.0 33.8 %collective-permute-start.32 = (bf16[576,128]{1,0:T(8,128)(2,1)}, bf16[576,128]{1,0:T(8,128)(2,1)}, u32[]{:S(2)}, u32[]{:S(2)}) collective-permute-start(bf16[576,128]{1,0:T(8,128)(2,1)} %gate_2_12.1.refs_3_), channel_id=1, source_target_pairs={{0,12},{1,13},{2,14},{3,15},{4,8},{5,9},{6,10},{7,11},{8,4},{9,5},... | collective-permute-start | bytes 442376 | tf_op jit(solution)/shard_map/ppermute | solution.py:460
  166.9 31.9 %collective-permute-start.36 = (bf16[576,128]{1,0:T(8,128)(2,1)}, bf16[576,128]{1,0:T(8,128)(2,1)}, u32[]{:S(2)}, u32[]{:S(2)}) collective-permute-start(bf16[576,128]{1,0:T(8,128)(2,1)} %gate_2_9.1.refs_3_), channel_id=1, source_target_pairs={{0,9},{1,8},{2,11},{3,10},{4,13},{5,12},{6,15},{7,14},{8,1},{9,0},... | collective-permute-start | bytes 442376 | tf_op jit(solution)/shard_map/ppermute | solution.py:460
  170.2 31.9 %collective-permute-start.35 = (bf16[576,128]{1,0:T(8,128)(2,1)}, bf16[576,128]{1,0:T(8,128)(2,1)}, u32[]{:S(2)}, u32[]{:S(2)}) collective-permute-start(bf16[576,128]{1,0:T(8,128)(2,1)} %gate_2_13.1.refs_3_), channel_id=1, source_target_pairs={{0,13},{1,12},{2,15},{3,14},{4,9},{5,8},{6,11},{7,10},{8,5},{9,4},... | collective-permute-start | bytes 442376 | tf_op jit(solution)/shard_map/ppermute | solution.py:460
  183.9 18.3 %collective-permute-start.31 = (bf16[576,128]{1,0:T(8,128)(2,1)}, bf16[576,128]{1,0:T(8,128)(2,1)}, u32[]{:S(2)}, u32[]{:S(2)}) collective-permute-start(bf16[576,128]{1,0:T(8,128)(2,1)} %gate_2_1.1.refs_3_), channel_id=1, source_target_pairs={{0,1},{1,0},{2,3},{3,2},{4,5},{5,4},{6,7},{7,6},{8,9},{9,8},{10,11... | collective-permute-start | bytes 442376 | tf_op jit(solution)/shard_map/ppermute | solution.py:460
  188.3 26.0 %collective-permute-start.39 = (bf16[576,128]{1,0:T(8,128)(2,1)}, bf16[576,128]{1,0:T(8,128)(2,1)}, u32[]{:S(2)}, u32[]{:S(2)}) collective-permute-start(bf16[576,128]{1,0:T(8,128)(2,1)} %gate_2_10.1.refs_3_), channel_id=1, source_target_pairs={{0,10},{1,11},{2,8},{3,9},{4,14},{5,15},{6,12},{7,13},{8,2},{9,3},... | collective-permute-start | bytes 442376 | tf_op jit(solution)/shard_map/ppermute | solution.py:460
  198.8 18.8 %collective-permute-start.34 = (bf16[576,128]{1,0:T(8,128)(2,1)}, bf16[576,128]{1,0:T(8,128)(2,1)}, u32[]{:S(2)}, u32[]{:S(2)}) collective-permute-start(bf16[576,128]{1,0:T(8,128)(2,1)} %gate_2_2.1.refs_3_), channel_id=1, source_target_pairs={{0,2},{1,3},{2,0},{3,1},{4,6},{5,7},{6,4},{7,5},{8,10},{9,11},{10,... | collective-permute-start | bytes 442376 | tf_op jit(solution)/shard_map/ppermute | solution.py:460
  198.8 18.8 %collective-permute-start.41 = (bf16[576,128]{1,0:T(8,128)(2,1)}, bf16[576,128]{1,0:T(8,128)(2,1)}, u32[]{:S(2)}, u32[]{:S(2)}) collective-permute-start(bf16[576,128]{1,0:T(8,128)(2,1)} %gate_2_14.1.refs_3_), channel_id=1, source_target_pairs={{0,14},{1,15},{2,12},{3,13},{4,10},{5,11},{6,8},{7,9},{8,6},{9,7},... | collective-permute-start | bytes 442376 | tf_op jit(solution)/shard_map/ppermute | solution.py:460
  214.3 19.5 %collective-permute-start.44 = (bf16[576,128]{1,0:T(8,128)(2,1)}, bf16[576,128]{1,0:T(8,128)(2,1)}, u32[]{:S(2)}, u32[]{:S(2)}) collective-permute-start(bf16[576,128]{1,0:T(8,128)(2,1)} %gate_2_11.1.refs_3_), channel_id=1, source_target_pairs={{0,11},{1,10},{2,9},{3,8},{4,15},{5,14},{6,13},{7,12},{8,3},{9,2},... | collective-permute-start | bytes 442376 | tf_op jit(solution)/shard_map/ppermute | solution.py:460
  (22 other events, 298.0 us)

commit v7 on v6

--- a/solution.py
+++ b/solution.py
@@ -544,14 +544,19 @@
             )
             if chunk == len(sizes):
                 break
-            final = index == len(pieces) - 1
-            first_near = near_left[0]
-            for turn in range(len(near_left) if final else 3):
-                if near_left:
-                    send(chunk + 1, near_left.pop(0), [token])
-                if far_left and turn < (len(near) if final else 2):
-                    send(chunk + 1, far_left.pop(0), [token])
-            after = [arrived[chunk + 1][first_near]]
+            if index == len(pieces) - 1:
+                turns = [near_left.pop(0) for _ in range(len(near_left))]
+                turns = far_left + turns
+            else:
+                near_now = [near_left.pop(0) for _ in range(parts // 4 - 1)]
+                turns = []
+                for near_one in near_now:
+                    turns += [near_one, far_left.pop(0)]
+                turns = turns[:-2] + [turns[-1], turns[-2]] + far_left
+                far_left = []
+            for s in turns:
+                send(chunk + 1, s, [token])
+            after = [arrived[chunk + 1][turns[1]], arrived[chunk + 1][turns[-2]]]
     return out
 
 

time: 266 us -> 272 us (1.023)
  waiting for transfers between devices: 63.7 us -> 70.9 us
    ppermute x45, waiting for transfers between devices: 63.7 us -> 70.9 us  [send(): lax.ppermute(message, axes, [(i, i ^ s) for i in range(parts)])]
  transfers between devices with their start and end apart: 46 -> 46, of which waited for: 16 -> 17; matrix products, arithmetic and copies ran while one was open for 0% -> 0% of each run, Pallas kernels for 19% -> 18%
where the time goes in v7:
time: 272 us; the launch traced here: 269 us
  Pallas kernels  103 us (38%)
  starting transfers between devices  95.6 us (35%)
  waiting for transfers between devices  70.9 us (26%)
    ppermute x45, starting transfers between devices, send(): lax.ppermute(message, axes, [(i, i ^ s) for i in range(parts)])  91.3 us
    ppermute x45, waiting for transfers between devices, send(): lax.ppermute(message, axes, [(i, i ^ s) for i in range(parts)])  70.9 us
    pallas_call x2, Pallas kernels, front(): pl.pallas_call(kernel, name=f'front_{block}', grid_spec=pltpu.PrefetchSca...  53.2 us
    pallas_call x3, Pallas kernels, correlated(): pl.pallas_call(kernel, name=name, grid_spec=pltpu.PrefetchScalarGridSpec(...  49.3 us
  transfers between devices with their start and end apart: 46, of which 17 were waited for; matrix products, arithmetic and copies ran while one was open for 0% of the time, Pallas kernels for 18%

profile of v7, /device:TPU:0, one launch (start us, length us, event | category | flops | bytes accessed | tf_op | source)
XLA Modules:
  0.0 269.4 jit_solution(4472434227691103518)
XLA Ops:
  0.0 27.5 %front_1.1 = (bf16[1024,128]{1,0:T(8,128)(2,1)}, bf16[1024,128]{1,0:T(8,128)(2,1)}, bf16[1024,128]{1,0:T(8,128)(2,1)}, bf16[1024,128]{1,0:T(8,128)(2,1)}, bf16[1...) custom-call(s32[1]{0:T(128)} %bitcast.me_ref, ...), custom_call_target="tpu_custom_call" | custom-call | tf_op jit(solution)/shard_map/front_1/pallas_call | solution.py:259
  27.5 4.3 %collective-permute-start = (bf16[8,128,2048]{2,1,0:T(8,128)(2,1)}, bf16[8,128,2048]{2,1,0:T(8,128)(2,1)}, u32[]{:S(2)}, u32[]{:S(2)}) collective-permute-start(bf16[8,128,2048]{2,1,0:T(8,128)(2,1)} %get-tuple-element.63), channel_id=1, source_target_pairs={{0,1},{2,3},{4,5},{6,7},{8,9},{10,11},{12,13},{14,15},{16,17},{18,... | collective-permute-start | bytes 12582920 | tf_op jit(solution)/shard_map/ppermute | solution.py:29
  31.8 3.4 %collective-permute-start.2 = (bf16[1024,128]{1,0:T(8,128)(2,1)}, bf16[1024,128]{1,0:T(8,128)(2,1)}, u32[]{:S(2)}, u32[]{:S(2)}) collective-permute-start(bf16[1024,128]{1,0:T(8,128)(2,1)} %get-tuple-element.69), channel_id=1, source_target_pairs={{0,8},{1,9},{2,10},{3,11},{4,12},{5,13},{6,14},{7,15},{8,0},{9,1},... | collective-permute-start | bytes 786440 | tf_op jit(solution)/shard_map/ppermute | solution.py:460
  38.9 25.7 %front_0.1 = (bf16[464,128]{1,0:T(8,128)(2,1)}, bf16[464,128]{1,0:T(8,128)(2,1)}, bf16[464,128]{1,0:T(8,128)(2,1)}, bf16[464,128]{1,0:T(8,128)(2,1)}, bf16[464,1...) custom-call(s32[1]{0:T(128)} %bitcast.me_ref, ...), custom_call_target="tpu_custom_call" | custom-call | tf_op jit(solution)/shard_map/front_0/pallas_call | solution.py:259
  66.3 5.1 %collective-permute-start.3 = (bf16[1024,128]{1,0:T(8,128)(2,1)}, bf16[1024,128]{1,0:T(8,128)(2,1)}, u32[]{:S(2)}, u32[]{:S(2)}) collective-permute-start(bf16[1024,128]{1,0:T(8,128)(2,1)} %gate_0_10.1.refs_3_), channel_id=1, source_target_pairs={{0,10},{1,11},{2,8},{3,9},{4,14},{5,15},{6,12},{7,13},{8,2},{9,3},... | collective-permute-start | bytes 786440 | tf_op jit(solution)/shard_map/ppermute | solution.py:460
  79.5 8.8 %collective-permute-start.12 = (bf16[1024,128]{1,0:T(8,128)(2,1)}, bf16[1024,128]{1,0:T(8,128)(2,1)}, u32[]{:S(2)}, u32[]{:S(2)}) collective-permute-start(bf16[1024,128]{1,0:T(8,128)(2,1)} %gate_0_7.1.refs_3_), channel_id=1, source_target_pairs={{0,7},{1,6},{2,5},{3,4},{4,3},{5,2},{6,1},{7,0},{8,15},{9,14},{10,... | collective-permute-start | bytes 786440 | tf_op jit(solution)/shard_map/ppermute | solution.py:460
  88.4 8.9 %collective-permute-done.3.refs_2_.refs_10_ = bf16[1024,128]{1,0:T(8,128)(2,1)} collective-permute-done((bf16[1024,128]{1,0:T(8,128)(2,1)}, bf16[1024,128]{1,0:T(8,128)(2,1)}, u32[]{:S(2)}, u32[]{:S(2)}) %collective-permute-start.3) | collective-permute-done | bytes 262176 | tf_op jit(solution)/shard_map/ppermute | solution.py:460
  97.3 5.0 %collective-permute-done.10.refs_2_.refs_6_ = bf16[1024,128]{1,0:T(8,128)(2,1)} collective-permute-done((bf16[1024,128]{1,0:T(8,128)(2,1)}, bf16[1024,128]{1,0:T(8,128)(2,1)}, u32[]{:S(2)}, u32[]{:S(2)}) %collective-permute-start.10) | collective-permute-done | bytes 262176 | tf_op jit(solution)/shard_map/ppermute | solution.py:460
  109.0 12.8 %collective-permute-done.14.refs_2_.refs_11_ = bf16[1024,128]{1,0:T(8,128)(2,1)} collective-permute-done((bf16[1024,128]{1,0:T(8,128)(2,1)}, bf16[1024,128]{1,0:T(8,128)(2,1)}, u32[]{:S(2)}, u32[]{:S(2)}) %collective-permute-start.14) | collective-permute-done | bytes 262176 | tf_op jit(solution)/shard_map/ppermute | solution.py:460
  122.7 4.9 %collective-permute-start.19 = (bf16[464,128]{1,0:T(8,128)(2,1)}, bf16[464,128]{1,0:T(8,128)(2,1)}, u32[]{:S(2)}, u32[]{:S(2)}) collective-permute-start(bf16[464,128]{1,0:T(8,128)(2,1)} %gate_1_4.1.refs_3_), channel_id=1, source_target_pairs={{0,4},{1,5},{2,6},{3,7},{4,0},{5,1},{6,2},{7,3},{8,12},{9,13},{10,... | collective-permute-start | bytes 356360 | tf_op jit(solution)/shard_map/ppermute | solution.py:460
  127.6 9.2 %collective-permute-start.17 = (bf16[464,128]{1,0:T(8,128)(2,1)}, bf16[464,128]{1,0:T(8,128)(2,1)}, u32[]{:S(2)}, u32[]{:S(2)}) collective-permute-start(bf16[464,128]{1,0:T(8,128)(2,1)} %gate_1_5.1.refs_3_), channel_id=1, source_target_pairs={{0,5},{1,4},{2,7},{3,6},{4,1},{5,0},{6,3},{7,2},{8,13},{9,12},{10,... | collective-permute-start | bytes 356360 | tf_op jit(solution)/shard_map/ppermute | solution.py:460
  141.7 3.1 %collective-permute-start.25 = (bf16[464,128]{1,0:T(8,128)(2,1)}, bf16[464,128]{1,0:T(8,128)(2,1)}, u32[]{:S(2)}, u32[]{:S(2)}) collective-permute-start(bf16[464,128]{1,0:T(8,128)(2,1)} %gate_1_10.1.refs_3_), channel_id=1, source_target_pairs={{0,10},{1,11},{2,8},{3,9},{4,14},{5,15},{6,12},{7,13},{8,2},{9,3},... | collective-permute-start | bytes 356360 | tf_op jit(solution)/shard_map/ppermute | solution.py:460
  147.1 4.3 %collective-permute-done.23.refs_2_.refs_22_.refs_38_ = bf16[464,128]{1,0:T(8,128)(2,1)} collective-permute-done((bf16[464,128]{1,0:T(8,128)(2,1)}, bf16[464,128]{1,0:T(8,128)(2,1)}, u32[]{:S(2)}, u32[]{:S(2)}) %collective-permute-start.23) | collective-permute-done | bytes 118816 | tf_op jit(solution)/shard_map/ppermute | solution.py:460
  153.8 3.7 %collective-permute-done.25.refs_2_.refs_26_.refs_42_ = bf16[464,128]{1,0:T(8,128)(2,1)} collective-permute-done((bf16[464,128]{1,0:T(8,128)(2,1)}, bf16[464,128]{1,0:T(8,128)(2,1)}, u32[]{:S(2)}, u32[]{:S(2)}) %collective-permute-start.25) | collective-permute-done | bytes 118816 | tf_op jit(solution)/shard_map/ppermute | solution.py:460
  157.4 4.7 %collective-permute-start.27 = (bf16[464,128]{1,0:T(8,128)(2,1)}, bf16[464,128]{1,0:T(8,128)(2,1)}, u32[]{:S(2)}, u32[]{:S(2)}) collective-permute-start(bf16[464,128]{1,0:T(8,128)(2,1)} %gate_1_3.1.refs_3_), channel_id=1, source_target_pairs={{0,3},{1,2},{2,1},{3,0},{4,7},{5,6},{6,5},{7,4},{8,11},{9,10},{10,... | collective-permute-start | bytes 356360 | tf_op jit(solution)/shard_map/ppermute | solution.py:460
  172.0 11.8 %correlate_1_0.1 = (bf16[32,2,36,128,128]{4,3,2,1,0:T(8,128)(2,1)}, f32[8,128]{1,0:T(8,128)}) custom-call(s32[1]{0:T(128)} %bitcast.me_ref, bf16[1024,128]{1,0:T(8,128)(2,1)} %get-tuple-element.61.refs_0_, bf16[1024,128]{1,0:T(8,128)(2,1)} %collective-permute-done.8.refs_2_.refs_1_, bf16[1024,128]{1,0:T(8,128)(2,1)} %collective-permute-done.11.refs_2_, ...), custom_call_target="tpu_custom_call" | custom-call | tf_op jit(solution)/shard_map/correlate_1_0/pallas_call | solution.py:377
  184.4 3.8 %collective-permute-done.33.refs_2_.refs_24_ = bf16[576,128]{1,0:T(8,128)(2,1)} collective-permute-done((bf16[576,128]{1,0:T(8,128)(2,1)}, bf16[576,128]{1,0:T(8,128)(2,1)}, u32[]{:S(2)}, u32[]{:S(2)}) %collective-permute-start.33) | collective-permute-done | bytes 147488 | tf_op jit(solution)/shard_map/ppermute | solution.py:460
  188.3 10.5 %collective-permute-start.38 = (bf16[576,128]{1,0:T(8,128)(2,1)}, bf16[576,128]{1,0:T(8,128)(2,1)}, u32[]{:S(2)}, u32[]{:S(2)}) collective-permute-start(bf16[576,128]{1,0:T(8,128)(2,1)} %gate_2_10.1.refs_3_), channel_id=1, source_target_pairs={{0,10},{1,11},{2,8},{3,9},{4,14},{5,15},{6,12},{7,13},{8,2},{9,3},... | collective-permute-start | bytes 442376 | tf_op jit(solution)/shard_map/ppermute | solution.py:460
  202.4 10.9 %collective-permute-done.38.refs_49_.refs_2_.refs_26_ = bf16[576,128]{1,0:T(8,128)(2,1)} collective-permute-done((bf16[576,128]{1,0:T(8,128)(2,1)}, bf16[576,128]{1,0:T(8,128)(2,1)}, u32[]{:S(2)}, u32[]{:S(2)}) %collective-permute-start.38) | collective-permute-done | bytes 147488 | tf_op jit(solution)/shard_map/ppermute | solution.py:460
  213.3 12.0 %correlate_1_1.1 = (bf16[32,2,36,128,128]{4,3,2,1,0:T(8,128)(2,1)}, f32[8,128]{1,0:T(8,128)}) custom-call(s32[1]{0:T(128)} %bitcast.me_ref, bf16[1024,128]{1,0:T(8,128)(2,1)} %get-tuple-element.61.refs_0_, bf16[1024,128]{1,0:T(8,128)(2,1)} %collective-permute-done.8.refs_2_.refs_1_, ...), custom_call_target="tpu_custom_call", output_to_operand_aliasing={{0}: (49, {})} | custom-call | tf_op jit(solution)/shard_map/correlate_1_1/pallas_call | solution.py:377
  225.5 4.3 %collective-permute-start.43 = (bf16[576,128]{1,0:T(8,128)(2,1)}, bf16[576,128]{1,0:T(8,128)(2,1)}, u32[]{:S(2)}, u32[]{:S(2)}) collective-permute-start(bf16[576,128]{1,0:T(8,128)(2,1)} %gate_2_6.1.refs_3_), channel_id=1, source_target_pairs={{0,6},{1,7},{2,4},{3,5},{4,2},{5,3},{6,0},{7,1},{8,14},{9,15},{10,... | collective-permute-start | bytes 442376 | tf_op jit(solution)/shard_map/ppermute | solution.py:460
  231.5 4.7 %collective-permute-done.43.refs_22_ = bf16[576,128]{1,0:T(8,128)(2,1)} collective-permute-done((bf16[576,128]{1,0:T(8,128)(2,1)}, bf16[576,128]{1,0:T(8,128)(2,1)}, u32[]{:S(2)}, u32[]{:S(2)}) %collective-permute-start.43) | collective-permute-done | bytes 147488 | tf_op jit(solution)/shard_map/ppermute | solution.py:460
  238.7 5.2 %collective-permute-done.39.refs_20_ = bf16[576,128]{1,0:T(8,128)(2,1)} collective-permute-done((bf16[576,128]{1,0:T(8,128)(2,1)}, bf16[576,128]{1,0:T(8,128)(2,1)}, u32[]{:S(2)}, u32[]{:S(2)}) %collective-permute-start.39) | collective-permute-done | bytes 147488 | tf_op jit(solution)/shard_map/ppermute | solution.py:460
  243.9 25.4 %correlate_2_0.1 = (bf16[32,2,36,128,128]{4,3,2,1,0:T(8,128)(2,1)}, f32[8,128]{1,0:T(8,128)}) custom-call(s32[1]{0:T(128)} %bitcast.me_ref, bf16[1024,128]{1,0:T(8,128)(2,1)} %get-tuple-element.61.refs_0_, bf16[1024,128]{1,0:T(8,128)(2,1)} %collective-permute-done.8.refs_2_.refs_1_, ...), custom_call_target="tpu_custom_call", output_to_operand_aliasing={{0}: (49, {})} | custom-call | tf_op jit(solution)/shard_map/correlate_2_0/pallas_call | solution.py:377
  (114 shorter events, 48.9 us)
Async XLA Ops:
  31.8 33.8 %collective-permute-start.2 = (bf16[1024,128]{1,0:T(8,128)(2,1)}, bf16[1024,128]{1,0:T(8,128)(2,1)}, u32[]{:S(2)}, u32[]{:S(2)}) collective-permute-start(bf16[1024,128]{1,0:T(8,128)(2,1)} %get-tuple-element.69), channel_id=1, source_target_pairs={{0,8},{1,9},{2,10},{3,11},{4,12},{5,13},{6,14},{7,15},{8,0},{9,1},... | collective-permute-start | bytes 786440 | tf_op jit(solution)/shard_map/ppermute | solution.py:460
  35.3 31.1 %collective-permute-start.1 = (bf16[1024,128]{1,0:T(8,128)(2,1)}, bf16[1024,128]{1,0:T(8,128)(2,1)}, u32[]{:S(2)}, u32[]{:S(2)}) collective-permute-start(bf16[1024,128]{1,0:T(8,128)(2,1)} %get-tuple-element.67), channel_id=1, source_target_pairs={{0,12},{1,13},{2,14},{3,15},{4,8},{5,9},{6,10},{7,11},{8,4},{9,5},... | collective-permute-start | bytes 786440 | tf_op jit(solution)/shard_map/ppermute | solution.py:460
  36.6 35.7 %collective-permute-start.7 = (bf16[1024,128]{1,0:T(8,128)(2,1)}, bf16[1024,128]{1,0:T(8,128)(2,1)}, u32[]{:S(2)}, u32[]{:S(2)}) collective-permute-start(bf16[1024,128]{1,0:T(8,128)(2,1)} %get-tuple-element.76), channel_id=1, source_target_pairs={{0,9},{1,8},{2,11},{3,10},{4,13},{5,12},{6,15},{7,14},{8,1},{9,0},... | collective-permute-start | bytes 786440 | tf_op jit(solution)/shard_map/ppermute | solution.py:460
  36.6 38.6 %collective-permute-start.6 = (bf16[1024,128]{1,0:T(8,128)(2,1)}, bf16[1024,128]{1,0:T(8,128)(2,1)}, u32[]{:S(2)}, u32[]{:S(2)}) collective-permute-start(bf16[1024,128]{1,0:T(8,128)(2,1)} %get-tuple-element.74), channel_id=1, source_target_pairs={{0,13},{1,12},{2,15},{3,14},{4,9},{5,8},{6,11},{7,10},{8,5},{9,4},... | collective-permute-start | bytes 786440 | tf_op jit(solution)/shard_map/ppermute | solution.py:460
  65.6 22.8 %collective-permute-start.4 = (bf16[1024,128]{1,0:T(8,128)(2,1)}, bf16[1024,128]{1,0:T(8,128)(2,1)}, u32[]{:S(2)}, u32[]{:S(2)}) collective-permute-start(bf16[1024,128]{1,0:T(8,128)(2,1)} %gate_0_5.1.refs_3_), channel_id=1, source_target_pairs={{0,5},{1,4},{2,7},{3,6},{4,1},{5,0},{6,3},{7,2},{8,13},{9,12},{10,... | collective-permute-start | bytes 786440 | tf_op jit(solution)/shard_map/ppermute | solution.py:460
  66.3 30.9 %collective-permute-start.3 = (bf16[1024,128]{1,0:T(8,128)(2,1)}, bf16[1024,128]{1,0:T(8,128)(2,1)}, u32[]{:S(2)}, u32[]{:S(2)}) collective-permute-start(bf16[1024,128]{1,0:T(8,128)(2,1)} %gate_0_10.1.refs_3_), channel_id=1, source_target_pairs={{0,10},{1,11},{2,8},{3,9},{4,14},{5,15},{6,12},{7,13},{8,2},{9,3},... | collective-permute-start | bytes 786440 | tf_op jit(solution)/shard_map/ppermute | solution.py:460
  72.3 30.0 %collective-permute-start.10 = (bf16[1024,128]{1,0:T(8,128)(2,1)}, bf16[1024,128]{1,0:T(8,128)(2,1)}, u32[]{:S(2)}, u32[]{:S(2)}) collective-permute-start(bf16[1024,128]{1,0:T(8,128)(2,1)} %gate_0_6.1.refs_3_), channel_id=1, source_target_pairs={{0,6},{1,7},{2,4},{3,5},{4,2},{5,3},{6,0},{7,1},{8,14},{9,15},{10,... | collective-permute-start | bytes 786440 | tf_op jit(solution)/shard_map/ppermute | solution.py:460
  75.2 28.7 %collective-permute-start.9 = (bf16[1024,128]{1,0:T(8,128)(2,1)}, bf16[1024,128]{1,0:T(8,128)(2,1)}, u32[]{:S(2)}, u32[]{:S(2)}) collective-permute-start(bf16[1024,128]{1,0:T(8,128)(2,1)} %gate_0_14.1.refs_3_), channel_id=1, source_target_pairs={{0,14},{1,15},{2,12},{3,13},{4,10},{5,11},{6,8},{7,9},{8,6},{9,7},... | collective-permute-start | bytes 786440 | tf_op jit(solution)/shard_map/ppermute | solution.py:460
  79.5 28.8 %collective-permute-start.12 = (bf16[1024,128]{1,0:T(8,128)(2,1)}, bf16[1024,128]{1,0:T(8,128)(2,1)}, u32[]{:S(2)}, u32[]{:S(2)}) collective-permute-start(bf16[1024,128]{1,0:T(8,128)(2,1)} %gate_0_7.1.refs_3_), channel_id=1, source_target_pairs={{0,7},{1,6},{2,5},{3,4},{4,3},{5,2},{6,1},{7,0},{8,15},{9,14},{10,... | collective-permute-start | bytes 786440 | tf_op jit(solution)/shard_map/ppermute | solution.py:460
  88.4 33.4 %collective-permute-start.14 = (bf16[1024,128]{1,0:T(8,128)(2,1)}, bf16[1024,128]{1,0:T(8,128)(2,1)}, u32[]{:S(2)}, u32[]{:S(2)}) collective-permute-start(bf16[1024,128]{1,0:T(8,128)(2,1)} %gate_0_11.1.refs_3_), channel_id=1, source_target_pairs={{0,11},{1,10},{2,9},{3,8},{4,15},{5,14},{6,13},{7,12},{8,3},{9,2},... | collective-permute-start | bytes 786440 | tf_op jit(solution)/shard_map/ppermute | solution.py:460
  97.3 25.4 %collective-permute-start.8 = (bf16[1024,128]{1,0:T(8,128)(2,1)}, bf16[1024,128]{1,0:T(8,128)(2,1)}, u32[]{:S(2)}, u32[]{:S(2)}) collective-permute-start(bf16[1024,128]{1,0:T(8,128)(2,1)} %gate_0_1.1.refs_3_), channel_id=1, source_target_pairs={{0,1},{1,0},{2,3},{3,2},{4,5},{5,4},{6,7},{7,6},{8,9},{9,8},{10,11... | collective-permute-start | bytes 786440 | tf_op jit(solution)/shard_map/ppermute | solution.py:460
  102.3 25.3 %collective-permute-start.15 = (bf16[1024,128]{1,0:T(8,128)(2,1)}, bf16[1024,128]{1,0:T(8,128)(2,1)}, u32[]{:S(2)}, u32[]{:S(2)}) collective-permute-start(bf16[1024,128]{1,0:T(8,128)(2,1)} %gate_0_15.1.refs_3_), channel_id=1, source_target_pairs={{0,15},{1,14},{2,13},{3,12},{4,11},{5,10},{6,9},{7,8},{8,7},{9,6},... | collective-permute-start | bytes 786440 | tf_op jit(solution)/shard_map/ppermute | solution.py:460
  103.9 23.7 %collective-permute-start.11 = (bf16[1024,128]{1,0:T(8,128)(2,1)}, bf16[1024,128]{1,0:T(8,128)(2,1)}, u32[]{:S(2)}, u32[]{:S(2)}) collective-permute-start(bf16[1024,128]{1,0:T(8,128)(2,1)} %gate_0_2.1.refs_3_), channel_id=1, source_target_pairs={{0,2},{1,3},{2,0},{3,1},{4,6},{5,7},{6,4},{7,5},{8,10},{9,11},{10,... | collective-permute-start | bytes 786440 | tf_op jit(solution)/shard_map/ppermute | solution.py:460
  108.4 28.4 %collective-permute-start.13 = (bf16[1024,128]{1,0:T(8,128)(2,1)}, bf16[1024,128]{1,0:T(8,128)(2,1)}, u32[]{:S(2)}, u32[]{:S(2)}) collective-permute-start(bf16[1024,128]{1,0:T(8,128)(2,1)} %gate_0_3.1.refs_3_), channel_id=1, source_target_pairs={{0,3},{1,2},{2,1},{3,0},{4,7},{5,6},{6,5},{7,4},{8,11},{9,10},{10,... | collective-permute-start | bytes 786440 | tf_op jit(solution)/shard_map/ppermute | solution.py:460
  121.8 17.9 %collective-permute-start.20 = (bf16[464,128]{1,0:T(8,128)(2,1)}, bf16[464,128]{1,0:T(8,128)(2,1)}, u32[]{:S(2)}, u32[]{:S(2)}) collective-permute-start(bf16[464,128]{1,0:T(8,128)(2,1)} %gate_1_8.1.refs_3_), channel_id=1, source_target_pairs={{0,8},{1,9},{2,10},{3,11},{4,12},{5,13},{6,14},{7,15},{8,0},{9,1},... | collective-permute-start | bytes 356360 | tf_op jit(solution)/shard_map/ppermute | solution.py:460
  164.5 23.7 %collective-permute-start.33 = (bf16[576,128]{1,0:T(8,128)(2,1)}, bf16[576,128]{1,0:T(8,128)(2,1)}, u32[]{:S(2)}, u32[]{:S(2)}) collective-permute-start(bf16[576,128]{1,0:T(8,128)(2,1)} %gate_2_8.1.refs_3_), channel_id=1, source_target_pairs={{0,8},{1,9},{2,10},{3,11},{4,12},{5,13},{6,14},{7,15},{8,0},{9,1},... | collective-permute-start | bytes 442376 | tf_op jit(solution)/shard_map/ppermute | solution.py:460
  165.0 33.8 %collective-permute-start.32 = (bf16[576,128]{1,0:T(8,128)(2,1)}, bf16[576,128]{1,0:T(8,128)(2,1)}, u32[]{:S(2)}, u32[]{:S(2)}) collective-permute-start(bf16[576,128]{1,0:T(8,128)(2,1)} %gate_2_12.1.refs_3_), channel_id=1, source_target_pairs={{0,12},{1,13},{2,14},{3,15},{4,8},{5,9},{6,10},{7,11},{8,4},{9,5},... | collective-permute-start | bytes 442376 | tf_op jit(solution)/shard_map/ppermute | solution.py:460
  166.9 31.9 %collective-permute-start.36 = (bf16[576,128]{1,0:T(8,128)(2,1)}, bf16[576,128]{1,0:T(8,128)(2,1)}, u32[]{:S(2)}, u32[]{:S(2)}) collective-permute-start(bf16[576,128]{1,0:T(8,128)(2,1)} %gate_2_9.1.refs_3_), channel_id=1, source_target_pairs={{0,9},{1,8},{2,11},{3,10},{4,13},{5,12},{6,15},{7,14},{8,1},{9,0},... | collective-permute-start | bytes 442376 | tf_op jit(solution)/shard_map/ppermute | solution.py:460
  170.2 28.6 %collective-permute-start.35 = (bf16[576,128]{1,0:T(8,128)(2,1)}, bf16[576,128]{1,0:T(8,128)(2,1)}, u32[]{:S(2)}, u32[]{:S(2)}) collective-permute-start(bf16[576,128]{1,0:T(8,128)(2,1)} %gate_2_13.1.refs_3_), channel_id=1, source_target_pairs={{0,13},{1,12},{2,15},{3,14},{4,9},{5,8},{6,11},{7,10},{8,5},{9,4},... | collective-permute-start | bytes 442376 | tf_op jit(solution)/shard_map/ppermute | solution.py:460
  188.3 25.0 %collective-permute-start.38 = (bf16[576,128]{1,0:T(8,128)(2,1)}, bf16[576,128]{1,0:T(8,128)(2,1)}, u32[]{:S(2)}, u32[]{:S(2)}) collective-permute-start(bf16[576,128]{1,0:T(8,128)(2,1)} %gate_2_10.1.refs_3_), channel_id=1, source_target_pairs={{0,10},{1,11},{2,8},{3,9},{4,14},{5,15},{6,12},{7,13},{8,2},{9,3},... | collective-permute-start | bytes 442376 | tf_op jit(solution)/shard_map/ppermute | solution.py:460
  198.9 26.4 %collective-permute-start.34 = (bf16[576,128]{1,0:T(8,128)(2,1)}, bf16[576,128]{1,0:T(8,128)(2,1)}, u32[]{:S(2)}, u32[]{:S(2)}) collective-permute-start(bf16[576,128]{1,0:T(8,128)(2,1)} %gate_2_2.1.refs_3_), channel_id=1, source_target_pairs={{0,2},{1,3},{2,0},{3,1},{4,6},{5,7},{6,4},{7,5},{8,10},{9,11},{10,... | collective-permute-start | bytes 442376 | tf_op jit(solution)/shard_map/ppermute | solution.py:460
  200.4 25.0 %collective-permute-start.40 = (bf16[576,128]{1,0:T(8,128)(2,1)}, bf16[576,128]{1,0:T(8,128)(2,1)}, u32[]{:S(2)}, u32[]{:S(2)}) collective-permute-start(bf16[576,128]{1,0:T(8,128)(2,1)} %gate_2_14.1.refs_3_), channel_id=1, source_target_pairs={{0,14},{1,15},{2,12},{3,13},{4,10},{5,11},{6,8},{7,9},{8,6},{9,7},... | collective-permute-start | bytes 442376 | tf_op jit(solution)/shard_map/ppermute | solution.py:460
  202.4 23.0 %collective-permute-start.42 = (bf16[576,128]{1,0:T(8,128)(2,1)}, bf16[576,128]{1,0:T(8,128)(2,1)}, u32[]{:S(2)}, u32[]{:S(2)}) collective-permute-start(bf16[576,128]{1,0:T(8,128)(2,1)} %gate_2_11.1.refs_3_), channel_id=1, source_target_pairs={{0,11},{1,10},{2,9},{3,8},{4,15},{5,14},{6,13},{7,12},{8,3},{9,2},... | collective-permute-start | bytes 442376 | tf_op jit(solution)/shard_map/ppermute | solution.py:460
  213.3 18.2 %collective-permute-start.45 = (bf16[576,128]{1,0:T(8,128)(2,1)}, bf16[576,128]{1,0:T(8,128)(2,1)}, u32[]{:S(2)}, u32[]{:S(2)}) collective-permute-start(bf16[576,128]{1,0:T(8,128)(2,1)} %gate_2_15.1.refs_3_), channel_id=1, source_target_pairs={{0,15},{1,14},{2,13},{3,12},{4,11},{5,10},{6,9},{7,8},{8,7},{9,6},... | collective-permute-start | bytes 442376 | tf_op jit(solution)/shard_map/ppermute | solution.py:460
  (22 other events, 278.6 us)

commit v8 on v6

--- a/solution.py
+++ b/solution.py
@@ -522,7 +522,7 @@
         if chunk == len(sizes):
             pieces = [size]
         else:
-            pieces = [size - size // 2, size // 2]
+            pieces = [size]
             far_left, near_left = list(far), near[parts // 4 :] + near[: parts // 4]
             for s in far_left[: FLIGHT - 1]:
                 send(chunk + 1, s, [token])

time: 266 us -> 270 us (1.015)
  Pallas kernels: 103 us -> 99.4 us
  waiting for transfers between devices: 63.7 us -> 67.1 us
  starting transfers between devices: 96.3 us -> 99.4 us
    ppermute x45, waiting for transfers between devices: 63.7 us -> 67.1 us  [send(): lax.ppermute(message, axes, [(i, i ^ s) for i in range(parts)])]
    pallas_call x3 -> x2, Pallas kernels: 49.3 us -> 46.1 us  [correlated(): pl.pallas_call(kernel, name=name, grid_spec=pltpu.PrefetchScalarGridSpec(...]
    ppermute x45, starting transfers between devices: 92 us -> 95.1 us  [send(): lax.ppermute(message, axes, [(i, i ^ s) for i in range(parts)])]
  transfers between devices with their start and end apart: 46 -> 46, of which waited for: 16 -> 16; matrix products, arithmetic and copies ran while one was open for 0% -> 0% of each run, Pallas kernels for 19% -> 17%
where the time goes in v8:
time: 270 us; the launch traced here: 266 us
  Pallas kernels  99.4 us (37%)
  starting transfers between devices  99.4 us (37%)
  waiting for transfers between devices  67.1 us (25%)
    ppermute x45, starting transfers between devices, send(): lax.ppermute(message, axes, [(i, i ^ s) for i in range(parts)])  95.1 us
    ppermute x45, waiting for transfers between devices, send(): lax.ppermute(message, axes, [(i, i ^ s) for i in range(parts)])  67.1 us
    pallas_call x2, Pallas kernels, front(): pl.pallas_call(kernel, name=f'front_{block}', grid_spec=pltpu.PrefetchSca...  53.2 us
    pallas_call x2, Pallas kernels, correlated(): pl.pallas_call(kernel, name=name, grid_spec=pltpu.PrefetchScalarGridSpec(...  46.1 us
  transfers between devices with their start and end apart: 46, of which 16 were waited for; matrix products, arithmetic and copies ran while one was open for 0% of the time, Pallas kernels for 17%

profile of v8, /device:TPU:0, one launch (start us, length us, event | category | flops | bytes accessed | tf_op | source)
XLA Modules:
  0.0 266.2 jit_solution(591797121301119217)
XLA Ops:
  0.0 27.5 %front_1.1 = (bf16[1024,128]{1,0:T(8,128)(2,1)}, bf16[1024,128]{1,0:T(8,128)(2,1)}, bf16[1024,128]{1,0:T(8,128)(2,1)}, bf16[1024,128]{1,0:T(8,128)(2,1)}, bf16[1...) custom-call(s32[1]{0:T(128)} %bitcast.me_ref, ...), custom_call_target="tpu_custom_call" | custom-call | tf_op jit(solution)/shard_map/front_1/pallas_call | solution.py:259
  27.5 4.3 %collective-permute-start = (bf16[8,128,2048]{2,1,0:T(8,128)(2,1)}, bf16[8,128,2048]{2,1,0:T(8,128)(2,1)}, u32[]{:S(2)}, u32[]{:S(2)}) collective-permute-start(bf16[8,128,2048]{2,1,0:T(8,128)(2,1)} %get-tuple-element.61), channel_id=1, source_target_pairs={{0,1},{2,3},{4,5},{6,7},{8,9},{10,11},{12,13},{14,15},{16,17},{18,... | collective-permute-start | bytes 12582920 | tf_op jit(solution)/shard_map/ppermute | solution.py:29
  31.9 3.4 %collective-permute-start.2 = (bf16[1024,128]{1,0:T(8,128)(2,1)}, bf16[1024,128]{1,0:T(8,128)(2,1)}, u32[]{:S(2)}, u32[]{:S(2)}) collective-permute-start(bf16[1024,128]{1,0:T(8,128)(2,1)} %get-tuple-element.67), channel_id=1, source_target_pairs={{0,8},{1,9},{2,10},{3,11},{4,12},{5,13},{6,14},{7,15},{8,0},{9,1},... | collective-permute-start | bytes 786440 | tf_op jit(solution)/shard_map/ppermute | solution.py:460
  38.9 25.7 %front_0.1 = (bf16[464,128]{1,0:T(8,128)(2,1)}, bf16[464,128]{1,0:T(8,128)(2,1)}, bf16[464,128]{1,0:T(8,128)(2,1)}, bf16[464,128]{1,0:T(8,128)(2,1)}, bf16[464,1...) custom-call(s32[1]{0:T(128)} %bitcast.me_ref, ...), custom_call_target="tpu_custom_call" | custom-call | tf_op jit(solution)/shard_map/front_0/pallas_call | solution.py:259
  66.4 5.1 %collective-permute-start.3 = (bf16[1024,128]{1,0:T(8,128)(2,1)}, bf16[1024,128]{1,0:T(8,128)(2,1)}, u32[]{:S(2)}, u32[]{:S(2)}) collective-permute-start(bf16[1024,128]{1,0:T(8,128)(2,1)} %gate_0_10.1.refs_3_), channel_id=1, source_target_pairs={{0,10},{1,11},{2,8},{3,9},{4,14},{5,15},{6,12},{7,13},{8,2},{9,3},... | collective-permute-start | bytes 786440 | tf_op jit(solution)/shard_map/ppermute | solution.py:460
  72.3 2.9 %collective-permute-start.10 = (bf16[1024,128]{1,0:T(8,128)(2,1)}, bf16[1024,128]{1,0:T(8,128)(2,1)}, u32[]{:S(2)}, u32[]{:S(2)}) collective-permute-start(bf16[1024,128]{1,0:T(8,128)(2,1)} %gate_0_6.1.refs_3_), channel_id=1, source_target_pairs={{0,6},{1,7},{2,4},{3,5},{4,2},{5,3},{6,0},{7,1},{8,14},{9,15},{10,... | collective-permute-start | bytes 786440 | tf_op jit(solution)/shard_map/ppermute | solution.py:460
  79.6 8.8 %collective-permute-start.12 = (bf16[1024,128]{1,0:T(8,128)(2,1)}, bf16[1024,128]{1,0:T(8,128)(2,1)}, u32[]{:S(2)}, u32[]{:S(2)}) collective-permute-start(bf16[1024,128]{1,0:T(8,128)(2,1)} %gate_0_7.1.refs_3_), channel_id=1, source_target_pairs={{0,7},{1,6},{2,5},{3,4},{4,3},{5,2},{6,1},{7,0},{8,15},{9,14},{10,... | collective-permute-start | bytes 786440 | tf_op jit(solution)/shard_map/ppermute | solution.py:460
  88.4 8.9 %collective-permute-done.3.refs_2_.refs_10_ = bf16[1024,128]{1,0:T(8,128)(2,1)} collective-permute-done((bf16[1024,128]{1,0:T(8,128)(2,1)}, bf16[1024,128]{1,0:T(8,128)(2,1)}, u32[]{:S(2)}, u32[]{:S(2)}) %collective-permute-start.3) | collective-permute-done | bytes 262176 | tf_op jit(solution)/shard_map/ppermute | solution.py:460
  97.2 5.0 %collective-permute-done.10.refs_2_.refs_6_ = bf16[1024,128]{1,0:T(8,128)(2,1)} collective-permute-done((bf16[1024,128]{1,0:T(8,128)(2,1)}, bf16[1024,128]{1,0:T(8,128)(2,1)}, u32[]{:S(2)}, u32[]{:S(2)}) %collective-permute-start.10) | collective-permute-done | bytes 262176 | tf_op jit(solution)/shard_map/ppermute | solution.py:460
  105.4 3.0 %collective-permute-done.12.refs_2_.refs_7_ = bf16[1024,128]{1,0:T(8,128)(2,1)} collective-permute-done((bf16[1024,128]{1,0:T(8,128)(2,1)}, bf16[1024,128]{1,0:T(8,128)(2,1)}, u32[]{:S(2)}, u32[]{:S(2)}) %collective-permute-start.12) | collective-permute-done | bytes 262176 | tf_op jit(solution)/shard_map/ppermute | solution.py:460
  111.3 10.5 %collective-permute-done.14.refs_2_.refs_11_ = bf16[1024,128]{1,0:T(8,128)(2,1)} collective-permute-done((bf16[1024,128]{1,0:T(8,128)(2,1)}, bf16[1024,128]{1,0:T(8,128)(2,1)}, u32[]{:S(2)}, u32[]{:S(2)}) %collective-permute-start.14) | collective-permute-done | bytes 262176 | tf_op jit(solution)/shard_map/ppermute | solution.py:460
  121.8 5.7 %collective-permute-start.19 = (bf16[464,128]{1,0:T(8,128)(2,1)}, bf16[464,128]{1,0:T(8,128)(2,1)}, u32[]{:S(2)}, u32[]{:S(2)}) collective-permute-start(bf16[464,128]{1,0:T(8,128)(2,1)} %gate_1_4.1.refs_3_), channel_id=1, source_target_pairs={{0,4},{1,5},{2,6},{3,7},{4,0},{5,1},{6,2},{7,3},{8,12},{9,13},{10,... | collective-permute-start | bytes 356360 | tf_op jit(solution)/shard_map/ppermute | solution.py:460
  127.6 9.2 %collective-permute-start.17 = (bf16[464,128]{1,0:T(8,128)(2,1)}, bf16[464,128]{1,0:T(8,128)(2,1)}, u32[]{:S(2)}, u32[]{:S(2)}) collective-permute-start(bf16[464,128]{1,0:T(8,128)(2,1)} %gate_1_5.1.refs_3_), channel_id=1, source_target_pairs={{0,5},{1,4},{2,7},{3,6},{4,1},{5,0},{6,3},{7,2},{8,13},{9,12},{10,... | collective-permute-start | bytes 356360 | tf_op jit(solution)/shard_map/ppermute | solution.py:460
  136.7 3.2 %collective-permute-start.16 = (bf16[464,128]{1,0:T(8,128)(2,1)}, bf16[464,128]{1,0:T(8,128)(2,1)}, u32[]{:S(2)}, u32[]{:S(2)}) collective-permute-start(bf16[464,128]{1,0:T(8,128)(2,1)} %gate_1_9.1.refs_3_), channel_id=1, source_target_pairs={{0,9},{1,8},{2,11},{3,10},{4,13},{5,12},{6,15},{7,14},{8,1},{9,0},... | collective-permute-start | bytes 356360 | tf_op jit(solution)/shard_map/ppermute | solution.py:460
  141.7 3.4 %collective-permute-start.25 = (bf16[464,128]{1,0:T(8,128)(2,1)}, bf16[464,128]{1,0:T(8,128)(2,1)}, u32[]{:S(2)}, u32[]{:S(2)}) collective-permute-start(bf16[464,128]{1,0:T(8,128)(2,1)} %gate_1_10.1.refs_3_), channel_id=1, source_target_pairs={{0,10},{1,11},{2,8},{3,9},{4,14},{5,15},{6,12},{7,13},{8,2},{9,3},... | collective-permute-start | bytes 356360 | tf_op jit(solution)/shard_map/ppermute | solution.py:460
  147.1 4.6 %collective-permute-done.23.refs_2_.refs_22_.refs_38_ = bf16[464,128]{1,0:T(8,128)(2,1)} collective-permute-done((bf16[464,128]{1,0:T(8,128)(2,1)}, bf16[464,128]{1,0:T(8,128)(2,1)}, u32[]{:S(2)}, u32[]{:S(2)}) %collective-permute-start.23) | collective-permute-done | bytes 118816 | tf_op jit(solution)/shard_map/ppermute | solution.py:460
  153.7 3.7 %collective-permute-done.25.refs_2_.refs_26_.refs_42_ = bf16[464,128]{1,0:T(8,128)(2,1)} collective-permute-done((bf16[464,128]{1,0:T(8,128)(2,1)}, bf16[464,128]{1,0:T(8,128)(2,1)}, u32[]{:S(2)}, u32[]{:S(2)}) %collective-permute-start.25) | collective-permute-done | bytes 118816 | tf_op jit(solution)/shard_map/ppermute | solution.py:460
  157.4 5.4 %collective-permute-start.27 = (bf16[464,128]{1,0:T(8,128)(2,1)}, bf16[464,128]{1,0:T(8,128)(2,1)}, u32[]{:S(2)}, u32[]{:S(2)}) collective-permute-start(bf16[464,128]{1,0:T(8,128)(2,1)} %gate_1_3.1.refs_3_), channel_id=1, source_target_pairs={{0,3},{1,2},{2,1},{3,0},{4,7},{5,6},{6,5},{7,4},{8,11},{9,10},{10,... | collective-permute-start | bytes 356360 | tf_op jit(solution)/shard_map/ppermute | solution.py:460
  172.0 20.7 %correlate_1_0.1 = (bf16[32,2,36,128,128]{4,3,2,1,0:T(8,128)(2,1)}, f32[8,128]{1,0:T(8,128)}) custom-call(s32[1]{0:T(128)} %bitcast.me_ref, bf16[1024,128]{1,0:T(8,128)(2,1)} %get-tuple-element.59.refs_0_, bf16[1024,128]{1,0:T(8,128)(2,1)} %collective-permute-done.8.refs_2_.refs_1_, bf16[1024,128]{1,0:T(8,128)(2,1)} %collective-permute-done.11.refs_2_, ...), custom_call_target="tpu_custom_call" | custom-call | tf_op jit(solution)/shard_map/correlate_1_0/pallas_call | solution.py:377
  193.2 14.4 %collective-permute-start.38 = (bf16[576,128]{1,0:T(8,128)(2,1)}, bf16[576,128]{1,0:T(8,128)(2,1)}, u32[]{:S(2)}, u32[]{:S(2)}) collective-permute-start(bf16[576,128]{1,0:T(8,128)(2,1)} %gate_2_10.1.refs_3_), channel_id=1, source_target_pairs={{0,10},{1,11},{2,8},{3,9},{4,14},{5,15},{6,12},{7,13},{8,2},{9,3},... | collective-permute-start | bytes 442376 | tf_op jit(solution)/shard_map/ppermute | solution.py:460
  207.7 3.3 %collective-permute-start.40 = (bf16[576,128]{1,0:T(8,128)(2,1)}, bf16[576,128]{1,0:T(8,128)(2,1)}, u32[]{:S(2)}, u32[]{:S(2)}) collective-permute-start(bf16[576,128]{1,0:T(8,128)(2,1)} %gate_2_14.1.refs_3_), channel_id=1, source_target_pairs={{0,14},{1,15},{2,12},{3,13},{4,10},{5,11},{6,8},{7,9},{8,6},{9,7},... | collective-permute-start | bytes 442376 | tf_op jit(solution)/shard_map/ppermute | solution.py:460
  211.1 11.0 %collective-permute-done.38.refs_2_.refs_26_ = bf16[576,128]{1,0:T(8,128)(2,1)} collective-permute-done((bf16[576,128]{1,0:T(8,128)(2,1)}, bf16[576,128]{1,0:T(8,128)(2,1)}, u32[]{:S(2)}, u32[]{:S(2)}) %collective-permute-start.38) | collective-permute-done | bytes 147488 | tf_op jit(solution)/shard_map/ppermute | solution.py:460
  228.2 12.2 %collective-permute-done.42.refs_22_ = bf16[576,128]{1,0:T(8,128)(2,1)} collective-permute-done((bf16[576,128]{1,0:T(8,128)(2,1)}, bf16[576,128]{1,0:T(8,128)(2,1)}, u32[]{:S(2)}, u32[]{:S(2)}) %collective-permute-start.42) | collective-permute-done | bytes 147488 | tf_op jit(solution)/shard_map/ppermute | solution.py:460
  240.6 25.4 %correlate_2_0.1 = (bf16[32,2,36,128,128]{4,3,2,1,0:T(8,128)(2,1)}, f32[8,128]{1,0:T(8,128)}) custom-call(s32[1]{0:T(128)} %bitcast.me_ref, bf16[1024,128]{1,0:T(8,128)(2,1)} %get-tuple-element.59.refs_0_, bf16[1024,128]{1,0:T(8,128)(2,1)} %collective-permute-done.8.refs_2_.refs_1_, ...), custom_call_target="tpu_custom_call", output_to_operand_aliasing={{0}: (49, {})} | custom-call | tf_op jit(solution)/shard_map/correlate_2_0/pallas_call | solution.py:377
  (113 shorter events, 38.3 us)
Async XLA Ops:
  31.9 33.8 %collective-permute-start.2 = (bf16[1024,128]{1,0:T(8,128)(2,1)}, bf16[1024,128]{1,0:T(8,128)(2,1)}, u32[]{:S(2)}, u32[]{:S(2)}) collective-permute-start(bf16[1024,128]{1,0:T(8,128)(2,1)} %get-tuple-element.67), channel_id=1, source_target_pairs={{0,8},{1,9},{2,10},{3,11},{4,12},{5,13},{6,14},{7,15},{8,0},{9,1},... | collective-permute-start | bytes 786440 | tf_op jit(solution)/shard_map/ppermute | solution.py:460
  35.3 31.1 %collective-permute-start.1 = (bf16[1024,128]{1,0:T(8,128)(2,1)}, bf16[1024,128]{1,0:T(8,128)(2,1)}, u32[]{:S(2)}, u32[]{:S(2)}) collective-permute-start(bf16[1024,128]{1,0:T(8,128)(2,1)} %get-tuple-element.65), channel_id=1, source_target_pairs={{0,12},{1,13},{2,14},{3,15},{4,8},{5,9},{6,10},{7,11},{8,4},{9,5},... | collective-permute-start | bytes 786440 | tf_op jit(solution)/shard_map/ppermute | solution.py:460
  36.6 35.7 %collective-permute-start.7 = (bf16[1024,128]{1,0:T(8,128)(2,1)}, bf16[1024,128]{1,0:T(8,128)(2,1)}, u32[]{:S(2)}, u32[]{:S(2)}) collective-permute-start(bf16[1024,128]{1,0:T(8,128)(2,1)} %get-tuple-element.74), channel_id=1, source_target_pairs={{0,9},{1,8},{2,11},{3,10},{4,13},{5,12},{6,15},{7,14},{8,1},{9,0},... | collective-permute-start | bytes 786440 | tf_op jit(solution)/shard_map/ppermute | solution.py:460
  36.6 38.6 %collective-permute-start.6 = (bf16[1024,128]{1,0:T(8,128)(2,1)}, bf16[1024,128]{1,0:T(8,128)(2,1)}, u32[]{:S(2)}, u32[]{:S(2)}) collective-permute-start(bf16[1024,128]{1,0:T(8,128)(2,1)} %get-tuple-element.72), channel_id=1, source_target_pairs={{0,13},{1,12},{2,15},{3,14},{4,9},{5,8},{6,11},{7,10},{8,5},{9,4},... | collective-permute-start | bytes 786440 | tf_op jit(solution)/shard_map/ppermute | solution.py:460
  65.6 22.7 %collective-permute-start.4 = (bf16[1024,128]{1,0:T(8,128)(2,1)}, bf16[1024,128]{1,0:T(8,128)(2,1)}, u32[]{:S(2)}, u32[]{:S(2)}) collective-permute-start(bf16[1024,128]{1,0:T(8,128)(2,1)} %gate_0_5.1.refs_3_), channel_id=1, source_target_pairs={{0,5},{1,4},{2,7},{3,6},{4,1},{5,0},{6,3},{7,2},{8,13},{9,12},{10,... | collective-permute-start | bytes 786440 | tf_op jit(solution)/shard_map/ppermute | solution.py:460
  66.4 30.9 %collective-permute-start.3 = (bf16[1024,128]{1,0:T(8,128)(2,1)}, bf16[1024,128]{1,0:T(8,128)(2,1)}, u32[]{:S(2)}, u32[]{:S(2)}) collective-permute-start(bf16[1024,128]{1,0:T(8,128)(2,1)} %gate_0_10.1.refs_3_), channel_id=1, source_target_pairs={{0,10},{1,11},{2,8},{3,9},{4,14},{5,15},{6,12},{7,13},{8,2},{9,3},... | collective-permute-start | bytes 786440 | tf_op jit(solution)/shard_map/ppermute | solution.py:460
  72.3 29.9 %collective-permute-start.10 = (bf16[1024,128]{1,0:T(8,128)(2,1)}, bf16[1024,128]{1,0:T(8,128)(2,1)}, u32[]{:S(2)}, u32[]{:S(2)}) collective-permute-start(bf16[1024,128]{1,0:T(8,128)(2,1)} %gate_0_6.1.refs_3_), channel_id=1, source_target_pairs={{0,6},{1,7},{2,4},{3,5},{4,2},{5,3},{6,0},{7,1},{8,14},{9,15},{10,... | collective-permute-start | bytes 786440 | tf_op jit(solution)/shard_map/ppermute | solution.py:460
  75.2 28.7 %collective-permute-start.9 = (bf16[1024,128]{1,0:T(8,128)(2,1)}, bf16[1024,128]{1,0:T(8,128)(2,1)}, u32[]{:S(2)}, u32[]{:S(2)}) collective-permute-start(bf16[1024,128]{1,0:T(8,128)(2,1)} %gate_0_14.1.refs_3_), channel_id=1, source_target_pairs={{0,14},{1,15},{2,12},{3,13},{4,10},{5,11},{6,8},{7,9},{8,6},{9,7},... | collective-permute-start | bytes 786440 | tf_op jit(solution)/shard_map/ppermute | solution.py:460
  79.6 28.9 %collective-permute-start.12 = (bf16[1024,128]{1,0:T(8,128)(2,1)}, bf16[1024,128]{1,0:T(8,128)(2,1)}, u32[]{:S(2)}, u32[]{:S(2)}) collective-permute-start(bf16[1024,128]{1,0:T(8,128)(2,1)} %gate_0_7.1.refs_3_), channel_id=1, source_target_pairs={{0,7},{1,6},{2,5},{3,4},{4,3},{5,2},{6,1},{7,0},{8,15},{9,14},{10,... | collective-permute-start | bytes 786440 | tf_op jit(solution)/shard_map/ppermute | solution.py:460
  88.4 33.4 %collective-permute-start.14 = (bf16[1024,128]{1,0:T(8,128)(2,1)}, bf16[1024,128]{1,0:T(8,128)(2,1)}, u32[]{:S(2)}, u32[]{:S(2)}) collective-permute-start(bf16[1024,128]{1,0:T(8,128)(2,1)} %gate_0_11.1.refs_3_), channel_id=1, source_target_pairs={{0,11},{1,10},{2,9},{3,8},{4,15},{5,14},{6,13},{7,12},{8,3},{9,2},... | collective-permute-start | bytes 786440 | tf_op jit(solution)/shard_map/ppermute | solution.py:460
  97.2 24.6 %collective-permute-start.8 = (bf16[1024,128]{1,0:T(8,128)(2,1)}, bf16[1024,128]{1,0:T(8,128)(2,1)}, u32[]{:S(2)}, u32[]{:S(2)}) collective-permute-start(bf16[1024,128]{1,0:T(8,128)(2,1)} %gate_0_1.1.refs_3_), channel_id=1, source_target_pairs={{0,1},{1,0},{2,3},{3,2},{4,5},{5,4},{6,7},{7,6},{8,9},{9,8},{10,11... | collective-permute-start | bytes 786440 | tf_op jit(solution)/shard_map/ppermute | solution.py:460
  102.2 25.3 %collective-permute-start.15 = (bf16[1024,128]{1,0:T(8,128)(2,1)}, bf16[1024,128]{1,0:T(8,128)(2,1)}, u32[]{:S(2)}, u32[]{:S(2)}) collective-permute-start(bf16[1024,128]{1,0:T(8,128)(2,1)} %gate_0_15.1.refs_3_), channel_id=1, source_target_pairs={{0,15},{1,14},{2,13},{3,12},{4,11},{5,10},{6,9},{7,8},{8,7},{9,6},... | collective-permute-start | bytes 786440 | tf_op jit(solution)/shard_map/ppermute | solution.py:460
  103.9 23.7 %collective-permute-start.11 = (bf16[1024,128]{1,0:T(8,128)(2,1)}, bf16[1024,128]{1,0:T(8,128)(2,1)}, u32[]{:S(2)}, u32[]{:S(2)}) collective-permute-start(bf16[1024,128]{1,0:T(8,128)(2,1)} %gate_0_2.1.refs_3_), channel_id=1, source_target_pairs={{0,2},{1,3},{2,0},{3,1},{4,6},{5,7},{6,4},{7,5},{8,10},{9,11},{10,... | collective-permute-start | bytes 786440 | tf_op jit(solution)/shard_map/ppermute | solution.py:460
  108.4 28.3 %collective-permute-start.13 = (bf16[1024,128]{1,0:T(8,128)(2,1)}, bf16[1024,128]{1,0:T(8,128)(2,1)}, u32[]{:S(2)}, u32[]{:S(2)}) collective-permute-start(bf16[1024,128]{1,0:T(8,128)(2,1)} %gate_0_3.1.refs_3_), channel_id=1, source_target_pairs={{0,3},{1,2},{2,1},{3,0},{4,7},{5,6},{6,5},{7,4},{8,11},{9,10},{10,... | collective-permute-start | bytes 786440 | tf_op jit(solution)/shard_map/ppermute | solution.py:460
  121.8 18.2 %collective-permute-start.20 = (bf16[464,128]{1,0:T(8,128)(2,1)}, bf16[464,128]{1,0:T(8,128)(2,1)}, u32[]{:S(2)}, u32[]{:S(2)}) collective-permute-start(bf16[464,128]{1,0:T(8,128)(2,1)} %gate_1_8.1.refs_3_), channel_id=1, source_target_pairs={{0,8},{1,9},{2,10},{3,11},{4,12},{5,13},{6,14},{7,15},{8,0},{9,1},... | collective-permute-start | bytes 356360 | tf_op jit(solution)/shard_map/ppermute | solution.py:460
  121.8 18.1 %collective-permute-start.19 = (bf16[464,128]{1,0:T(8,128)(2,1)}, bf16[464,128]{1,0:T(8,128)(2,1)}, u32[]{:S(2)}, u32[]{:S(2)}) collective-permute-start(bf16[464,128]{1,0:T(8,128)(2,1)} %gate_1_4.1.refs_3_), channel_id=1, source_target_pairs={{0,4},{1,5},{2,6},{3,7},{4,0},{5,1},{6,2},{7,3},{8,12},{9,13},{10,... | collective-permute-start | bytes 356360 | tf_op jit(solution)/shard_map/ppermute | solution.py:460
  164.5 28.7 %collective-permute-start.33 = (bf16[576,128]{1,0:T(8,128)(2,1)}, bf16[576,128]{1,0:T(8,128)(2,1)}, u32[]{:S(2)}, u32[]{:S(2)}) collective-permute-start(bf16[576,128]{1,0:T(8,128)(2,1)} %gate_2_8.1.refs_3_), channel_id=1, source_target_pairs={{0,8},{1,9},{2,10},{3,11},{4,12},{5,13},{6,14},{7,15},{8,0},{9,1},... | collective-permute-start | bytes 442376 | tf_op jit(solution)/shard_map/ppermute | solution.py:460
  164.9 42.7 %collective-permute-start.32 = (bf16[576,128]{1,0:T(8,128)(2,1)}, bf16[576,128]{1,0:T(8,128)(2,1)}, u32[]{:S(2)}, u32[]{:S(2)}) collective-permute-start(bf16[576,128]{1,0:T(8,128)(2,1)} %gate_2_12.1.refs_3_), channel_id=1, source_target_pairs={{0,12},{1,13},{2,14},{3,15},{4,8},{5,9},{6,10},{7,11},{8,4},{9,5},... | collective-permute-start | bytes 442376 | tf_op jit(solution)/shard_map/ppermute | solution.py:460
  166.9 40.8 %collective-permute-start.36 = (bf16[576,128]{1,0:T(8,128)(2,1)}, bf16[576,128]{1,0:T(8,128)(2,1)}, u32[]{:S(2)}, u32[]{:S(2)}) collective-permute-start(bf16[576,128]{1,0:T(8,128)(2,1)} %gate_2_9.1.refs_3_), channel_id=1, source_target_pairs={{0,9},{1,8},{2,11},{3,10},{4,13},{5,12},{6,15},{7,14},{8,1},{9,0},... | collective-permute-start | bytes 442376 | tf_op jit(solution)/shard_map/ppermute | solution.py:460
  171.1 39.9 %collective-permute-start.35 = (bf16[576,128]{1,0:T(8,128)(2,1)}, bf16[576,128]{1,0:T(8,128)(2,1)}, u32[]{:S(2)}, u32[]{:S(2)}) collective-permute-start(bf16[576,128]{1,0:T(8,128)(2,1)} %gate_2_13.1.refs_3_), channel_id=1, source_target_pairs={{0,13},{1,12},{2,15},{3,14},{4,9},{5,8},{6,11},{7,10},{8,5},{9,4},... | collective-permute-start | bytes 442376 | tf_op jit(solution)/shard_map/ppermute | solution.py:460
  192.7 18.3 %collective-permute-start.31 = (bf16[576,128]{1,0:T(8,128)(2,1)}, bf16[576,128]{1,0:T(8,128)(2,1)}, u32[]{:S(2)}, u32[]{:S(2)}) collective-permute-start(bf16[576,128]{1,0:T(8,128)(2,1)} %gate_2_1.1.refs_3_), channel_id=1, source_target_pairs={{0,1},{1,0},{2,3},{3,2},{4,5},{5,4},{6,7},{7,6},{8,9},{9,8},{10,11... | collective-permute-start | bytes 442376 | tf_op jit(solution)/shard_map/ppermute | solution.py:460
  193.2 28.9 %collective-permute-start.38 = (bf16[576,128]{1,0:T(8,128)(2,1)}, bf16[576,128]{1,0:T(8,128)(2,1)}, u32[]{:S(2)}, u32[]{:S(2)}) collective-permute-start(bf16[576,128]{1,0:T(8,128)(2,1)} %gate_2_10.1.refs_3_), channel_id=1, source_target_pairs={{0,10},{1,11},{2,8},{3,9},{4,14},{5,15},{6,12},{7,13},{8,2},{9,3},... | collective-permute-start | bytes 442376 | tf_op jit(solution)/shard_map/ppermute | solution.py:460
  222.1 18.3 %collective-permute-start.39 = (bf16[576,128]{1,0:T(8,128)(2,1)}, bf16[576,128]{1,0:T(8,128)(2,1)}, u32[]{:S(2)}, u32[]{:S(2)}) collective-permute-start(bf16[576,128]{1,0:T(8,128)(2,1)} %gate_2_4.1.refs_3_), channel_id=1, source_target_pairs={{0,4},{1,5},{2,6},{3,7},{4,0},{5,1},{6,2},{7,3},{8,12},{9,13},{10,... | collective-permute-start | bytes 442376 | tf_op jit(solution)/shard_map/ppermute | solution.py:460
  222.1 18.3 %collective-permute-start.45 = (bf16[576,128]{1,0:T(8,128)(2,1)}, bf16[576,128]{1,0:T(8,128)(2,1)}, u32[]{:S(2)}, u32[]{:S(2)}) collective-permute-start(bf16[576,128]{1,0:T(8,128)(2,1)} %gate_2_15.1.refs_3_), channel_id=1, source_target_pairs={{0,15},{1,14},{2,13},{3,12},{4,11},{5,10},{6,9},{7,8},{8,7},{9,6},... | collective-permute-start | bytes 442376 | tf_op jit(solution)/shard_map/ppermute | solution.py:460
  (22 other events, 300.1 us)
